TPU v7x, 32 devices: a whole 2x2x4 slice. The times are simulated.
32 devices in a mesh: dp: 8 (over y, x, core), seq: 4 (over z).
Axes of the slice: x: 2, y: 2, z: 4, core: 2. Of those that a mesh axis runs over, the one named last changes fastest.
Arguments:
- tokens: bfloat16 [24, 1280, 640], P('dp', 'seq'), may hold values from -6 to 6
- cotangent: bfloat16 [24, 1280, 640], P('dp', 'seq'), may hold values from -6 to 6
- segments: int32 [24, 1280], P('dp'), may hold values from 0 to 1, as said below
- positions: int32 [24, 1280], P('dp', 'seq'), may hold values from 0 to 2558, as said below
- query_weight: float32 [1024, 640], P('dp'), may hold values from -0.25 to 0.25
- key_weight: float32 [256, 640], P('dp'), may hold values from -0.25 to 0.25
- value_weight: float32 [256, 640], P('dp'), may hold values from -0.25 to 0.25
- output_weight: float32 [640, 1024], P('dp'), may hold values from -0.75 to 0.75
- gate_weight: float32 [2048, 640], P('dp'), may hold values from -0.25 to 0.25
- up_weight: float32 [2048, 640], P('dp'), may hold values from -0.25 to 0.25
- down_weight: float32 [640, 2048], P('dp'), may hold values from -0.125 to 0.125
- norm_gains: float32 [3072], P('dp'), may hold values from -0.4 to 0.4
- query_first: float32 [1024, 640], P('dp'), may hold values from -112 to 112
- key_first: float32 [256, 640], P('dp'), may hold values from -112 to 112
- value_first: float32 [256, 640], P('dp'), may hold values from -112 to 112
- output_first: float32 [640, 1024], P('dp'), may hold values from -56 to 56
- gate_first: float32 [2048, 640], P('dp'), may hold values from -112 to 112
- up_first: float32 [2048, 640], P('dp'), may hold values from -112 to 112
- down_first: float32 [640, 2048], P('dp'), may hold values from -112 to 112
- gains_first: float32 [3072], P('dp'), may hold values from -160 to 160
- query_second: float32 [1024, 640], P('dp'), may hold values from 921.6 to 7680
- key_second: float32 [256, 640], P('dp'), may hold values from 921.6 to 7680
- value_second: float32 [256, 640], P('dp'), may hold values from 921.6 to 7680
- output_second: float32 [640, 1024], P('dp'), may hold values from 153.6 to 1228.8
- gate_second: float32 [2048, 640], P('dp'), may hold values from 921.6 to 7680
- up_second: float32 [2048, 640], P('dp'), may hold values from 921.6 to 7680
- down_second: float32 [640, 2048], P('dp'), may hold values from 921.6 to 7680
- gains_second: float32 [3072], P('dp'), may hold values from 1843.2 to 15360
Outputs:
- layer_output: bfloat16 [24, 1280, 640], P('dp', 'seq')
- input_grad: float32 [24, 1280, 640], P('dp', 'seq')
- query_momentum: float32 [1024, 640], P('dp')
- key_momentum: float32 [256, 640], P('dp')
- value_momentum: float32 [256, 640], P('dp')
- output_momentum: float32 [640, 1024], P('dp')
- gate_momentum: float32 [2048, 640], P('dp')
- up_momentum: float32 [2048, 640], P('dp')
- down_momentum: float32 [640, 2048], P('dp')
- gains_momentum: float32 [3072], P('dp')
- query_variance: float32 [1024, 640], P('dp')
- key_variance: float32 [256, 640], P('dp')
- value_variance: float32 [256, 640], P('dp')
- output_variance: float32 [640, 1024], P('dp')
- gate_variance: float32 [2048, 640], P('dp')
- up_variance: float32 [2048, 640], P('dp')
- down_variance: float32 [640, 2048], P('dp')
- gains_variance: float32 [3072], P('dp')
- query_updated: float32 [1024, 640], P('dp')
- key_updated: float32 [256, 640], P('dp')
- value_updated: float32 [256, 640], P('dp')
- output_updated: float32 [640, 1024], P('dp')
- gate_updated: float32 [2048, 640], P('dp')
- up_updated: float32 [2048, 640], P('dp')
- down_updated: float32 [640, 2048], P('dp')
- gains_updated: float32 [3072], P('dp')
Inputs may be any that keep to these rules, and one draw needn't show every extreme that they name: `segments`: along each sequence the ids start at 0 and rise by one at the first token of each document. Of the 3 sequences on one index of dp, one, drawn from the seed, is a single document; each of the others holds exactly 2 documents of varying lengths. `positions`: at the first token of a document the position is 0; within a document it rises by 1 or 2 from one token to the next, and by 2 throughout in the sequences that are a single document.
All inputs are finite; a program needn't handle non-finite values.
Results may differ from a plain program's by a relative error of at most 0.025.
Values may be sent and summed in bfloat16 or wider, within the bound.
No kernel may reach another device: no remote copies, remote signals or barrier semaphores. Data moves between devices by JAX's collectives and lax.ppermute only.
A program may use at most 192 MiB of HBM per device.

v0:
```python
import functools
import math

import jax
import jax.numpy as jnp
from jax import lax
from jax.experimental import pallas as pl
from jax.experimental.pallas import tpu as pltpu
from jax.sharding import PartitionSpec as P

WINDOW = 512
STEP = 10


NORM_EPSILON = 1e-06
ROPE_BASE = 10000.0
LEARN_RATE = 0.08
BETA_FIRST = 0.9
BETA_SECOND = 0.95
ADAM_EPSILON = 1e-08
WEIGHT_DECAY = 0.01
MASKED_SCORE = -1000000000.0


def frequencies(size):
    return ROPE_BASE ** (-2.0 * jnp.arange(size // 2).astype(jnp.float32) / size)


def weight_grad(gradients, inputs):
    return lax.dot_general(
        gradients, inputs, (((0,), (0,)), ((), ())), preferred_element_type=jnp.float32
    )


def adam_step(weight, first_moment, second_moment, gradient, decay_rate):
    momentum = BETA_FIRST * first_moment + (1.0 - BETA_FIRST) * gradient
    variance = BETA_SECOND * second_moment + (1.0 - BETA_SECOND) * gradient * gradient
    corrected = momentum / (1.0 - BETA_FIRST**STEP)
    scaled = variance / (1.0 - BETA_SECOND**STEP)
    updated = weight - LEARN_RATE * (
        corrected / (jnp.sqrt(scaled) + ADAM_EPSILON) + decay_rate * weight
    )
    return (momentum, variance, updated)


VMEM_BYTES = 56 * 1024 * 1024


def kernel_params():
    return pltpu.CompilerParams(
        dimension_semantics=("arbitrary",), vmem_limit_bytes=VMEM_BYTES
    )


def per_seq(*tail):
    return pl.BlockSpec((1,) + tail, lambda s: (s,) + (0,) * len(tail))


def whole(*shape):
    return pl.BlockSpec(shape, lambda s: (0,) * len(shape), pipeline_mode=pl.Buffered(1))


def dot_nt(a, b):
    return lax.dot_general(a, b, (((1,), (1,)), ((), ())), preferred_element_type=jnp.float32)


def dot_nn(a, b):
    return lax.dot_general(a, b, (((1,), (0,)), ((), ())), preferred_element_type=jnp.float32)


def dot_tn(a, b):
    return lax.dot_general(a, b, (((0,), (0,)), ((), ())), preferred_element_type=jnp.float32)


def inverse_rms(values):
    return lax.rsqrt(jnp.mean(values * values, axis=-1, keepdims=True) + NORM_EPSILON)


def rms_back(values, gain, grad):
    inverse = inverse_rms(values)
    unit = values * inverse
    scaled = grad * (1.0 + gain)
    return (
        inverse * (scaled - unit * jnp.mean(unit * scaled, axis=-1, keepdims=True)),
        jnp.sum(grad * unit, axis=0, keepdims=True),
    )


def turn(values, cosine, sine):
    half = values.shape[-1] // 2
    first, second = values[:, :half], values[:, half:]
    return jnp.concatenate(
        [first * cosine - second * sine, second * cosine + first * sine], axis=-1
    )


def stack_heads(values, heads):
    return jnp.concatenate([values] * heads, axis=0)


def cast_first_kernel(wq_ref, wk_ref, wv_ref, gain_ref, q_ref, rest_ref):
    q_ref[...] = wq_ref[...].astype(jnp.bfloat16)
    width = wq_ref.shape[1]
    gains = gain_ref[...]
    tail = width - gains.shape[1]
    block = jnp.broadcast_to(gains, (16, gains.shape[1]))
    if tail:
        block = jnp.concatenate([block, jnp.zeros((16, tail), jnp.float32)], axis=1)
    rest_ref[...] = jnp.concatenate([wk_ref[...], wv_ref[...], block], axis=0).astype(jnp.bfloat16)


def cast_gate_up_kernel(wg_ref, wu_ref, out_ref):
    rows = wg_ref.shape[0]
    out_ref[:rows, :] = wg_ref[...].astype(jnp.bfloat16)
    out_ref[rows:, :] = wu_ref[...].astype(jnp.bfloat16)


def cast_pair_kernel(waits, wd_ref, wo_ref, *refs):
    pair_ref = refs[waits]
    units = wd_ref.shape[1]
    pair_ref[:, :units] = wd_ref[...].astype(jnp.bfloat16)
    pair_ref[:, units:] = wo_ref[...].astype(jnp.bfloat16)


def stack_kernel(waits, side_ref, own_ref, received_ref, *refs):
    out_ref = refs[waits]
    upper = side_ref[0]
    out_ref[:, upper] = own_ref[...]
    out_ref[:, 1 - upper] = received_ref[...]


def gate_up_grad_kernel(dgate_ref, dup_ref, pre_ref, out_ref):
    rows = dgate_ref.shape[1]
    out_ref[0, :rows, :] = dot_tn(dgate_ref[...], pre_ref[...]).astype(jnp.bfloat16)
    out_ref[0, rows:, :] = dot_tn(dup_ref[...], pre_ref[...]).astype(jnp.bfloat16)


def query_grad_kernel(waits, dq_ref, normed_ref, *refs):
    refs[waits][...] = dot_tn(dq_ref[...], normed_ref[...]).astype(jnp.bfloat16)


def project_kernel(
    heads, x_ref, cos_ref, sin_ref, wq_ref, wk_ref, wv_ref, gi_ref, gq_ref, gk_ref,
    normed_ref, q_ref, qraw_ref, kv_ref, kraw_ref,
):
    x = x_ref[0].astype(jnp.float32)
    size = wk_ref.shape[0]
    rows = x.shape[0]
    part = rows // 2
    normed = (x * inverse_rms(x) * (1.0 + gi_ref[...])).astype(jnp.bfloat16)
    normed_ref[0] = normed
    cosine, sine = cos_ref[0], sin_ref[0]
    k_raw = dot_nt(normed, wk_ref[...])
    kraw_ref[0] = k_raw.astype(jnp.bfloat16)
    key = turn(k_raw * inverse_rms(k_raw) * (1.0 + gk_ref[...]), cosine, sine)
    kv_ref[0, :, :size] = key.astype(jnp.bfloat16)
    kv_ref[0, :, size:] = dot_nt(normed, wv_ref[...]).astype(jnp.bfloat16)
    for head in range(heads):
        raw = dot_nt(normed, wq_ref[head * size : (head + 1) * size, :])
        query = turn(raw * inverse_rms(raw) * (1.0 + gq_ref[...]), cosine, sine)
        query = (query * size ** (-0.5)).astype(jnp.bfloat16)
        raw = raw.astype(jnp.bfloat16)
        for t in range(2):
            span = slice(head * part, (head + 1) * part)
            q_ref[0, t, span, :] = query[t * part : (t + 1) * part]
            qraw_ref[0, t, span, :] = raw[t * part : (t + 1) * part]


def load_window(far_ref, near_ref, own_ref, win_ref):
    far, near = far_ref.shape[1], near_ref.shape[1]
    win_ref[:far, :] = far_ref[0]
    win_ref[far : far + near, :] = near_ref[0]
    win_ref[far + near :, :] = own_ref[0]


def mask_bias(qid_ref, kid_ref, t, part, span):
    ids = qid_ref[0, t * part : (t + 1) * part, :] == kid_ref[0, t]
    row = lax.broadcasted_iota(jnp.int32, (part, span), 0)
    column = lax.broadcasted_iota(jnp.int32, (part, span), 1)
    ok = ids & (column > row) & (column <= row + WINDOW)
    return jnp.where(ok, 0.0, MASKED_SCORE)


def attend_kernel(heads, q_ref, far_ref, near_ref, own_ref, qid_ref, kid_ref, mixed_ref, win_ref):
    size = q_ref.shape[-1]
    part = q_ref.shape[2] // heads
    span = part + WINDOW
    load_window(far_ref, near_ref, own_ref, win_ref)
    for t in range(2):
        bias = mask_bias(qid_ref, kid_ref, t, part, span)
        keys = win_ref[t * part : t * part + span, :size]
        values = win_ref[t * part : t * part + span, size:]
        for head in range(heads):
            scores = dot_nt(q_ref[0, t, head * part : (head + 1) * part, :], keys)
            weights = jnp.exp(scores + bias)
            total = jnp.sum(weights, axis=-1, keepdims=True)
            mixed = dot_nn(weights.astype(jnp.bfloat16), values) / total
            mixed_ref[0, t * part : (t + 1) * part, head * size : (head + 1) * size] = (
                mixed.astype(jnp.bfloat16)
            )


def middle_kernel(
    heads, chunk, mixed_ref, x_ref, cot_ref, wgu_ref, wdo_ref, ga_ref, gp_ref, gf_ref,
    out_ref, pre_ref, product_ref, ddown_ref, dgate_ref, dup_ref, datt_ref, dhid_ref, dmix_ref, dg_ref,
    act_ref, slope_ref,
):
    shard = wgu_ref.shape[1] // 2
    units = wgu_ref.shape[0] * shard
    group = chunk // shard

    def gate_up_rows(start, which):
        first = start // shard
        picked = wgu_ref[first : first + group, which * shard : (which + 1) * shard, :]
        return picked.reshape(chunk, picked.shape[-1])

    size = dmix_ref.shape[-1]
    part = dmix_ref.shape[2] // heads
    x = x_ref[0].astype(jnp.float32)
    attended = dot_nt(mixed_ref[0], wdo_ref[:, units:])
    hidden = x + attended * inverse_rms(attended) * (1.0 + ga_ref[...])
    pre = (hidden * inverse_rms(hidden) * (1.0 + gp_ref[...])).astype(jnp.bfloat16)
    pre_ref[0] = pre
    down = jnp.zeros(x.shape, jnp.float32)
    root = (2.0 / math.pi) ** 0.5
    for start in range(0, units, chunk):
        span = slice(start, start + chunk)
        gate = dot_nt(pre, gate_up_rows(start, 0))
        up = dot_nt(pre, gate_up_rows(start, 1))
        square = gate * gate
        bend = jnp.tanh(gate * (root + (root * 0.044715) * square))
        half = 0.5 + 0.5 * bend
        act = gate * half
        slope = half + act * (1.0 - bend) * (root + (3.0 * root * 0.044715) * square)
        act_ref[:, span] = act
        slope_ref[:, span] = up * slope
        product = (act * up).astype(jnp.bfloat16)
        product_ref[0, :, span] = product
        down += dot_nt(product, wdo_ref[:, span])
    out_ref[0] = (hidden + down * inverse_rms(down) * (1.0 + gf_ref[...])).astype(jnp.bfloat16)
    dy = cot_ref[0].astype(jnp.float32)
    d_down, dg_ffn = rms_back(down, gf_ref[...], dy)
    d_down = d_down.astype(jnp.bfloat16)
    ddown_ref[0] = d_down
    d_pre = jnp.zeros(x.shape, jnp.float32)
    for start in range(0, units, chunk):
        span = slice(start, start + chunk)
        d_product = dot_nn(d_down, wdo_ref[:, span])
        d_gate = (d_product * slope_ref[:, span]).astype(jnp.bfloat16)
        d_up = (d_product * act_ref[:, span]).astype(jnp.bfloat16)
        dgate_ref[0, :, span] = d_gate
        dup_ref[0, :, span] = d_up
        d_pre += dot_nn(d_gate, gate_up_rows(start, 0)) + dot_nn(
            d_up, gate_up_rows(start, 1)
        )
    d_hidden, dg_pre = rms_back(hidden, gp_ref[...], d_pre)
    d_hidden = dy + d_hidden
    dhid_ref[0] = d_hidden
    d_att, dg_attn = rms_back(attended, ga_ref[...], d_hidden)
    d_att = d_att.astype(jnp.bfloat16)
    datt_ref[0] = d_att
    dg_ref[0] = jnp.concatenate([dg_attn, dg_pre, dg_ffn], axis=0)
    for head in range(heads):
        d_mixed = dot_nn(
            d_att, wdo_ref[:, units + head * size : units + (head + 1) * size]
        ).astype(jnp.bfloat16)
        for t in range(2):
            dmix_ref[0, t, head * part : (head + 1) * part, :] = d_mixed[t * part : (t + 1) * part]


def attend_back_kernel(
    heads, waits, q_ref, qraw_ref, far_ref, near_ref, own_ref, qid_ref, kid_ref, mixed_ref, dmix_ref,
    cos_ref, sin_ref, gq_ref, *refs
):
    dfar_ref, dnear_ref, down_ref, dqraw_ref, dg_ref, win_ref, grad_ref = refs[waits:]
    size = q_ref.shape[-1]
    part = q_ref.shape[2] // heads
    span = part + WINDOW
    far, near = far_ref.shape[1], near_ref.shape[1]
    load_window(far_ref, near_ref, own_ref, win_ref)
    grad_ref[...] = jnp.zeros_like(grad_ref)
    dg = jnp.zeros((1, size), jnp.float32)
    for t in range(2):
        rows = slice(t * part, (t + 1) * part)
        window = slice(t * part, t * part + span)
        bias = mask_bias(qid_ref, kid_ref, t, part, span)
        keys = win_ref[window, :size]
        values = win_ref[window, size:]
        cosine, sine = cos_ref[0, rows, :], sin_ref[0, rows, :]
        for head in range(heads):
            line = slice(head * part, (head + 1) * part)
            lanes = slice(head * size, (head + 1) * size)
            query = q_ref[0, t, line, :]
            d_out = dmix_ref[0, t, line, :]
            weights = jnp.exp(dot_nt(query, keys) + bias)
            weights = weights * (1.0 / jnp.sum(weights, axis=-1, keepdims=True))
            delta = jnp.sum(
                d_out.astype(jnp.float32) * mixed_ref[0, rows, lanes].astype(jnp.float32),
                axis=-1,
                keepdims=True,
            )
            d_scores = (weights * (dot_nt(d_out, values) - delta)).astype(jnp.bfloat16)
            weights = weights.astype(jnp.bfloat16)
            grad_ref[window, :size] += dot_tn(d_scores, query)
            grad_ref[window, size:] += dot_tn(weights, d_out)
            d_query = dot_nn(d_scores, keys) * size ** (-0.5)
            d_raw, part_g = rms_back(
                qraw_ref[0, t, line, :].astype(jnp.float32),
                gq_ref[...],
                turn(d_query, cosine, -sine),
            )
            dqraw_ref[0, rows, lanes] = d_raw.astype(jnp.bfloat16)
            dg += part_g
    dg_ref[0] = dg
    dfar_ref[0] = grad_ref[:far, :].astype(jnp.bfloat16)
    dnear_ref[0] = grad_ref[far : far + near, :]
    down_ref[0] = grad_ref[far + near :, :]


def input_back_kernel(
    waits, own_ref, recv_ref, kraw_ref, cos_ref, sin_ref, wk_ref, wv_ref, dq_ref, wq_ref, x_ref, dhid_ref,
    gi_ref, gk_ref, *refs
):
    grad_ref, dpair_ref, dgi_ref, dgk_ref = refs[waits:]
    size = wk_ref.shape[0]
    total = own_ref[0] + recv_ref[0].astype(jnp.float32)
    d_key = turn(total[:, :size], cos_ref[0], -sin_ref[0])
    d_raw, dg_key = rms_back(kraw_ref[0].astype(jnp.float32), gk_ref[...], d_key)
    d_raw = d_raw.astype(jnp.bfloat16)
    d_value = total[:, size:].astype(jnp.bfloat16)
    dpair_ref[0, :, :size] = d_raw
    dpair_ref[0, :, size:] = d_value
    d_normed = dot_nn(dq_ref[0], wq_ref[...])
    d_normed += dot_nn(d_raw, wk_ref[...]) + dot_nn(d_value, wv_ref[...])
    d_x, dg_input = rms_back(x_ref[0].astype(jnp.float32), gi_ref[...], d_normed)
    grad_ref[0] = dhid_ref[0] + d_x
    dgi_ref[0] = dg_input
    dgk_ref[0] = dg_key


def flips(bit):
    return [(i, i ^ (1 << bit)) for i in range(lax.axis_size("dp"))]


def side(bit):
    return (lax.axis_index("dp") >> bit) & 1


def gather_rows(shard, order):
    current, done, steps = shard, [], []
    for bit in order:
        received = lax.ppermute(current, "dp", flips(bit))
        steps.append(received)
        upper = side(bit) == 1
        axis = sum(1 for other in done if other > bit)
        current = jnp.stack(
            [jnp.where(upper, received, current), jnp.where(upper, current, received)], axis=axis
        )
        done.append(bit)
    return current.reshape((lax.axis_size("dp"),) + shard.shape), steps


class RowSum:
    def __init__(self, parts, order, axis):
        self.terms = [
            (part.reshape((2,) * len(order) + part.shape[1:]), list(range(len(order) - 1, -1, -1)))
            for part in parts
        ]
        self.join = axis
        self.order = order
        self.chosen = {}
        self.received = []

    def total(self, other=None):
        picks = dict(self.chosen)
        if other is not None:
            picks[other] = 1 - side(other)
        pieces = [self.pick(part, bits, picks) for part, bits in self.terms]
        value = jnp.concatenate(pieces, axis=self.join) if len(pieces) > 1 else pieces[0]
        value = value.astype(jnp.float32)
        for part, bits in self.received:
            value += self.pick(part, bits, picks).astype(jnp.float32)
        return value.astype(jnp.bfloat16)

    def pick(self, part, bits, picks):
        bits = list(bits)
        for bit, where in picks.items():
            if bit in bits:
                part = lax.dynamic_index_in_dim(part, where, bits.index(bit), keepdims=False)
                bits.remove(bit)
        return part

    def send(self, bit):
        self.sent = self.total(bit)
        return self.sent

    def step(self, bit):
        received = lax.ppermute(self.send(bit), "dp", flips(bit))
        self.chosen[bit] = side(bit)
        left = [b for b in range(len(self.order) - 1, -1, -1) if b not in self.chosen]
        self.received.append((received, left))
        return received


def seq_sum(part):
    count = lax.axis_size("seq")
    index = lax.axis_index("seq")
    half = count // 2
    terms = [part]

    def total():
        return sum(term.astype(jnp.float32) for term in terms)

    for t in range(half - 1):
        pairs = [(t, t + 1), (count - 1 - t, count - 2 - t)]
        terms.append(lax.ppermute(total().astype(jnp.bfloat16), "seq", pairs))
    middle = [(half - 1, half), (half, half - 1)]
    terms.append(lax.ppermute(total().astype(jnp.bfloat16), "seq", middle))
    result = total()
    for t in range(half - 2, -1, -1):
        pairs = [(t + 1, t), (count - 2 - t, count - 1 - t)]
        received = lax.ppermute(result.astype(jnp.bfloat16), "seq", pairs)
        outer = (index == t) | (index == count - 1 - t)
        result = jnp.where(outer, received.astype(jnp.float32), result)
    return result


def body(
    tokens,
    cotangent,
    segments,
    positions,
    query_weight,
    key_weight,
    value_weight,
    output_weight,
    gate_weight,
    up_weight,
    down_weight,
    norm_gains,
    query_first,
    key_first,
    value_first,
    output_first,
    gate_first,
    up_first,
    down_first,
    gains_first,
    query_second,
    key_second,
    value_second,
    output_second,
    gate_second,
    up_second,
    down_second,
    gains_second,
):
    count = lax.axis_size("dp")
    bits = (count - 1).bit_length()
    order_a = list(range(1, bits)) + [0]
    order_b = list(range(bits - 1, 0, -1)) + [0]
    low = jnp.bfloat16
    f32 = jnp.float32
    width = tokens.shape[2]
    key_rows = key_weight.shape[0]
    gain_rows = norm_gains.shape[0]
    rest_rows = 2 * key_rows + 16

    def array(shape, kind):
        return jax.ShapeDtypeStruct(shape, kind)

    query_shard, rest_shard = pl.pallas_call(
        cast_first_kernel,
        out_shape=[array(query_weight.shape, low), array((rest_rows, width), low)],
    )(query_weight, key_weight, value_weight, norm_gains[None])
    query_all, query_steps = gather_rows(query_shard, order_a)
    rest_all, rest_steps = gather_rows(rest_shard, order_b)
    w_query = query_all.reshape(-1, width)
    w_key = rest_all[:, :key_rows].reshape(-1, width)
    w_value = rest_all[:, key_rows : 2 * key_rows].reshape(-1, width)
    gains_all = rest_all[:, 2 * key_rows, :gain_rows].reshape(-1)
    block = pl.BlockSpec(memory_space=pltpu.VMEM)
    anywhere = pl.BlockSpec(memory_space=pl.ANY)
    gate_up_shard = pl.pallas_call(
        cast_gate_up_kernel,
        out_shape=array((2 * gate_weight.shape[0], width), low),
    )(gate_weight, up_weight)
    gate_up_all = lax.all_gather(gate_up_shard, "dp", axis=0)
    arrived = [query_steps[-2], rest_steps[-2]]
    pair_shard = pl.pallas_call(
        functools.partial(cast_pair_kernel, len(arrived)),
        out_shape=array(
            (down_weight.shape[0], down_weight.shape[1] + output_weight.shape[1]), low
        ),
        in_specs=[block] * 2 + [anywhere] * len(arrived),
    )(down_weight, output_weight, *arrived)

    def stack_pair(own, received, bit, arrived):
        shape = own.shape
        return pl.pallas_call(
            functools.partial(stack_kernel, len(arrived)),
            out_shape=array((shape[0], 2) + shape[1:], low),
            in_specs=[pl.BlockSpec(memory_space=pltpu.SMEM)]
            + [block] * 2
            + [anywhere] * len(arrived),
            compiler_params=pltpu.CompilerParams(vmem_limit_bytes=VMEM_BYTES),
        )(side(bit)[None].astype(jnp.int32), own, received, *arrived).reshape(
            (2 * shape[0],) + shape[1:]
        )

    seqs, rows, _ = tokens.shape
    size = w_key.shape[0]
    heads = w_query.shape[0] // size
    units = down_weight.shape[1]
    shards = lax.axis_size("seq")
    far = WINDOW - rows
    part = rows // 2
    span = part + WINDOW
    gains_float = gains_all.astype(jnp.float32)[None]
    g_input, g_attn, g_pre, g_ffn = (
        gains_float[:, i * width : (i + 1) * width] for i in range(4)
    )
    g_query = gains_float[:, 4 * width : 4 * width + size]
    g_key = gains_float[:, 4 * width + size : 4 * width + 2 * size]
    angles = positions.astype(jnp.float32)[..., None] * frequencies(size)
    cosine, sine = jnp.cos(angles), jnp.sin(angles)
    first_row = lax.axis_index("seq") * rows
    padded = jnp.concatenate([jnp.full((seqs, WINDOW), -1, jnp.int32), segments], axis=1)
    window_ids = lax.dynamic_slice_in_dim(padded, first_row, WINDOW + rows, 1)
    query_ids = window_ids[:, WINDOW:, None]
    key_ids = jnp.stack([window_ids[:, :span], window_ids[:, part:]], axis=1)[:, :, None, :]

    def call(kernel, outs, out_specs, in_specs, scratch, flops, moved):
        return pl.pallas_call(
            kernel,
            grid=(seqs,),
            out_shape=outs,
            in_specs=in_specs,
            out_specs=out_specs,
            scratch_shapes=scratch,
            compiler_params=kernel_params(),
            cost_estimate=pl.CostEstimate(flops=flops, bytes_accessed=moved, transcendentals=0),
        )

    tokens_all = seqs * rows
    head_block = per_seq(2, heads * part, size)
    q_shape = (seqs, 2, heads * part, size)
    normed, query, query_raw, pair_own, key_raw = call(
        functools.partial(project_kernel, heads),
        [
            array((seqs, rows, width), low),
            array(q_shape, low),
            array(q_shape, low),
            array((seqs, rows, 2 * size), low),
            array((seqs, rows, size), low),
        ],
        [per_seq(rows, width), head_block, head_block, per_seq(rows, 2 * size), per_seq(rows, size)],
        [
            per_seq(rows, width),
            per_seq(rows, size // 2),
            per_seq(rows, size // 2),
            whole(*w_query.shape),
            whole(*w_key.shape),
            whole(*w_value.shape),
            whole(1, width),
            whole(1, size),
            whole(1, size),
        ],
        [],
        4 * tokens_all * width * (heads + 2) * size,
        16_000_000,
    )(tokens, cosine, sine, w_query, w_key, w_value, g_input, g_query, g_key)

    upward = [(i, i + 1) for i in range(shards - 1)]
    pair_near = lax.ppermute(pair_own, "seq", upward)
    far_send = pair_near[:, rows - far :]
    pair_far = lax.ppermute(far_send, "seq", upward[1:])
    pair_stack = pair_shard[None]
    for bit in order_b:
        received = lax.ppermute(pair_stack, "dp", flips(bit))
        if bit == order_b[0]:
            waits = [pair_own]
        elif bit == order_b[-2]:
            waits = [far_send]
        else:
            waits = []
        pair_stack = stack_pair(pair_stack, received, bit, waits)
    w_pair = pair_stack.reshape(-1, pair_stack.shape[-1])

    window_specs = [
        per_seq(far, 2 * size),
        per_seq(rows, 2 * size),
        per_seq(rows, 2 * size),
        per_seq(rows, 1),
        per_seq(2, 1, span),
    ]
    attend_flops = 8 * tokens_all * heads * span * size
    mixed = call(
        functools.partial(attend_kernel, heads),
        array((seqs, rows, heads * size), low),
        per_seq(rows, heads * size),
        [head_block] + window_specs,
        [pltpu.VMEM((WINDOW + rows, 2 * size), low)],
        attend_flops,
        16_000_000,
    )(query, pair_far, pair_near, pair_own, query_ids, key_ids)

    (
        layer_output,
        pre_low,
        product_low,
        grad_down_low,
        grad_gate_low,
        grad_up_low,
        grad_attended_low,
        grad_hidden,
        grad_mixed,
        grad_gains_middle,
    ) = call(
        functools.partial(middle_kernel, heads, 512),
        [
            array((seqs, rows, width), low),
            array((seqs, rows, width), low),
            array((seqs, rows, units), low),
            array((seqs, rows, width), low),
            array((seqs, rows, units), low),
            array((seqs, rows, units), low),
            array((seqs, rows, width), low),
            array((seqs, rows, width), f32),
            array(q_shape, low),
            array((seqs, 3, width), f32),
        ],
        [
            per_seq(rows, width),
            per_seq(rows, width),
            per_seq(rows, units),
            per_seq(rows, width),
            per_seq(rows, units),
            per_seq(rows, units),
            per_seq(rows, width),
            per_seq(rows, width),
            head_block,
            per_seq(3, width),
        ],
        [
            per_seq(rows, heads * size),
            per_seq(rows, width),
            per_seq(rows, width),
            whole(*gate_up_all.shape),
            whole(*w_pair.shape),
            whole(1, width),
            whole(1, width),
            whole(1, width),
        ],
        [pltpu.VMEM((rows, units), f32), pltpu.VMEM((rows, units), f32)],
        4 * tokens_all * width * (heads * size + 3 * units),
        40_000_000,
    )(mixed, tokens, cotangent, gate_up_all, w_pair, g_attn, g_pre, g_ffn)

    def flat(values):
        return values.reshape(tokens_all, values.shape[-1])

    def grad_blocks(gradient, inputs):
        product = weight_grad(flat(gradient), flat(inputs)).astype(low)
        return product.reshape(count, -1, product.shape[1])

    back_a = [0] + order_a[:-1]
    back_b = [0] + order_b[:-1]
    shard_units = gate_weight.shape[0]
    if shard_units % 128 == 0:
        gate_up_blocks = pl.pallas_call(
            gate_up_grad_kernel,
            grid=(count,),
            out_shape=array((count, 2 * shard_units, width), low),
            in_specs=[
                pl.BlockSpec((tokens_all, shard_units), lambda i: (0, i)),
                pl.BlockSpec((tokens_all, shard_units), lambda i: (0, i)),
                whole(tokens_all, width),
            ],
            out_specs=pl.BlockSpec((1, 2 * shard_units, width), lambda i: (i, 0, 0)),
            compiler_params=kernel_params(),
            cost_estimate=pl.CostEstimate(
                flops=4 * tokens_all * width * units, bytes_accessed=14_000_000, transcendentals=0
            ),
        )(flat(grad_gate_low), flat(grad_up_low), flat(pre_low))
    else:
        gate_up_blocks = jnp.concatenate(
            [grad_blocks(grad_gate_low, pre_low), grad_blocks(grad_up_low, pre_low)], axis=1
        )
    gate_up_part = lax.psum_scatter(gate_up_blocks, "dp", scatter_dimension=0, tiled=False)
    down_out_sum = RowSum(
        [
            grad_blocks(grad_down_low, product_low),
            grad_blocks(grad_attended_low, mixed),
        ],
        back_b,
        -1,
    )
    down_out_core = down_out_sum.step(back_b[0])

    def at_seq(s, *tail):
        return pl.BlockSpec((1,) + tail, lambda g: (s,) + (0,) * len(tail))

    def seq_call(kernel, outs, out_specs, in_specs, operands, scratch, alias, flops):
        return pl.pallas_call(
            kernel,
            grid=(1,),
            out_shape=outs,
            in_specs=in_specs,
            out_specs=out_specs,
            scratch_shapes=scratch,
            input_output_aliases=alias,
            compiler_params=kernel_params(),
            cost_estimate=pl.CostEstimate(
                flops=flops, bytes_accessed=8_000_000, transcendentals=0
            ),
        )(*operands)

    def attend_back(s, buffer, arrived):
        kinds = [
            array((1, far, 2 * size), low),
            array((1, rows, 2 * size), f32),
            array((1, rows, 2 * size), f32),
            array((seqs, rows, heads * size), low),
            array((1, 1, size), f32),
        ]
        specs = [
            at_seq(0, far, 2 * size),
            at_seq(0, rows, 2 * size),
            at_seq(0, rows, 2 * size),
            at_seq(s, rows, heads * size),
            at_seq(0, 1, size),
        ]
        in_specs = [
            at_seq(s, 2, heads * part, size),
            at_seq(s, 2, heads * part, size),
            at_seq(s, far, 2 * size),
            at_seq(s, rows, 2 * size),
            at_seq(s, rows, 2 * size),
            at_seq(s, rows, 1),
            at_seq(s, 2, 1, span),
            at_seq(s, rows, heads * size),
            at_seq(s, 2, heads * part, size),
            at_seq(s, rows, size // 2),
            at_seq(s, rows, size // 2),
            whole(1, size),
        ]
        operands = [
            query, query_raw, pair_far, pair_near, pair_own, query_ids, key_ids, mixed, grad_mixed,
            cosine, sine, g_query,
        ]
        alias = {}
        extra = list(arrived)
        if buffer is not None:
            alias = {len(operands): 3}
            extra = [buffer] + extra
        return seq_call(
            functools.partial(attend_back_kernel, heads, len(extra)),
            kinds,
            specs,
            in_specs + [anywhere] * len(extra),
            operands + extra,
            [
                pltpu.VMEM((WINDOW + rows, 2 * size), low),
                pltpu.VMEM((WINDOW + rows, 2 * size), f32),
            ],
            alias,
            attend_flops * 3 // seqs,
        )

    downward = [(i + 1, i) for i in range(shards - 1)]
    grad_query_low = None
    arrived = [down_out_sum.sent]
    own_parts, query_gains, near_sums, from_near = [], [], [], []
    for s in range(seqs):
        grad_far, grad_near, grad_own, grad_query_low, g_part = attend_back(
            s, grad_query_low, arrived
        )
        from_far = lax.ppermute(grad_far, "seq", downward[1:])
        own_parts.append(grad_own)
        query_gains.append(g_part)
        near_sum = (
            grad_near
            + jnp.pad(from_far.astype(f32), ((0, 0), (rows - far, 0), (0, 0)))
        ).astype(low)
        near_sums.append(near_sum)
        from_near.append(lax.ppermute(near_sum, "seq", downward))
        if s == 0:
            down_out_sum.step(back_b[1])
            arrived = [down_out_sum.sent, near_sums[0]]
        elif s == 1:
            arrived = [from_near[0]]
    query_columns = heads * size
    grad_w_query = pl.pallas_call(
        functools.partial(query_grad_kernel, 1),
        grid=(heads,),
        out_shape=array((query_columns, width), low),
        in_specs=[
            pl.BlockSpec((tokens_all, size), lambda i: (0, i)),
            whole(tokens_all, width),
            anywhere,
        ],
        out_specs=pl.BlockSpec((size, width), lambda i: (i, 0)),
        compiler_params=kernel_params(),
        cost_estimate=pl.CostEstimate(
            flops=2 * tokens_all * width * query_columns, bytes_accessed=5_000_000, transcendentals=0
        ),
    )(flat(grad_query_low), flat(normed), near_sums[1])
    for bit in back_b[2:]:
        down_out_sum.step(bit)
    down_out_last = down_out_sum.received[-1][0]

    def input_back(s, buffers, arrived):
        kinds = [
            array((seqs, rows, width), f32),
            array((seqs, rows, 2 * size), low),
            array((1, 1, width), f32),
            array((1, 1, size), f32),
        ]
        specs = [
            at_seq(s, rows, width),
            at_seq(s, rows, 2 * size),
            at_seq(0, 1, width),
            at_seq(0, 1, size),
        ]
        in_specs = [
            at_seq(0, rows, 2 * size),
            at_seq(0, rows, 2 * size),
            at_seq(s, rows, size),
            at_seq(s, rows, size // 2),
            at_seq(s, rows, size // 2),
            whole(*w_key.shape),
            whole(*w_value.shape),
            at_seq(s, rows, heads * size),
            whole(*w_query.shape),
            at_seq(s, rows, width),
            at_seq(s, rows, width),
            whole(1, width),
            whole(1, size),
        ]
        operands = [
            own_parts[s], from_near[s], key_raw, cosine, sine, w_key, w_value, grad_query_low,
            w_query, tokens, grad_hidden, g_input, g_key,
        ]
        alias = {}
        extra = list(arrived)
        if buffers:
            alias = {len(operands): 0, len(operands) + 1: 1}
            extra = list(buffers) + extra
        return seq_call(
            functools.partial(input_back_kernel, len(extra)),
            kinds,
            specs,
            in_specs + [anywhere] * len(extra),
            operands + extra,
            [],
            alias,
            2 * rows * width * size * (heads + 2),
        )

    buffers = []
    input_gains, key_gains = [], []
    waits = [[grad_w_query, near_sums[-1]], [down_out_sum.sent], [down_out_last]]
    waits += [[]] * seqs
    for s in range(seqs):
        *buffers, g_part, g_key_part = input_back(s, buffers, waits[s])
        input_gains.append(g_part)
        key_gains.append(g_key_part)
    input_grad, grad_pair_low = buffers
    pair_blocks = grad_blocks(grad_pair_low, normed).reshape(2, count, key_rows, width)
    grad_gains = jnp.concatenate(
        [
            sum(input_gains).reshape(-1),
            jnp.sum(grad_gains_middle, axis=0).reshape(-1),
            sum(query_gains).reshape(-1),
            sum(key_gains).reshape(-1),
        ]
    )
    gain_block = jnp.pad(
        grad_gains.astype(low).reshape(count, 1, gain_rows),
        ((0, 0), (0, 15), (0, width - gain_rows)),
    )
    query_rows = query_weight.shape[0]
    rest_sum = RowSum(
        [grad_w_query.reshape(count, query_rows, width), pair_blocks[0], pair_blocks[1], gain_block],
        back_b,
        -2,
    )
    for bit in back_b:
        rest_sum.step(bit)
    down_out_total = seq_sum(down_out_sum.total())
    gate_total = seq_sum(gate_up_part[:shard_units])
    up_total = seq_sum(gate_up_part[shard_units:])
    rest_total = seq_sum(rest_sum.total())
    query_total = rest_total[:query_rows]
    rest_total = rest_total[query_rows:]
    down_total = down_out_total[:, :units]
    output_total = down_out_total[:, units:]
    key_total = rest_total[:key_rows]
    value_total = rest_total[key_rows : 2 * key_rows]
    gains_total = rest_total[2 * key_rows, :gain_rows]
    query_momentum, query_variance, query_updated = adam_step(
        query_weight, query_first, query_second, query_total, WEIGHT_DECAY
    )
    key_momentum, key_variance, key_updated = adam_step(
        key_weight, key_first, key_second, key_total, WEIGHT_DECAY
    )
    value_momentum, value_variance, value_updated = adam_step(
        value_weight, value_first, value_second, value_total, WEIGHT_DECAY
    )
    output_momentum, output_variance, output_updated = adam_step(
        output_weight, output_first, output_second, output_total, WEIGHT_DECAY
    )
    gate_momentum, gate_variance, gate_updated = adam_step(
        gate_weight, gate_first, gate_second, gate_total, WEIGHT_DECAY
    )
    up_momentum, up_variance, up_updated = adam_step(
        up_weight, up_first, up_second, up_total, WEIGHT_DECAY
    )
    down_momentum, down_variance, down_updated = adam_step(
        down_weight, down_first, down_second, down_total, WEIGHT_DECAY
    )
    gains_momentum, gains_variance, gains_updated = adam_step(
        norm_gains, gains_first, gains_second, gains_total, 0.0
    )
    return (
        layer_output,
        input_grad,
        query_momentum,
        key_momentum,
        value_momentum,
        output_momentum,
        gate_momentum,
        up_momentum,
        down_momentum,
        gains_momentum,
        query_variance,
        key_variance,
        value_variance,
        output_variance,
        gate_variance,
        up_variance,
        down_variance,
        gains_variance,
        query_updated,
        key_updated,
        value_updated,
        output_updated,
        gate_updated,
        up_updated,
        down_updated,
        gains_updated,
    )


def solution(mesh):
    return jax.shard_map(
        body,
        mesh=mesh,
        in_specs=(
            P("dp", "seq", None),
            P("dp", "seq", None),
            P("dp", None),
            P("dp", "seq"),
            P("dp", None),
            P("dp", None),
            P("dp", None),
            P("dp", None),
            P("dp", None),
            P("dp", None),
            P("dp", None),
            P("dp"),
            P("dp", None),
            P("dp", None),
            P("dp", None),
            P("dp", None),
            P("dp", None),
            P("dp", None),
            P("dp", None),
            P("dp"),
            P("dp", None),
            P("dp", None),
            P("dp", None),
            P("dp", None),
            P("dp", None),
            P("dp", None),
            P("dp", None),
            P("dp"),
        ),
        out_specs=(
            P("dp", "seq", None),
            P("dp", "seq", None),
            P("dp", None),
            P("dp", None),
            P("dp", None),
            P("dp", None),
            P("dp", None),
            P("dp", None),
            P("dp", None),
            P("dp"),
            P("dp", None),
            P("dp", None),
            P("dp", None),
            P("dp", None),
            P("dp", None),
            P("dp", None),
            P("dp", None),
            P("dp"),
            P("dp", None),
            P("dp", None),
            P("dp", None),
            P("dp", None),
            P("dp", None),
            P("dp", None),
            P("dp", None),
            P("dp"),
        ),
        check_vma=False,
    )
```

profile of v0, /device:TPU:0, one launch (start us, length us, event | category | flops | bytes accessed | tf_op | source)
XLA Modules:
  0.0 370.2 jit_solution(1859616635515357674)
XLA Ops:
  7.3 2.2 shard_map.470
  10.1 1.7 shard_map.467
  11.9 3.0 collective-permute-start.3
  16.3 1.6 collective-permute-done.3
  18.9 1.8 collective-permute-start.4
  21.7 1.6 collective-permute-start.1
  23.3 5.3 %collective-permute-done.4.refs_1_ = bf16[2,80,640]{2,1,0:T(8,128)(2,1)S(1)} collective-permute-done((bf16[2,80,640]{2,1,0:T(8,128)(2,1)S(1)}, bf16[2,80,640]{2,1,0:T(8,128)(2,1)S(1)}, u32[]{:S(2)}, u32[]{:S(2)}) %collective-permute-start.4) | collective-permute-done | bytes 204832 | tf_op jit(solution)/shard_map/ppermute | solution.py:352
  28.8 2.8 multiply_sine_fusion
  31.5 5.5 %collective-permute-done.1.refs_0_ = bf16[2,128,640]{2,1,0:T(8,128)(2,1)S(1)} collective-permute-done((bf16[2,128,640]{2,1,0:T(8,128)(2,1)S(1)}, bf16[2,128,640]{2,1,0:T(8,128)(2,1)S(1)}, u32[]{:S(2)}, u32[]{:S(2)}) %collective-permute-start.1) | collective-permute-done | bytes 327712 | tf_op jit(solution)/shard_map/ppermute | solution.py:352
  37.8 2.0 shard_map.471
  44.8 7.1 %shard_map.468 = (bf16[3,320,640]{2,1,0:T(8,128)(2,1)}, bf16[3,2,640,256]{3,2,1,0:T(8,128)(2,1)}, bf16[3,2,640,256]{3,2,1,0:T(8,128)(2,1)}, bf16[3,320,512]{2,1,0:T(8,128)(2,1)}, bf16[3,320,256]{2,1,0:T(8,128)(2,1)}) custom-call(bf16[3,320,640]{2,1,0:T(8,128)(2,1)} %x_ref.9, f32[3,320,128]{2,1,0:T(8,128)} %get-tuple-element.181.cos_ref, ...), custom_call_target="tpu_custom_call" | custom-call | flops 3774873600 | bytes 16000000 | tf_op jit(solution)/shard_map/pallas_call | solution.py:548
  51.8 3.6 collective-permute-start.6
  55.5 7.4 %collective-permute-done.8.received_ref = bf16[1,80,3072]{2,1,0:T(8,128)(2,1)S(1)} collective-permute-done((bf16[1,80,3072]{2,1,0:T(8,128)(2,1)}, bf16[1,80,3072]{2,1,0:T(8,128)(2,1)S(1)}, u32[]{:S(2)}, u32[]{:S(2)}) %collective-permute-start.8) | collective-permute-done | bytes 491552 | tf_op jit(solution)/shard_map/ppermute | solution.py:580
  63.7 2.2 shard_map.472
  67.4 9.3 %collective-permute-done.6.near_ref = bf16[3,320,512]{2,1,0:T(8,128)(2,1)S(1)} collective-permute-done((bf16[3,320,512]{2,1,0:T(8,128)(2,1)}, bf16[3,320,512]{2,1,0:T(8,128)(2,1)S(1)}, u32[]{:S(2)}, u32[]{:S(2)}) %collective-permute-start.6) | collective-permute-done | bytes 983072 | tf_op jit(solution)/shard_map/ppermute | solution.py:575
  77.5 9.6 %collective-permute-done.9.received_ref = bf16[2,80,3072]{2,1,0:T(8,128)(2,1)S(1)} collective-permute-done((bf16[2,80,3072]{2,1,0:T(8,128)(2,1)}, bf16[2,80,3072]{2,1,0:T(8,128)(2,1)S(1)}, u32[]{:S(2)}, u32[]{:S(2)}) %collective-permute-start.9) | collective-permute-done | bytes 983072 | tf_op jit(solution)/shard_map/ppermute | solution.py:580
  88.1 2.9 shard_map.473
  96.4 7.7 %shard_map.469.mixed_ref = bf16[3,320,1024]{2,1,0:T(8,128)(2,1)} custom-call(bf16[3,2,640,256]{3,2,1,0:T(8,128)(2,1)} %get-tuple-element.72.q_ref, bf16[3,192,512]{2,1,0:T(8,128)(2,1)} %copy-done.61, bf16[3,320,512]{2,1,0:T(8,128)(2,1)} %copy-done.35, bf16[3,320,512]{2,1,0:T(8,128)(2,1)} %get-tuple-element.73.own_ref.refs_0_, s32[3,320,1]{2,1,0:T(8,128)} %copy.80.qid_ref, ...), custom_call_target="tpu_custom_call" | custom-call | flops 5284823040 | bytes 16000000 | tf_op jit(solution)/shard_map/pallas_call | solution.py:598
  105.4 4.3 %shard_map.474 = bf16[4,2,80,3072]{3,2,1,0:T(8,128)(2,1)} custom-call(s32[1]{0:T(128)} %bitcast.21.side_ref, bf16[4,80,3072]{2,1,0:T(8,128)(2,1)} %bitcast.183, bf16[4,80,3072]{2,1,0:T(8,128)(2,1)} %copy-done.9), custom_call_target="tpu_custom_call" | custom-call | tf_op jit(solution)/shard_map/pallas_call | solution.py:500
  109.7 37.4 %shard_map.475 = (bf16[3,320,640]{2,1,0:T(8,128)(2,1)}, bf16[3,320,640]{2,1,0:T(8,128)(2,1)}, bf16[3,320,2048]{2,1,0:T(8,128)(2,1)}, bf16[3,320,640]{2,1,0:T(8,1...) custom-call(bf16[3,320,1024]{2,1,0:T(8,128)(2,1)} %shard_map.469.mix, ...), custom_call_target="tpu_custom_call" | custom-call | flops 17616076800 | bytes 40000000 | tf_op jit(solution)/shard_map/pallas_call | solution.py:619
  147.1 3.0 bitcast_convert_fusion.1
  150.1 3.3 bitcast_convert_fusion
  155.6 12.1 %shard_map.483 = bf16[8,512,640]{2,1,0:T(8,128)(2,1)} custom-call(bf16[960,2048]{1,0:T(8,128)(2,1)} %bitcast.219, bf16[960,2048]{1,0:T(8,128)(2,1)} %bitcast.220, bf16[960,640]{1,0:T(8,128)(2,1)} %bitcast.221), custom_call_target="tpu_custom_call" | custom-call | flops 5033164800 | bytes 14000000 | tf_op jit(solution)/shard_map/pallas_call | solution.py:671
  167.7 9.2 %shard_map.476 = (bf16[1,192,512]{2,1,0:T(8,128)(2,1)}, f32[1,320,512]{2,1,0:T(8,128)}, f32[1,320,512]{2,1,0:T(8,128)}, bf16[3,320,1024]{2,1,0:T(8,128)(2,1)}, f32[1,1,256]{2,1,0:T(1,128)}) custom-call(bf16[3,2,640,256]{3,2,1,0:T(8,128)(2,1)} %get-tuple-element.72.q_ref, bf16[3,2,640,256]{3,2,1,0:T(8,128)(2,1)} %get-tuple-element.75.qraw_ref, ...), custom_call_target="tpu_custom_call" | custom-call | flops 5284823040 | bytes 8000000 | tf_op jit(solution)/shard_map/pallas_call | solution.py:705
  184.4 2.0 collective-permute-start.18
  186.4 9.1 %shard_map.477 = (bf16[1,192,512]{2,1,0:T(8,128)(2,1)}, f32[1,320,512]{2,1,0:T(8,128)}, f32[1,320,512]{2,1,0:T(8,128)}, bf16[3,320,1024]{2,1,0:T(8,128)(2,1)}, f32[1,1,256]{2,1,0:T(1,128)}) custom-call(bf16[3,2,640,256]{3,2,1,0:T(8,128)(2,1)} %get-tuple-element.72.q_ref, ...), custom_call_target="tpu_custom_call", output_to_operand_aliasing={{3}: (12, {})} | custom-call | flops 5284823040 | bytes 8000000 | tf_op jit(solution)/shard_map/pallas_call | solution.py:705
  196.2 15.3 %collective-permute-done.13.refs_1_.recv_ref = bf16[1,320,512]{2,1,0:T(8,128)(2,1)S(1)} collective-permute-done((bf16[1,320,512]{2,1,0:T(8,128)(2,1)S(1)}, bf16[1,320,512]{2,1,0:T(8,128)(2,1)S(1)}, u32[]{:S(2)}, u32[]{:S(2)}) %collective-permute-start.13) | collective-permute-done | bytes 327712 | tf_op jit(solution)/shard_map/ppermute | solution.py:787
  212.2 9.3 %shard_map.478 = (bf16[1,192,512]{2,1,0:T(8,128)(2,1)}, f32[1,320,512]{2,1,0:T(8,128)}, f32[1,320,512]{2,1,0:T(8,128)}, bf16[3,320,1024]{2,1,0:T(8,128)(2,1)}, f32[1,1,256]{2,1,0:T(1,128)}) custom-call(bf16[3,2,640,256]{3,2,1,0:T(8,128)(2,1)} %get-tuple-element.72.q_ref, ...), custom_call_target="tpu_custom_call", output_to_operand_aliasing={{3}: (12, {})} | custom-call | flops 5284823040 | bytes 8000000 | tf_op jit(solution)/shard_map/pallas_call | solution.py:705
  227.3 1.5 collective-permute-start.15
  228.9 5.3 %shard_map.479.refs_0_ = bf16[1024,640]{1,0:T(8,128)(2,1)} custom-call(bf16[960,1024]{1,0:T(8,128)(2,1)} %bitcast.174, bf16[960,640]{1,0:T(8,128)(2,1)} %bitcast.211, bf16[1,320,512]{2,1,0:T(8,128)(2,1)} %copy-done.10), custom_call_target="tpu_custom_call" | custom-call | flops 1258291200 | bytes 5000000 | tf_op jit(solution)/shard_map/pallas_call | solution.py:794
  234.1 4.8 %shard_map.480 = (f32[3,320,640]{2,1,0:T(8,128)}, bf16[3,320,512]{2,1,0:T(8,128)(2,1)}, f32[1,1,640]{2,1,0:T(1,128)}, f32[1,1,256]{2,1,0:T(1,128)}) custom-call(f32[1,320,512]{2,1,0:T(8,128)} %get-tuple-element.93.own_ref, bf16[1,320,512]{2,1,0:T(8,128)(2,1)} %copy-done.45, bf16[3,320,256]{2,1,0:T(8,128)(2,1)} %get-tuple-element.87.kraw_ref, ...), custom_call_target="tpu_custom_call" | custom-call | flops 629145600 | bytes 8000000 | tf_op jit(solution)/shard_map/pallas_call | solution.py:705
  240.1 5.1 %shard_map.481 = (f32[3,320,640]{2,1,0:T(8,128)}, bf16[3,320,512]{2,1,0:T(8,128)(2,1)}, f32[1,1,640]{2,1,0:T(1,128)}, f32[1,1,256]{2,1,0:T(1,128)}) custom-call(f32[1,320,512]{2,1,0:T(8,128)} %get-tuple-element.90.own_ref, bf16[1,320,512]{2,1,0:T(8,128)(2,1)} %copy-done.37, ...), custom_call_target="tpu_custom_call", output_to_operand_aliasing={{0}: (13, {}), {1}: (14, {})} | custom-call | flops 629145600 | bytes 8000000 | tf_op jit(solution)/shard_map/pallas_call | solution.py:705
  245.1 10.2 %collective-permute-done.15.recv_ref = bf16[1,320,512]{2,1,0:T(8,128)(2,1)S(1)} collective-permute-done((bf16[1,320,512]{2,1,0:T(8,128)(2,1)S(1)}, bf16[1,320,512]{2,1,0:T(8,128)(2,1)S(1)}, u32[]{:S(2)}, u32[]{:S(2)}) %collective-permute-start.15) | collective-permute-done | bytes 327712 | tf_op jit(solution)/shard_map/ppermute | solution.py:787
  256.2 4.7 %shard_map.482 = (f32[3,320,640]{2,1,0:T(8,128)}, bf16[3,320,512]{2,1,0:T(8,128)(2,1)}, f32[1,1,640]{2,1,0:T(1,128)}, f32[1,1,256]{2,1,0:T(1,128)}) custom-call(f32[1,320,512]{2,1,0:T(8,128)} %get-tuple-element.84.own_ref, bf16[1,320,512]{2,1,0:T(8,128)(2,1)} %copy-done.36, ...), custom_call_target="tpu_custom_call", output_to_operand_aliasing={{0}: (13, {}), {1}: (14, {})} | custom-call | flops 629145600 | bytes 8000000 | tf_op jit(solution)/shard_map/pallas_call | solution.py:705
  262.7 2.6 fusion.1
  267.7 10.3 %collective-permute-start.26 = (bf16[80,3072]{1,0:T(8,128)(2,1)S(1)}, bf16[80,3072]{1,0:T(8,128)(2,1)S(1)}, u32[]{:S(2)}, u32[]{:S(2)}) collective-permute-start(bf16[80,3072]{1,0:T(8,128)(2,1)S(1)} %fusion.4), channel_id=1, source_target_pairs={{0,1},{3,2},{4,5},{7,6},{8,9},{11,10},{12,13},{15,14},{16,17},{19,... | collective-permute-start | bytes 1474568 | tf_op jit(solution)/shard_map/ppermute | solution.py:416
  279.3 9.1 %collective-permute-done.26 = bf16[80,3072]{1,0:T(8,128)(2,1)S(1)} collective-permute-done((bf16[80,3072]{1,0:T(8,128)(2,1)S(1)}, bf16[80,3072]{1,0:T(8,128)(2,1)S(1)}, u32[]{:S(2)}, u32[]{:S(2)}) %collective-permute-start.26) | collective-permute-done | bytes 491552 | tf_op jit(solution)/shard_map/ppermute | solution.py:416
  289.4 2.5 collective-permute-done.21
  295.0 3.9 %collective-permute-done.22 = bf16[208,640]{1,0:T(8,128)(2,1)S(1)} collective-permute-done((bf16[208,640]{1,0:T(8,128)(2,1)S(1)}, bf16[208,640]{1,0:T(8,128)(2,1)S(1)}, u32[]{:S(2)}, u32[]{:S(2)}) %collective-permute-start.22) | collective-permute-done | bytes 266272 | tf_op jit(solution)/shard_map/ppermute | solution.py:398
  300.1 11.2 %collective-permute-start.23 = (bf16[208,640]{1,0:T(8,128)(2,1)S(1)}, bf16[208,640]{1,0:T(8,128)(2,1)S(1)}, u32[]{:S(2)}, u32[]{:S(2)}) collective-permute-start(bf16[208,640]{1,0:T(8,128)(2,1)S(1)} %fusion.15), channel_id=1, source_target_pairs={{0,1},{3,2},{4,5},{7,6},{8,9},{11,10},{12,13},{15,14},{16,17},{19,... | collective-permute-start | bytes 798728 | tf_op jit(solution)/shard_map/ppermute | solution.py:416
  313.9 3.2 collective-permute-done.28
  319.1 3.1 collective-permute-done.32
  323.0 1.6 multiply_subtract_fusion
  326.2 8.6 %collective-permute-start.29 = (bf16[256,640]{1,0:T(8,128)(2,1)S(1)}, bf16[256,640]{1,0:T(8,128)(2,1)S(1)}, u32[]{:S(2)}, u32[]{:S(2)}) collective-permute-start(bf16[256,640]{1,0:T(8,128)(2,1)S(1)} %get-tuple-element.152), channel_id=1, source_target_pairs={{0,1},{3,2},{4,5},{7,6},{8,9},{11,10},{12,13},{15,14},{16,17},{19,... | collective-permute-start | bytes 983048 | tf_op jit(solution)/shard_map/ppermute | solution.py:416
  339.4 4.9 %collective-permute-done.34 = bf16[256,640]{1,0:T(8,128)(2,1)S(1)} collective-permute-done((bf16[256,640]{1,0:T(8,128)(2,1)S(1)}, bf16[256,640]{1,0:T(8,128)(2,1)S(1)}, u32[]{:S(2)}, u32[]{:S(2)}) %collective-permute-start.34) | collective-permute-done | bytes 327712 | tf_op jit(solution)/shard_map/ppermute | solution.py:422
  344.3 1.8 multiply_subtract_fusion.1
  351.1 10.1 %collective-permute-done.31 = bf16[256,640]{1,0:T(8,128)(2,1)S(1)} collective-permute-done((bf16[256,640]{1,0:T(8,128)(2,1)S(1)}, bf16[256,640]{1,0:T(8,128)(2,1)S(1)}, u32[]{:S(2)}, u32[]{:S(2)}) %collective-permute-start.31) | collective-permute-done | bytes 327712 | tf_op jit(solution)/shard_map/ppermute | solution.py:422
  361.2 1.7 multiply_subtract_fusion.2
  (266 shorter events, 66.1 us)
Async XLA Ops:
  7.2 102.5 %all-gather.3.cloned.1.call-start = ((), (), s32[]{:S(2)}) async-start(), calls=%async_computation.2 | async-start | bytes 5898240 | tf_op jit(solution)/shard_map/all_gather | solution.py:488
  9.5 301.8 %reduce-scatter.2.cloned.1.call-start = ((), (), s32[]{:S(2)}) async-start(), calls=%async_computation.1 | async-start | bytes 5898240 | tf_op jit(solution)/shard_map/reduce_scatter | solution.py:690
  11.9 6.1 %collective-permute-start.3 = (bf16[80,640]{1,0:T(8,128)(2,1)}, bf16[80,640]{1,0:T(8,128)(2,1)S(1)}, u32[]{:S(2)}, u32[]{:S(2)}) collective-permute-start(bf16[80,640]{1,0:T(8,128)(2,1)} %get-tuple-element.71), channel_id=1, source_target_pairs={{0,16},{4,20},{8,24},{12,28},{16,0},{20,4},{24,8},{28,12},{1,17},{... | collective-permute-start | bytes 307208 | tf_op jit(solution)/shard_map/ppermute | solution.py:352
  14.8 5.9 %collective-permute-start = (bf16[128,640]{1,0:T(8,128)(2,1)}, bf16[128,640]{1,0:T(8,128)(2,1)S(1)}, u32[]{:S(2)}, u32[]{:S(2)}) collective-permute-start(bf16[128,640]{1,0:T(8,128)(2,1)} %get-tuple-element.70), channel_id=1, source_target_pairs={{0,8},{4,12},{8,0},{12,4},{16,24},{20,28},{24,16},{28,20},{1,9},{5... | collective-permute-start | bytes 491528 | tf_op jit(solution)/shard_map/ppermute | solution.py:352
  18.9 9.7 %collective-permute-start.4 = (bf16[2,80,640]{2,1,0:T(8,128)(2,1)S(1)}, bf16[2,80,640]{2,1,0:T(8,128)(2,1)S(1)}, u32[]{:S(2)}, u32[]{:S(2)}) collective-permute-start(bf16[2,80,640]{2,1,0:T(8,128)(2,1)S(1)} %pad_maximum_fusion.7), channel_id=1, source_target_pairs={{0,8},{4,12},{8,0},{12,4},{16,24},{20,28},{24,16},{28,20},{1,9},{5... | collective-permute-start | bytes 614408 | tf_op jit(solution)/shard_map/ppermute | solution.py:352
  21.7 15.4 %collective-permute-start.1 = (bf16[2,128,640]{2,1,0:T(8,128)(2,1)S(1)}, bf16[2,128,640]{2,1,0:T(8,128)(2,1)S(1)}, u32[]{:S(2)}, u32[]{:S(2)}) collective-permute-start(bf16[2,128,640]{2,1,0:T(8,128)(2,1)S(1)} %pad_maximum_fusion.6), channel_id=1, source_target_pairs={{0,16},{4,20},{8,24},{12,28},{16,0},{20,4},{24,8},{28,12},{1,17},{... | collective-permute-start | bytes 983048 | tf_op jit(solution)/shard_map/ppermute | solution.py:352
  28.7 12.3 %collective-permute-start.5 = (bf16[2,2,80,640]{3,2,0,1:T(8,128)(2,1)S(1)}, bf16[2,2,80,640]{3,2,0,1:T(8,128)(2,1)S(1)}, u32[]{:S(2)}, u32[]{:S(2)}) collective-permute-start(bf16[2,2,80,640]{3,2,0,1:T(8,128)(2,1)S(1)} %pad_maximum_fusion.5), channel_id=1, source_target_pairs={{0,4},{4,0},{8,12},{12,8},{16,20},{20,16},{24,28},{28,24},{1,5},{5... | collective-permute-start | bytes 1228808 | tf_op jit(solution)/shard_map/ppermute | solution.py:352
  37.2 6.1 %collective-permute-start.2 = (bf16[2,2,128,640]{3,2,1,0:T(8,128)(2,1)S(1)}, bf16[2,2,128,640]{3,2,1,0:T(8,128)(2,1)S(1)}, u32[]{:S(2)}, u32[]{:S(2)}) collective-permute-start(bf16[2,2,128,640]{3,2,1,0:T(8,128)(2,1)S(1)} %pad_maximum_fusion.4), channel_id=1, source_target_pairs={{0,4},{4,0},{8,12},{12,8},{16,20},{20,16},{24,28},{28,24},{1,5},{5... | collective-permute-start | bytes 1966088 | tf_op jit(solution)/shard_map/ppermute | solution.py:352
  39.8 23.1 %collective-permute-start.8 = (bf16[1,80,3072]{2,1,0:T(8,128)(2,1)}, bf16[1,80,3072]{2,1,0:T(8,128)(2,1)S(1)}, u32[]{:S(2)}, u32[]{:S(2)}) collective-permute-start(bf16[1,80,3072]{2,1,0:T(8,128)(2,1)} %bitcast.200), channel_id=1, source_target_pairs={{0,16},{4,20},{8,24},{12,28},{16,0},{20,4},{24,8},{28,12},{1,17},{... | collective-permute-start | bytes 1474568 | tf_op jit(solution)/shard_map/ppermute | solution.py:580
  51.8 24.8 %collective-permute-start.6 = (bf16[3,320,512]{2,1,0:T(8,128)(2,1)}, bf16[3,320,512]{2,1,0:T(8,128)(2,1)S(1)}, u32[]{:S(2)}, u32[]{:S(2)}) collective-permute-start(bf16[3,320,512]{2,1,0:T(8,128)(2,1)} %get-tuple-element.73.own_ref.refs_0_), channel_id=1, source_target_pairs={{0,1},{1,2},{2,3},{4,5},{5,6},{6,7},{8,9},{9,10},{10,11},{12,13},{... | collective-permute-start | bytes 2949128 | tf_op jit(solution)/shard_map/ppermute | solution.py:575
  65.9 21.3 %collective-permute-start.9 = (bf16[2,80,3072]{2,1,0:T(8,128)(2,1)}, bf16[2,80,3072]{2,1,0:T(8,128)(2,1)S(1)}, u32[]{:S(2)}, u32[]{:S(2)}) collective-permute-start(bf16[2,80,3072]{2,1,0:T(8,128)(2,1)} %bitcast.192), channel_id=1, source_target_pairs={{0,8},{4,12},{8,0},{12,4},{16,24},{20,28},{24,16},{28,20},{1,9},{5... | collective-permute-start | bytes 2949128 | tf_op jit(solution)/shard_map/ppermute | solution.py:580
  76.6 14.4 %copy-start.35 = (bf16[3,320,512]{2,1,0:T(8,128)(2,1)}, bf16[3,320,512]{2,1,0:T(8,128)(2,1)S(1)}, u32[]{:S(2)}) copy-start(bf16[3,320,512]{2,1,0:T(8,128)(2,1)S(1)} %collective-permute-done.6.near_ref) | copy-start | bytes 2949124
  91.0 13.1 %collective-permute-start.10 = (bf16[4,80,3072]{2,1,0:T(8,128)(2,1)}, bf16[4,80,3072]{2,1,0:T(8,128)(2,1)S(1)}, u32[]{:S(2)}, u32[]{:S(2)}) collective-permute-start(bf16[4,80,3072]{2,1,0:T(8,128)(2,1)} %bitcast.182), channel_id=1, source_target_pairs={{0,4},{4,0},{8,12},{12,8},{16,20},{20,16},{24,28},{28,24},{1,5},{5... | collective-permute-start | bytes 5898248 | tf_op jit(solution)/shard_map/ppermute | solution.py:580
  91.1 4.5 %collective-permute-start.7 = (bf16[3,192,512]{2,1,0:T(8,128)(2,1)S(1)}, bf16[3,192,512]{2,1,0:T(8,128)(2,1)S(1)}, u32[]{:S(2)}, u32[]{:S(2)}) collective-permute-start(bf16[3,192,512]{2,1,0:T(8,128)(2,1)S(1)} %copy-done.5), channel_id=1, source_target_pairs={{1,2},{2,3},{5,6},{6,7},{9,10},{10,11},{13,14},{14,15},{17,18},{18... | collective-permute-start | bytes 1769480 | tf_op jit(solution)/shard_map/ppermute | solution.py:577
  109.7 37.4 %copy-start.64 = (bf16[3,320,1024]{2,1,0:T(8,128)(2,1)S(1)}, bf16[3,320,1024]{2,1,0:T(8,128)(2,1)}, u32[]{:S(2)}) copy-start(bf16[3,320,1024]{2,1,0:T(8,128)(2,1)} %shard_map.469.mixed_ref) | copy-start | bytes 5898244
  155.1 27.8 %collective-permute-start.11 = (bf16[2,2,80,3072]{3,2,1,0:T(8,128)(2,1)}, bf16[2,2,80,3072]{3,2,1,0:T(8,128)(2,1)}, u32[]{:S(2)}, u32[]{:S(2)}) collective-permute-start(bf16[2,2,80,3072]{3,2,1,0:T(8,128)(2,1)} %pad_maximum_fusion.refs_0_), channel_id=1, source_target_pairs={{0,4},{4,0},{8,12},{12,8},{16,20},{20,16},{24,28},{28,24},{1,5},{5... | collective-permute-start | bytes 5898248 | tf_op jit(solution)/shard_map/ppermute | solution.py:398
  176.9 3.2 collective-permute-start.12
  181.3 30.2 %collective-permute-start.13 = (bf16[1,320,512]{2,1,0:T(8,128)(2,1)S(1)}, bf16[1,320,512]{2,1,0:T(8,128)(2,1)S(1)}, u32[]{:S(2)}, u32[]{:S(2)}) collective-permute-start(bf16[1,320,512]{2,1,0:T(8,128)(2,1)S(1)} %add_convert_fusion.2.refs_2_), channel_id=1, source_target_pairs={{1,0},{2,1},{3,2},{5,4},{6,5},{7,6},{9,8},{10,9},{11,10},{13,12},{... | collective-permute-start | bytes 983048 | tf_op jit(solution)/shard_map/ppermute | solution.py:787
  184.4 40.1 %collective-permute-start.18 = (bf16[2,80,3072]{2,1,0:T(8,128)(2,1)S(1)}, bf16[2,80,3072]{2,1,0:T(8,128)(2,1)S(1)}, u32[]{:S(2)}, u32[]{:S(2)}) collective-permute-start(bf16[2,80,3072]{2,1,0:T(8,128)(2,1)S(1)} %fusion.refs_1_), channel_id=1, source_target_pairs={{0,16},{4,20},{8,24},{12,28},{16,0},{20,4},{24,8},{28,12},{1,17},{... | collective-permute-start | bytes 2949128 | tf_op jit(solution)/shard_map/ppermute | solution.py:398
  195.5 27.5 %collective-permute-start.16 = (bf16[1,192,512]{2,1,0:T(8,128)(2,1)}, bf16[1,192,512]{2,1,0:T(8,128)(2,1)S(1)}, u32[]{:S(2)}, u32[]{:S(2)}) collective-permute-start(bf16[1,192,512]{2,1,0:T(8,128)(2,1)} %get-tuple-element.92), channel_id=1, source_target_pairs={{2,1},{3,2},{6,5},{7,6},{10,9},{11,10},{14,13},{15,14},{18,17},{19... | collective-permute-start | bytes 589832 | tf_op jit(solution)/shard_map/ppermute | solution.py:779
  212.2 10.8 %copy-start.30 = (f32[1,320,512]{2,1,0:T(8,128)S(1)}, f32[1,320,512]{2,1,0:T(8,128)}, u32[]{:S(2)}) copy-start(f32[1,320,512]{2,1,0:T(8,128)} %get-tuple-element.91) | copy-start | bytes 1966084
  212.2 12.2 %copy-start.24 = (bf16[80,1024]{1,0:T(8,128)(2,1)S(1)}, bf16[80,1024]{1,0:T(8,128)(2,1)}, u32[]{:S(2)}) copy-start(bf16[80,1024]{1,0:T(8,128)(2,1)} %get-tuple-element.141) | copy-start | bytes 491524
  221.5 5.7 %collective-permute-start.14 = (bf16[1,192,512]{2,1,0:T(8,128)(2,1)}, bf16[1,192,512]{2,1,0:T(8,128)(2,1)S(1)}, u32[]{:S(2)}, u32[]{:S(2)}) collective-permute-start(bf16[1,192,512]{2,1,0:T(8,128)(2,1)} %get-tuple-element.86), channel_id=1, source_target_pairs={{2,1},{3,2},{6,5},{7,6},{10,9},{11,10},{14,13},{15,14},{18,17},{19... | collective-permute-start | bytes 589832 | tf_op jit(solution)/shard_map/ppermute | solution.py:779
  223.1 16.2 %collective-permute-start.17 = (bf16[1,320,512]{2,1,0:T(8,128)(2,1)S(1)}, bf16[1,320,512]{2,1,0:T(8,128)(2,1)S(1)}, u32[]{:S(2)}, u32[]{:S(2)}) collective-permute-start(bf16[1,320,512]{2,1,0:T(8,128)(2,1)S(1)} %add_convert_fusion.refs_0_), channel_id=1, source_target_pairs={{1,0},{2,1},{3,2},{5,4},{6,5},{7,6},{9,8},{10,9},{11,10},{13,12},{... | collective-permute-start | bytes 983048 | tf_op jit(solution)/shard_map/ppermute | solution.py:787
  225.7 29.6 %collective-permute-start.19 = (bf16[80,3072]{1,0:T(8,128)(2,1)S(1)}, bf16[80,3072]{1,0:T(8,128)(2,1)S(1)}, u32[]{:S(2)}, u32[]{:S(2)}) collective-permute-start(bf16[80,3072]{1,0:T(8,128)(2,1)S(1)} %fusion.5.refs_2_), channel_id=1, source_target_pairs={{0,8},{4,12},{8,0},{12,4},{16,24},{20,28},{24,16},{28,20},{1,9},{5... | collective-permute-start | bytes 1474568 | tf_op jit(solution)/shard_map/ppermute | solution.py:398
  227.3 28.0 %collective-permute-start.15 = (bf16[1,320,512]{2,1,0:T(8,128)(2,1)S(1)}, bf16[1,320,512]{2,1,0:T(8,128)(2,1)S(1)}, u32[]{:S(2)}, u32[]{:S(2)}) collective-permute-start(bf16[1,320,512]{2,1,0:T(8,128)(2,1)S(1)} %add_convert_fusion.1.refs_1_), channel_id=1, source_target_pairs={{1,0},{2,1},{3,2},{5,4},{6,5},{7,6},{9,8},{10,9},{11,10},{13,12},{... | collective-permute-start | bytes 983048 | tf_op jit(solution)/shard_map/ppermute | solution.py:787
  265.6 12.8 %collective-permute-start.20 = (bf16[2,2,208,640]{3,2,1,0:T(8,128)(2,1)S(1)}, bf16[2,2,208,640]{3,2,1,0:T(8,128)(2,1)S(1)}, u32[]{:S(2)}, u32[]{:S(2)}) collective-permute-start(bf16[2,2,208,640]{3,2,1,0:T(8,128)(2,1)S(1)} %pad_maximum_fusion.2), channel_id=1, source_target_pairs={{0,4},{4,0},{8,12},{12,8},{16,20},{20,16},{24,28},{28,24},{1,5},{5... | collective-permute-start | bytes 3194888 | tf_op jit(solution)/shard_map/ppermute | solution.py:398
  267.7 20.6 %collective-permute-start.26 = (bf16[80,3072]{1,0:T(8,128)(2,1)S(1)}, bf16[80,3072]{1,0:T(8,128)(2,1)S(1)}, u32[]{:S(2)}, u32[]{:S(2)}) collective-permute-start(bf16[80,3072]{1,0:T(8,128)(2,1)S(1)} %fusion.4), channel_id=1, source_target_pairs={{0,1},{3,2},{4,5},{7,6},{8,9},{11,10},{12,13},{15,14},{16,17},{19,... | collective-permute-start | bytes 1474568 | tf_op jit(solution)/shard_map/ppermute | solution.py:416
  278.3 13.6 %copy-start.19 = (bf16[2,2,208,640]{3,2,1,0:T(8,128)(2,1)}, bf16[2,2,208,640]{3,2,1,0:T(8,128)(2,1)S(1)}, u32[]{:S(2)}) copy-start(bf16[2,2,208,640]{3,2,1,0:T(8,128)(2,1)S(1)} %collective-permute-done.20) | copy-start | bytes 3194884
  278.5 13.5 %collective-permute-start.21 = (bf16[2,208,640]{2,1,0:T(8,128)(2,1)S(1)}, bf16[2,208,640]{2,1,0:T(8,128)(2,1)S(1)}, u32[]{:S(2)}, u32[]{:S(2)}) collective-permute-start(bf16[2,208,640]{2,1,0:T(8,128)(2,1)S(1)} %fusion.2), channel_id=1, source_target_pairs={{0,16},{4,20},{8,24},{12,28},{16,0},{20,4},{24,8},{28,12},{1,17},{... | collective-permute-start | bytes 1597448 | tf_op jit(solution)/shard_map/ppermute | solution.py:398
  288.5 4.2 %collective-permute-start.27 = (bf16[80,3072]{1,0:T(8,128)(2,1)S(1)}, bf16[80,3072]{1,0:T(8,128)(2,1)S(1)}, u32[]{:S(2)}, u32[]{:S(2)}) collective-permute-start(bf16[80,3072]{1,0:T(8,128)(2,1)S(1)} %fusion.6), channel_id=1, source_target_pairs={{1,2},{2,1},{5,6},{6,5},{9,10},{10,9},{13,14},{14,13},{17,18},{18,... | collective-permute-start | bytes 1474568 | tf_op jit(solution)/shard_map/ppermute | solution.py:418
  292.1 6.8 %collective-permute-start.22 = (bf16[208,640]{1,0:T(8,128)(2,1)S(1)}, bf16[208,640]{1,0:T(8,128)(2,1)S(1)}, u32[]{:S(2)}, u32[]{:S(2)}) collective-permute-start(bf16[208,640]{1,0:T(8,128)(2,1)S(1)} %fusion.13), channel_id=1, source_target_pairs={{0,8},{4,12},{8,0},{12,4},{16,24},{20,28},{24,16},{28,20},{1,9},{5... | collective-permute-start | bytes 798728 | tf_op jit(solution)/shard_map/ppermute | solution.py:398
  293.7 23.4 %collective-permute-start.28 = (bf16[80,3072]{1,0:T(8,128)(2,1)}, bf16[80,3072]{1,0:T(8,128)(2,1)}, u32[]{:S(2)}, u32[]{:S(2)}) collective-permute-start(bf16[80,3072]{1,0:T(8,128)(2,1)} %fusion.10), channel_id=1, source_target_pairs={{1,0},{2,3},{5,4},{6,7},{9,8},{10,11},{13,12},{14,15},{17,16},{18,... | collective-permute-start | bytes 1474568 | tf_op jit(solution)/shard_map/ppermute | solution.py:422
  300.1 18.3 %collective-permute-start.23 = (bf16[208,640]{1,0:T(8,128)(2,1)S(1)}, bf16[208,640]{1,0:T(8,128)(2,1)S(1)}, u32[]{:S(2)}, u32[]{:S(2)}) collective-permute-start(bf16[208,640]{1,0:T(8,128)(2,1)S(1)} %fusion.15), channel_id=1, source_target_pairs={{0,1},{3,2},{4,5},{7,6},{8,9},{11,10},{12,13},{15,14},{16,17},{19,... | collective-permute-start | bytes 798728 | tf_op jit(solution)/shard_map/ppermute | solution.py:416
  312.5 9.7 %collective-permute-start.32 = (bf16[256,640]{1,0:T(8,128)(2,1)S(1)}, bf16[256,640]{1,0:T(8,128)(2,1)S(1)}, u32[]{:S(2)}, u32[]{:S(2)}) collective-permute-start(bf16[256,640]{1,0:T(8,128)(2,1)S(1)} %get-tuple-element.151), channel_id=1, source_target_pairs={{0,1},{3,2},{4,5},{7,6},{8,9},{11,10},{12,13},{15,14},{16,17},{19,... | collective-permute-start | bytes 983048 | tf_op jit(solution)/shard_map/ppermute | solution.py:416
  318.4 6.2 %collective-permute-start.24 = (bf16[208,640]{1,0:T(8,128)(2,1)S(1)}, bf16[208,640]{1,0:T(8,128)(2,1)S(1)}, u32[]{:S(2)}, u32[]{:S(2)}) collective-permute-start(bf16[208,640]{1,0:T(8,128)(2,1)S(1)} %fusion.16), channel_id=1, source_target_pairs={{1,2},{2,1},{5,6},{6,5},{9,10},{10,9},{13,14},{14,13},{17,18},{18,... | collective-permute-start | bytes 798728 | tf_op jit(solution)/shard_map/ppermute | solution.py:418
  322.3 12.6 %collective-permute-start.33 = (bf16[256,640]{1,0:T(8,128)(2,1)S(1)}, bf16[256,640]{1,0:T(8,128)(2,1)S(1)}, u32[]{:S(2)}, u32[]{:S(2)}) collective-permute-start(bf16[256,640]{1,0:T(8,128)(2,1)S(1)} %fusion.12), channel_id=1, source_target_pairs={{1,2},{2,1},{5,6},{6,5},{9,10},{10,9},{13,14},{14,13},{17,18},{18,... | collective-permute-start | bytes 983048 | tf_op jit(solution)/shard_map/ppermute | solution.py:418
  324.6 11.8 %copy-start.16 = (f32[80,1024]{1,0:T(8,128)S(1)}, f32[80,1024]{1,0:T(8,128)}, u32[]{:S(2)}) copy-start(f32[80,1024]{1,0:T(8,128)} %wo_ref.1) | copy-start | bytes 983044
  324.6 11.8 %copy-start.40 = (f32[80,1024]{1,0:T(8,128)S(1)}, f32[80,1024]{1,0:T(8,128)}, u32[]{:S(2)}) copy-start(f32[80,1024]{1,0:T(8,128)} %param.51) | copy-start | bytes 983044
  324.6 11.8 %copy-start.41 = (f32[80,1024]{1,0:T(8,128)S(1)}, f32[80,1024]{1,0:T(8,128)}, u32[]{:S(2)}) copy-start(f32[80,1024]{1,0:T(8,128)} %param.43) | copy-start | bytes 983044
  324.7 13.7 %collective-permute-start.25 = (bf16[208,640]{1,0:T(8,128)(2,1)S(1)}, bf16[208,640]{1,0:T(8,128)(2,1)S(1)}, u32[]{:S(2)}, u32[]{:S(2)}) collective-permute-start(bf16[208,640]{1,0:T(8,128)(2,1)S(1)} %fusion.17), channel_id=1, source_target_pairs={{1,0},{2,3},{5,4},{6,7},{9,8},{10,11},{13,12},{14,15},{17,16},{18,... | collective-permute-start | bytes 798728 | tf_op jit(solution)/shard_map/ppermute | solution.py:422
  326.2 13.2 %collective-permute-start.29 = (bf16[256,640]{1,0:T(8,128)(2,1)S(1)}, bf16[256,640]{1,0:T(8,128)(2,1)S(1)}, u32[]{:S(2)}, u32[]{:S(2)}) collective-permute-start(bf16[256,640]{1,0:T(8,128)(2,1)S(1)} %get-tuple-element.152), channel_id=1, source_target_pairs={{0,1},{3,2},{4,5},{7,6},{8,9},{11,10},{12,13},{15,14},{16,17},{19,... | collective-permute-start | bytes 983048 | tf_op jit(solution)/shard_map/ppermute | solution.py:416
  335.0 9.3 %collective-permute-start.34 = (bf16[256,640]{1,0:T(8,128)(2,1)S(1)}, bf16[256,640]{1,0:T(8,128)(2,1)S(1)}, u32[]{:S(2)}, u32[]{:S(2)}) collective-permute-start(bf16[256,640]{1,0:T(8,128)(2,1)S(1)} %fusion.21), channel_id=1, source_target_pairs={{1,0},{2,3},{5,4},{6,7},{9,8},{10,11},{13,12},{14,15},{17,16},{18,... | collective-permute-start | bytes 983048 | tf_op jit(solution)/shard_map/ppermute | solution.py:422
  346.1 1.8 collective-permute-start.30
  347.8 13.4 %copy-start.4 = (f32[256,640]{1,0:T(8,128)S(1)}, f32[256,640]{1,0:T(8,128)}, u32[]{:S(2)}) copy-start(f32[256,640]{1,0:T(8,128)} %wg_ref.1) | copy-start | bytes 1966084
  347.8 13.4 %copy-start.31 = (f32[256,640]{1,0:T(8,128)S(1)}, f32[256,640]{1,0:T(8,128)}, u32[]{:S(2)}) copy-start(f32[256,640]{1,0:T(8,128)} %param.52) | copy-start | bytes 1966084
  347.8 13.4 %copy-start.32 = (f32[256,640]{1,0:T(8,128)S(1)}, f32[256,640]{1,0:T(8,128)}, u32[]{:S(2)}) copy-start(f32[256,640]{1,0:T(8,128)} %param.44) | copy-start | bytes 1966084
  348.0 13.3 %collective-permute-start.31 = (bf16[256,640]{1,0:T(8,128)(2,1)S(1)}, bf16[256,640]{1,0:T(8,128)(2,1)S(1)}, u32[]{:S(2)}, u32[]{:S(2)}) collective-permute-start(bf16[256,640]{1,0:T(8,128)(2,1)S(1)} %fusion.20), channel_id=1, source_target_pairs={{1,0},{2,3},{5,4},{6,7},{9,8},{10,11},{13,12},{14,15},{17,16},{18,... | collective-permute-start | bytes 983048 | tf_op jit(solution)/shard_map/ppermute | solution.py:422
  (54 other events, 277.3 us)
Sparse Core Ops, SparseCore 0:
  10.5 58.4 all-gather.2
  167.8 83.4 reduce-scatter.1
where the time goes:
time: 376 us; the launch traced here: 370 us
  Pallas kernels  127 us (34%)
  waiting for transfers between devices  103 us (27%)
  starting transfers between devices  67.6 us (18%)
  other arithmetic  27.7 us (7%)
  local copies, waits for them, and re-layouts  20.4 us (5%)
  between operations  15.7 us (4%)
  matrix products  8.9 us (2%)
    pallas_call x6, Pallas kernels, seq_call(): pl.pallas_call(kernel, grid=(1,), out_shape=outs, in_specs=in_specs, out_...  42.1 us
    pallas_call x1, Pallas kernels, body(): call(functools.partial(middle_kernel, heads, 512), [array((seqs, rows, wi...  37.4 us
    ppermute x4, starting transfers between devices, seq_sum(): terms.append(lax.ppermute(total().astype(jnp.bfloat16), 'seq', pairs))  31.6 us
    ppermute x3, waiting for transfers between devices, body(): from_near.append(lax.ppermute(near_sum, 'seq', downward))  25.8 us
    ppermute x4, waiting for transfers between devices, seq_sum(): received = lax.ppermute(result.astype(jnp.bfloat16), 'seq', pairs)  19 us
    ppermute x3, waiting for transfers between devices, body(): received = lax.ppermute(pair_stack, 'dp', flips(bit))  17 us
    ppermute x4, waiting for transfers between devices, seq_sum(): terms.append(lax.ppermute(total().astype(jnp.bfloat16), 'seq', pairs))  12.9 us
    ppermute x6, waiting for transfers between devices, gather_rows(): received = lax.ppermute(current, 'dp', flips(bit))  12.4 us
  transfers between devices with their start and end apart: 37, of which 18 were waited for; matrix products, arithmetic and copies ran while one was open for 10% of the time, Pallas kernels for 24%

commit v1 on v0

--- a/solution.py
+++ b/solution.py
@@ -109,52 +109,116 @@
     rest_ref[...] = jnp.concatenate([wk_ref[...], wv_ref[...], block], axis=0).astype(jnp.bfloat16)
 
 
-def cast_gate_up_kernel(wg_ref, wu_ref, out_ref):
+def cast_rest_kernel(waits, wg_ref, wu_ref, wd_ref, wo_ref, *refs):
+    out_ref, pair_ref = refs[waits:]
     rows = wg_ref.shape[0]
+    units = wd_ref.shape[1]
     out_ref[:rows, :] = wg_ref[...].astype(jnp.bfloat16)
     out_ref[rows:, :] = wu_ref[...].astype(jnp.bfloat16)
-
-
-def cast_pair_kernel(waits, wd_ref, wo_ref, *refs):
-    pair_ref = refs[waits]
-    units = wd_ref.shape[1]
     pair_ref[:, :units] = wd_ref[...].astype(jnp.bfloat16)
     pair_ref[:, units:] = wo_ref[...].astype(jnp.bfloat16)
 
 
-def stack_kernel(waits, side_ref, own_ref, received_ref, *refs):
-    out_ref = refs[waits]
+def stack_kernel(axis, waits, side_ref, own_ref, received_ref, *refs):
+    out_ref, sems = refs[waits:]
     upper = side_ref[0]
-    out_ref[:, upper] = own_ref[...]
-    out_ref[:, 1 - upper] = received_ref[...]
-
-
-def gate_up_grad_kernel(dgate_ref, dup_ref, pre_ref, out_ref):
+    lead = (slice(None),) * axis
+    mine = pltpu.make_async_copy(own_ref, out_ref.at[lead + (upper,)], sems.at[0])
+    other = pltpu.make_async_copy(received_ref, out_ref.at[lead + (1 - upper,)], sems.at[1])
+    mine.start()
+    other.start()
+    mine.wait()
+    other.wait()
+
+
+def tail_rows_kernel(waits, near_ref, *refs):
+    out_ref, sem = refs[waits:]
+    rows = out_ref.shape[1]
+    copy = pltpu.make_async_copy(near_ref.at[:, near_ref.shape[1] - rows :], out_ref, sem)
+    copy.start()
+    copy.wait()
+
+
+def gate_up_grad_kernel(side_ref, dgate_ref, dup_ref, pre_ref, after_ref, send_ref, keep_ref, turned_ref):
+    step = pl.program_id(0)
+    half = pl.num_programs(0) // 2
     rows = dgate_ref.shape[1]
-    out_ref[0, :rows, :] = dot_tn(dgate_ref[...], pre_ref[...]).astype(jnp.bfloat16)
-    out_ref[0, rows:, :] = dot_tn(dup_ref[...], pre_ref[...]).astype(jnp.bfloat16)
+
+    @pl.when(step == 0)
+    def _():
+        turned_ref[...] = pre_ref[...].T
+
+    gate = dot_nn(turned_ref[...], dgate_ref[...]).astype(jnp.bfloat16)
+    up = dot_nn(turned_ref[...], dup_ref[...]).astype(jnp.bfloat16)
+
+    @pl.when(step < half)
+    def _():
+        send_ref[0, :, :rows] = gate
+        send_ref[0, :, rows:] = up
+
+    @pl.when(step >= half)
+    def _():
+        keep_ref[0, :, :rows] = gate
+        keep_ref[0, :, rows:] = up
+
+
+def pair_grad_kernel(
+    first, side_ref, product_ref, mixed_ref, ddown_ref, datt_ref, send_ref, keep_ref, turned_ref, total_ref
+):
+    step = pl.program_id(0)
+    upper = side_ref[0]
+    half, rows = send_ref.shape[0], send_ref.shape[1]
+
+    @pl.when(step == 0)
+    def _():
+        turned_ref[...] = ddown_ref[...].T
+
+    @pl.when(step == first)
+    def _():
+        turned_ref[...] = datt_ref[...].T
+
+    @pl.when(step < first)
+    def _():
+        total_ref[...] = dot_nn(turned_ref[...], product_ref[...])
+
+    @pl.when(step >= first)
+    def _():
+        total_ref[...] = dot_nn(turned_ref[...], mixed_ref[...])
+
+    for i in range(half):
+        mine = pl.multiple_of((2 * i + upper) * rows, rows)
+        other = pl.multiple_of((2 * i + 1 - upper) * rows, rows)
+        keep_ref[i] = total_ref[pl.ds(mine, rows), :].astype(jnp.bfloat16)
+        send_ref[i] = total_ref[pl.ds(other, rows), :].astype(jnp.bfloat16)
 
 
 def query_grad_kernel(waits, dq_ref, normed_ref, *refs):
     refs[waits][...] = dot_tn(dq_ref[...], normed_ref[...]).astype(jnp.bfloat16)
 
 
-def project_kernel(
-    heads, x_ref, cos_ref, sin_ref, wq_ref, wk_ref, wv_ref, gi_ref, gq_ref, gk_ref,
-    normed_ref, q_ref, qraw_ref, kv_ref, kraw_ref,
+def project_pair_kernel(
+    waits, x_ref, cos_ref, sin_ref, wk_ref, wv_ref, gi_ref, gk_ref, *refs
 ):
+    normed_ref, kv_ref, kraw_ref = refs[waits:]
     x = x_ref[0].astype(jnp.float32)
     size = wk_ref.shape[0]
-    rows = x.shape[0]
-    part = rows // 2
     normed = (x * inverse_rms(x) * (1.0 + gi_ref[...])).astype(jnp.bfloat16)
     normed_ref[0] = normed
-    cosine, sine = cos_ref[0], sin_ref[0]
     k_raw = dot_nt(normed, wk_ref[...])
     kraw_ref[0] = k_raw.astype(jnp.bfloat16)
-    key = turn(k_raw * inverse_rms(k_raw) * (1.0 + gk_ref[...]), cosine, sine)
+    key = turn(k_raw * inverse_rms(k_raw) * (1.0 + gk_ref[...]), cos_ref[0], sin_ref[0])
     kv_ref[0, :, :size] = key.astype(jnp.bfloat16)
     kv_ref[0, :, size:] = dot_nt(normed, wv_ref[...]).astype(jnp.bfloat16)
+
+
+def project_query_kernel(
+    heads, waits, normed_ref, cos_ref, sin_ref, wq_ref, gq_ref, *refs
+):
+    q_ref, qraw_ref = refs[waits:]
+    size = gq_ref.shape[-1]
+    part = normed_ref.shape[1] // 2
+    normed = normed_ref[0]
+    cosine, sine = cos_ref[0], sin_ref[0]
     for head in range(heads):
         raw = dot_nt(normed, wq_ref[head * size : (head + 1) * size, :])
         query = turn(raw * inverse_rms(raw) * (1.0 + gq_ref[...]), cosine, sine)
@@ -201,23 +265,41 @@
 
 
 def middle_kernel(
-    heads, chunk, mixed_ref, x_ref, cot_ref, wgu_ref, wdo_ref, ga_ref, gp_ref, gf_ref,
+    heads, chunk, side_ref, mixed_ref, x_ref, cot_ref, gu_own_ref, gu_got_ref, do_own_ref, do_got_ref, ga_ref, gp_ref, gf_ref,
     out_ref, pre_ref, product_ref, ddown_ref, dgate_ref, dup_ref, datt_ref, dhid_ref, dmix_ref, dg_ref,
-    act_ref, slope_ref,
+    act_ref, slope_ref, wgu_ref, wdo_blocks_ref, sems,
 ):
-    shard = wgu_ref.shape[1] // 2
-    units = wgu_ref.shape[0] * shard
+    @pl.when(pl.program_id(0) == 0)
+    def _():
+        upper = side_ref[0]
+        copies = []
+        for i, (source, target) in enumerate(
+            [(do_own_ref, wdo_blocks_ref), (do_got_ref, wdo_blocks_ref), (gu_own_ref, wgu_ref), (gu_got_ref, wgu_ref)]
+        ):
+            place = upper if i % 2 == 0 else 1 - upper
+            copies.append(pltpu.make_async_copy(source, target.at[:, place], sems.at[i]))
+        for copy in copies:
+            copy.start()
+        for copy in copies:
+            copy.wait()
+
+    def pair_columns(start, stop):
+        picked = wdo_blocks_ref[:, :, :, start:stop]
+        return picked.reshape(-1, stop - start)
+
+    shard = wgu_ref.shape[2] // 2
+    units = 2 * wgu_ref.shape[0] * shard
     group = chunk // shard
 
     def gate_up_rows(start, which):
-        first = start // shard
-        picked = wgu_ref[first : first + group, which * shard : (which + 1) * shard, :]
+        first = start // shard // 2
+        picked = wgu_ref[first : first + group // 2, :, which * shard : (which + 1) * shard, :]
         return picked.reshape(chunk, picked.shape[-1])
 
     size = dmix_ref.shape[-1]
     part = dmix_ref.shape[2] // heads
     x = x_ref[0].astype(jnp.float32)
-    attended = dot_nt(mixed_ref[0], wdo_ref[:, units:])
+    attended = dot_nt(mixed_ref[0], pair_columns(units, units + heads * size))
     hidden = x + attended * inverse_rms(attended) * (1.0 + ga_ref[...])
     pre = (hidden * inverse_rms(hidden) * (1.0 + gp_ref[...])).astype(jnp.bfloat16)
     pre_ref[0] = pre
@@ -236,7 +318,7 @@
         slope_ref[:, span] = up * slope
         product = (act * up).astype(jnp.bfloat16)
         product_ref[0, :, span] = product
-        down += dot_nt(product, wdo_ref[:, span])
+        down += dot_nt(product, pair_columns(start, start + chunk))
     out_ref[0] = (hidden + down * inverse_rms(down) * (1.0 + gf_ref[...])).astype(jnp.bfloat16)
     dy = cot_ref[0].astype(jnp.float32)
     d_down, dg_ffn = rms_back(down, gf_ref[...], dy)
@@ -245,7 +327,7 @@
     d_pre = jnp.zeros(x.shape, jnp.float32)
     for start in range(0, units, chunk):
         span = slice(start, start + chunk)
-        d_product = dot_nn(d_down, wdo_ref[:, span])
+        d_product = dot_nn(d_down, pair_columns(start, start + chunk))
         d_gate = (d_product * slope_ref[:, span]).astype(jnp.bfloat16)
         d_up = (d_product * act_ref[:, span]).astype(jnp.bfloat16)
         dgate_ref[0, :, span] = d_gate
@@ -262,7 +344,7 @@
     dg_ref[0] = jnp.concatenate([dg_attn, dg_pre, dg_ffn], axis=0)
     for head in range(heads):
         d_mixed = dot_nn(
-            d_att, wdo_ref[:, units + head * size : units + (head + 1) * size]
+            d_att, pair_columns(units + head * size, units + (head + 1) * size)
         ).astype(jnp.bfloat16)
         for t in range(2):
             dmix_ref[0, t, head * part : (head + 1) * part, :] = d_mixed[t * part : (t + 1) * part]
@@ -346,17 +428,25 @@
     return (lax.axis_index("dp") >> bit) & 1
 
 
+def stack_step(own, received, bit, done, arrived=()):
+    axis = sum(1 for other in done if other > bit)
+    anywhere = pl.BlockSpec(memory_space=pl.ANY)
+    arrived = list(arrived)
+    return pl.pallas_call(
+        functools.partial(stack_kernel, axis, len(arrived)),
+        out_shape=jax.ShapeDtypeStruct(own.shape[:axis] + (2,) + own.shape[axis:], own.dtype),
+        in_specs=[pl.BlockSpec(memory_space=pltpu.SMEM)] + [anywhere] * (2 + len(arrived)),
+        out_specs=anywhere,
+        scratch_shapes=[pltpu.SemaphoreType.DMA((2,))],
+    )(side(bit)[None].astype(jnp.int32), own, received, *arrived)
+
+
 def gather_rows(shard, order):
-    current, done, steps = shard, [], []
-    for bit in order:
+    current, steps = shard, []
+    for i, bit in enumerate(order):
         received = lax.ppermute(current, "dp", flips(bit))
         steps.append(received)
-        upper = side(bit) == 1
-        axis = sum(1 for other in done if other > bit)
-        current = jnp.stack(
-            [jnp.where(upper, received, current), jnp.where(upper, current, received)], axis=axis
-        )
-        done.append(bit)
+        current = stack_step(current, received, bit, order[:i])
     return current.reshape((lax.axis_size("dp"),) + shard.shape), steps
 
 
@@ -370,6 +460,18 @@
         self.order = order
         self.chosen = {}
         self.received = []
+
+    @classmethod
+    def from_halves(cls, keep, send, order):
+        result = cls([], order, -1)
+        shape = (2,) * (len(order) - 1) + keep.shape[1:]
+        left = list(range(len(order) - 1, 0, -1))
+        received = lax.ppermute(send, "dp", flips(0))
+        result.terms = [(keep.reshape(shape), left)]
+        result.received = [(received.reshape(shape), left)]
+        result.chosen = {0: side(0)}
+        result.sent = send
+        return result
 
     def total(self, other=None):
         picks = dict(self.chosen)
@@ -481,32 +583,15 @@
     gains_all = rest_all[:, 2 * key_rows, :gain_rows].reshape(-1)
     block = pl.BlockSpec(memory_space=pltpu.VMEM)
     anywhere = pl.BlockSpec(memory_space=pl.ANY)
-    gate_up_shard = pl.pallas_call(
-        cast_gate_up_kernel,
-        out_shape=array((2 * gate_weight.shape[0], width), low),
-    )(gate_weight, up_weight)
-    gate_up_all = lax.all_gather(gate_up_shard, "dp", axis=0)
     arrived = [query_steps[-2], rest_steps[-2]]
-    pair_shard = pl.pallas_call(
-        functools.partial(cast_pair_kernel, len(arrived)),
-        out_shape=array(
-            (down_weight.shape[0], down_weight.shape[1] + output_weight.shape[1]), low
-        ),
-        in_specs=[block] * 2 + [anywhere] * len(arrived),
-    )(down_weight, output_weight, *arrived)
-
-    def stack_pair(own, received, bit, arrived):
-        shape = own.shape
-        return pl.pallas_call(
-            functools.partial(stack_kernel, len(arrived)),
-            out_shape=array((shape[0], 2) + shape[1:], low),
-            in_specs=[pl.BlockSpec(memory_space=pltpu.SMEM)]
-            + [block] * 2
-            + [anywhere] * len(arrived),
-            compiler_params=pltpu.CompilerParams(vmem_limit_bytes=VMEM_BYTES),
-        )(side(bit)[None].astype(jnp.int32), own, received, *arrived).reshape(
-            (2 * shape[0],) + shape[1:]
-        )
+    gate_up_shard, pair_shard = pl.pallas_call(
+        functools.partial(cast_rest_kernel, len(arrived)),
+        out_shape=[
+            array((2 * gate_weight.shape[0], width), low),
+            array((down_weight.shape[0], down_weight.shape[1] + output_weight.shape[1]), low),
+        ],
+        in_specs=[block] * 4 + [anywhere] * len(arrived),
+    )(gate_weight, up_weight, down_weight, output_weight, *arrived)
 
     seqs, rows, _ = tokens.shape
     size = w_key.shape[0]
@@ -524,6 +609,7 @@
     g_key = gains_float[:, 4 * width + size : 4 * width + 2 * size]
     angles = positions.astype(jnp.float32)[..., None] * frequencies(size)
     cosine, sine = jnp.cos(angles), jnp.sin(angles)
+    core_side = side(0)[None].astype(jnp.int32)
     first_row = lax.axis_index("seq") * rows
     padded = jnp.concatenate([jnp.full((seqs, WINDOW), -1, jnp.int32), segments], axis=1)
     window_ids = lax.dynamic_slice_in_dim(padded, first_row, WINDOW + rows, 1)
@@ -545,47 +631,72 @@
     tokens_all = seqs * rows
     head_block = per_seq(2, heads * part, size)
     q_shape = (seqs, 2, heads * part, size)
-    normed, query, query_raw, pair_own, key_raw = call(
-        functools.partial(project_kernel, heads),
+    normed, pair_own, key_raw = call(
+        functools.partial(project_pair_kernel, 2),
         [
             array((seqs, rows, width), low),
-            array(q_shape, low),
-            array(q_shape, low),
             array((seqs, rows, 2 * size), low),
             array((seqs, rows, size), low),
         ],
-        [per_seq(rows, width), head_block, head_block, per_seq(rows, 2 * size), per_seq(rows, size)],
+        [per_seq(rows, width), per_seq(rows, 2 * size), per_seq(rows, size)],
+        [
+            per_seq(rows, width),
+            per_seq(rows, size // 2),
+            per_seq(rows, size // 2),
+            whole(*w_key.shape),
+            whole(*w_value.shape),
+            whole(1, width),
+            whole(1, size),
+            anywhere,
+            anywhere,
+        ],
+        [],
+        4 * tokens_all * width * size,
+        6_000_000,
+    )(tokens, cosine, sine, w_key, w_value, g_input, g_key, query_ids, key_ids)
+    pair_first = lax.ppermute(pair_shard, "dp", flips(order_b[0]))
+    query, query_raw = call(
+        functools.partial(project_query_kernel, heads, 1),
+        [array(q_shape, low), array(q_shape, low)],
+        [head_block, head_block],
         [
             per_seq(rows, width),
             per_seq(rows, size // 2),
             per_seq(rows, size // 2),
             whole(*w_query.shape),
-            whole(*w_key.shape),
-            whole(*w_value.shape),
-            whole(1, width),
             whole(1, size),
-            whole(1, size),
+            anywhere,
         ],
         [],
-        4 * tokens_all * width * (heads + 2) * size,
-        16_000_000,
-    )(tokens, cosine, sine, w_query, w_key, w_value, g_input, g_query, g_key)
+        2 * tokens_all * width * heads * size,
+        8_000_000,
+    )(normed, cosine, sine, w_query, g_query, pair_first)
 
     upward = [(i, i + 1) for i in range(shards - 1)]
     pair_near = lax.ppermute(pair_own, "seq", upward)
-    far_send = pair_near[:, rows - far :]
-    pair_far = lax.ppermute(far_send, "seq", upward[1:])
-    pair_stack = pair_shard[None]
-    for bit in order_b:
-        received = lax.ppermute(pair_stack, "dp", flips(bit))
-        if bit == order_b[0]:
-            waits = [pair_own]
-        elif bit == order_b[-2]:
-            waits = [far_send]
-        else:
-            waits = []
-        pair_stack = stack_pair(pair_stack, received, bit, waits)
-    w_pair = pair_stack.reshape(-1, pair_stack.shape[-1])
+    gate_up_half, pair_half = gate_up_shard, pair_shard
+    pair_far = None
+    for i in range(bits - 1):
+        pair_received = pair_first
+        if i:
+            pair_received = lax.ppermute(pair_half, "dp", flips(order_b[i]))
+        gate_up_received = lax.ppermute(gate_up_half, "dp", flips(order_a[i]))
+        waits = [query] if i == 0 else [pair_far]
+        pair_half = stack_step(pair_half, pair_received, order_b[i], order_b[:i], waits)
+        gate_up_half = stack_step(gate_up_half, gate_up_received, order_a[i], order_a[:i], waits)
+        if i == 0:
+            far_send = pl.pallas_call(
+                functools.partial(tail_rows_kernel, 2),
+                out_shape=array((seqs, far, 2 * size), low),
+                in_specs=[anywhere] * 3,
+                out_specs=anywhere,
+                scratch_shapes=[pltpu.SemaphoreType.DMA],
+            )(pair_near, pair_half, gate_up_half)
+            pair_far = lax.ppermute(far_send, "seq", upward[1:])
+    pair_half = pair_half.reshape((count // 2,) + pair_shard.shape)
+    gate_up_half = gate_up_half.reshape((count // 2,) + gate_up_shard.shape)
+    pair_received = lax.ppermute(pair_half, "dp", flips(0))
+    gate_up_received = lax.ppermute(gate_up_half, "dp", flips(0))
 
     window_specs = [
         per_seq(far, 2 * size),
@@ -643,19 +754,31 @@
             per_seq(3, width),
         ],
         [
+            pl.BlockSpec(memory_space=pltpu.SMEM),
             per_seq(rows, heads * size),
             per_seq(rows, width),
             per_seq(rows, width),
-            whole(*gate_up_all.shape),
-            whole(*w_pair.shape),
+            anywhere,
+            anywhere,
+            anywhere,
+            anywhere,
             whole(1, width),
             whole(1, width),
             whole(1, width),
         ],
-        [pltpu.VMEM((rows, units), f32), pltpu.VMEM((rows, units), f32)],
+        [
+            pltpu.VMEM((rows, units), f32),
+            pltpu.VMEM((rows, units), f32),
+            pltpu.VMEM((count // 2, 2) + gate_up_shard.shape, low),
+            pltpu.VMEM((count // 2, 2) + pair_shard.shape, low),
+            pltpu.SemaphoreType.DMA((4,)),
+        ],
         4 * tokens_all * width * (heads * size + 3 * units),
         40_000_000,
-    )(mixed, tokens, cotangent, gate_up_all, w_pair, g_attn, g_pre, g_ffn)
+    )(
+        core_side, mixed, tokens, cotangent, gate_up_half, gate_up_received, pair_half, pair_received,
+        g_attn, g_pre, g_ffn,
+    )
 
     def flat(values):
         return values.reshape(tokens_all, values.shape[-1])
@@ -667,36 +790,94 @@
     back_a = [0] + order_a[:-1]
     back_b = [0] + order_b[:-1]
     shard_units = gate_weight.shape[0]
-    if shard_units % 128 == 0:
-        gate_up_blocks = pl.pallas_call(
+    shard_rows = down_weight.shape[0]
+    half = count // 2
+    direct = shard_units % 128 == 0 and shard_rows % 16 == 0
+    if direct:
+        columns = 512
+        first = units // columns
+        last = heads * size // columns
+        pair_block = pl.BlockSpec((half, shard_rows, columns), lambda k, side: (0, 0, k))
+        pair_shape = array((half, shard_rows, units + heads * size), low)
+        fixed = pl.BlockSpec(
+            (tokens_all, width), lambda k, side: (0, 0), pipeline_mode=pl.Buffered(1)
+        )
+        pair_send, pair_keep = pl.pallas_call(
+            functools.partial(pair_grad_kernel, first),
+            out_shape=[pair_shape, pair_shape],
+            grid_spec=pltpu.PrefetchScalarGridSpec(
+                num_scalar_prefetch=1,
+                grid=(first + last,),
+                in_specs=[
+                    pl.BlockSpec(
+                        (tokens_all, columns), lambda k, side: (0, jnp.minimum(k, first - 1))
+                    ),
+                    pl.BlockSpec(
+                        (tokens_all, columns), lambda k, side: (0, jnp.maximum(k - first, 0))
+                    ),
+                    fixed,
+                    fixed,
+                ],
+                out_specs=[pair_block, pair_block],
+                scratch_shapes=[
+                    pltpu.VMEM((width, tokens_all), low),
+                    pltpu.VMEM((width, columns), f32),
+                ],
+            ),
+            compiler_params=kernel_params(),
+            cost_estimate=pl.CostEstimate(
+                flops=2 * tokens_all * width * (units + heads * size),
+                bytes_accessed=13_000_000,
+                transcendentals=0,
+            ),
+        )(core_side, flat(product_low), flat(mixed), flat(grad_down_low), flat(grad_attended_low))
+        down_out_sum = RowSum.from_halves(pair_keep, pair_send, back_b)
+
+        def shard_of(g, side):
+            return (0, 2 * (g % half) + jnp.where(g < half, 1 - side[0], side[0]))
+
+        block_shape = (1, width, 2 * shard_units)
+        half_shape = array((half, width, 2 * shard_units), low)
+        gate_up_send, gate_up_keep = pl.pallas_call(
             gate_up_grad_kernel,
-            grid=(count,),
-            out_shape=array((count, 2 * shard_units, width), low),
-            in_specs=[
-                pl.BlockSpec((tokens_all, shard_units), lambda i: (0, i)),
-                pl.BlockSpec((tokens_all, shard_units), lambda i: (0, i)),
-                whole(tokens_all, width),
-            ],
-            out_specs=pl.BlockSpec((1, 2 * shard_units, width), lambda i: (i, 0, 0)),
+            out_shape=[half_shape, half_shape],
+            grid_spec=pltpu.PrefetchScalarGridSpec(
+                num_scalar_prefetch=1,
+                grid=(count,),
+                in_specs=[
+                    pl.BlockSpec((tokens_all, shard_units), shard_of),
+                    pl.BlockSpec((tokens_all, shard_units), shard_of),
+                    fixed,
+                    anywhere,
+                ],
+                out_specs=[
+                    pl.BlockSpec(block_shape, lambda g, side: (jnp.minimum(g, half - 1), 0, 0)),
+                    pl.BlockSpec(block_shape, lambda g, side: (jnp.maximum(g - half, 0), 0, 0)),
+                ],
+                scratch_shapes=[pltpu.VMEM((width, tokens_all), low)],
+            ),
             compiler_params=kernel_params(),
             cost_estimate=pl.CostEstimate(
                 flops=4 * tokens_all * width * units, bytes_accessed=14_000_000, transcendentals=0
             ),
-        )(flat(grad_gate_low), flat(grad_up_low), flat(pre_low))
+        )(core_side, flat(grad_gate_low), flat(grad_up_low), flat(pre_low), pair_send)
+        gate_up_sum = RowSum.from_halves(gate_up_keep, gate_up_send, back_a)
     else:
-        gate_up_blocks = jnp.concatenate(
-            [grad_blocks(grad_gate_low, pre_low), grad_blocks(grad_up_low, pre_low)], axis=1
+        down_out_sum = RowSum(
+            [grad_blocks(grad_down_low, product_low), grad_blocks(grad_attended_low, mixed)],
+            back_b,
+            -1,
         )
-    gate_up_part = lax.psum_scatter(gate_up_blocks, "dp", scatter_dimension=0, tiled=False)
-    down_out_sum = RowSum(
-        [
-            grad_blocks(grad_down_low, product_low),
-            grad_blocks(grad_attended_low, mixed),
-        ],
-        back_b,
-        -1,
-    )
-    down_out_core = down_out_sum.step(back_b[0])
+        down_out_sum.step(0)
+
+        def turned_blocks(gradient):
+            product = weight_grad(flat(pre_low), flat(gradient)).astype(low)
+            return product.reshape(width, count, shard_units).transpose(1, 0, 2)
+
+        gate_up_sum = RowSum(
+            [turned_blocks(grad_gate_low), turned_blocks(grad_up_low)], back_a, -1
+        )
+        gate_up_sum.step(0)
 
     def at_seq(s, *tail):
         return pl.BlockSpec((1,) + tail, lambda g: (s,) + (0,) * len(tail))
@@ -770,7 +951,8 @@
 
     downward = [(i + 1, i) for i in range(shards - 1)]
     grad_query_low = None
-    arrived = [down_out_sum.sent]
+    down_out_sum.step(back_b[1])
+    arrived = [gate_up_sum.sent, down_out_sum.sent]
     own_parts, query_gains, near_sums, from_near = [], [], [], []
     for s in range(seqs):
         grad_far, grad_near, grad_own, grad_query_low, g_part = attend_back(
@@ -786,18 +968,21 @@
         near_sums.append(near_sum)
         from_near.append(lax.ppermute(near_sum, "seq", downward))
         if s == 0:
-            down_out_sum.step(back_b[1])
-            arrived = [down_out_sum.sent, near_sums[0]]
+            gate_up_sum.step(back_a[1])
+            arrived = [gate_up_sum.sent]
         elif s == 1:
-            arrived = [from_near[0]]
+            arrived = [near_sums[0]]
+    for bit in back_b[2:]:
+        down_out_sum.step(bit)
     query_columns = heads * size
     grad_w_query = pl.pallas_call(
-        functools.partial(query_grad_kernel, 1),
+        functools.partial(query_grad_kernel, 2),
         grid=(heads,),
         out_shape=array((query_columns, width), low),
         in_specs=[
             pl.BlockSpec((tokens_all, size), lambda i: (0, i)),
             whole(tokens_all, width),
+            anywhere,
             anywhere,
         ],
         out_specs=pl.BlockSpec((size, width), lambda i: (i, 0)),
@@ -805,10 +990,10 @@
         cost_estimate=pl.CostEstimate(
             flops=2 * tokens_all * width * query_columns, bytes_accessed=5_000_000, transcendentals=0
         ),
-    )(flat(grad_query_low), flat(normed), near_sums[1])
-    for bit in back_b[2:]:
-        down_out_sum.step(bit)
-    down_out_last = down_out_sum.received[-1][0]
+    )(flat(grad_query_low), flat(normed), near_sums[1], down_out_sum.sent)
+    for bit in back_a[2:]:
+        gate_up_sum.step(bit)
+    down_out_part = down_out_sum.total()
 
     def input_back(s, buffers, arrived):
         kinds = [
@@ -860,7 +1045,7 @@
 
     buffers = []
     input_gains, key_gains = [], []
-    waits = [[grad_w_query, near_sums[-1]], [down_out_sum.sent], [down_out_last]]
+    waits = [[grad_w_query, near_sums[-1]], [gate_up_sum.sent], [down_out_part]]
     waits += [[]] * seqs
     for s in range(seqs):
         *buffers, g_part, g_key_part = input_back(s, buffers, waits[s])
@@ -888,9 +1073,10 @@
     )
     for bit in back_b:
         rest_sum.step(bit)
-    down_out_total = seq_sum(down_out_sum.total())
-    gate_total = seq_sum(gate_up_part[:shard_units])
-    up_total = seq_sum(gate_up_part[shard_units:])
+    down_out_total = seq_sum(down_out_part)
+    gate_up_part = gate_up_sum.total()
+    gate_total = seq_sum(gate_up_part[:, :shard_units]).T
+    up_total = seq_sum(gate_up_part[:, shard_units:]).T
     rest_total = seq_sum(rest_sum.total())
     query_total = rest_total[:query_rows]
     rest_total = rest_total[query_rows:]

time: 376 us -> 689 us (1.83)
  Pallas kernels: 127 us -> 482 us
  waiting for transfers between devices: 103 us -> 46.1 us
  local copies, waits for them, and re-layouts: 20.4 us -> 41.8 us
  between operations: 15.7 us -> 2.25 us
  starting transfers between devices: 67.6 us -> 77.3 us
    pallas_call x8 -> x17, Pallas kernels: 38 us -> 393 us  [the longest x10 333 us: stack_step(): pl.pallas_call(functools.partial(stack_kernel, axis, len(arrived)), out_s...]
    ppermute x3, waiting for transfers between devices: 25.8 us -> 0.01 us  [body(): from_near.append(lax.ppermute(near_sum, 'seq', downward))]
    unnamed x132 -> x175, local copies, waits for them, and re-layouts: 7.79 us -> 27.5 us
    ppermute x3 -> x8, waiting for transfers between devices: 17 us -> 0.02 us  [the longest x2 0.01 us: body(): gate_up_received = lax.ppermute(gate_up_half, 'dp', flips(order_a[i]))]
    ppermute x1, waiting for transfers between devices: 9.29 us -> 0.01 us  [body(): pair_near = lax.ppermute(pair_own, 'seq', upward)]
    convert_element_type x6 -> x9, other arithmetic: 5.45 us -> 13 us  [total(): return value.astype(jnp.bfloat16)]
  transfers between devices with their start and end apart: 37 -> 41, of which waited for: 18 -> 11; matrix products, arithmetic and copies ran while one was open for 10% -> 9% of each run, Pallas kernels for 24% -> 63%
where the time goes in v1:
time: 689 us; the launch traced here: 684 us
  Pallas kernels  482 us (70%)
  starting transfers between devices  77.3 us (11%)
  waiting for transfers between devices  46.1 us (7%)
  local copies, waits for them, and re-layouts  41.8 us (6%)
  other arithmetic  32.2 us (5%)
    pallas_call x10, Pallas kernels, stack_step(): pl.pallas_call(functools.partial(stack_kernel, axis, len(arrived)), out_s...  333 us
    pallas_call x6, Pallas kernels, seq_call(): pl.pallas_call(kernel, grid=(1,), out_shape=outs, in_specs=in_specs, out_...  41.5 us
    pallas_call x1, Pallas kernels, body(): call(functools.partial(middle_kernel, heads, 512), [array((seqs, rows, wi...  38 us
    ppermute x4, starting transfers between devices, seq_sum(): terms.append(lax.ppermute(total().astype(jnp.bfloat16), 'seq', pairs))  38 us
    unnamed x175, local copies, waits for them, and re-layouts  27.5 us
    pallas_call x1, Pallas kernels, body(): pl.pallas_call(functools.partial(tail_rows_kernel, 2), out_shape=array((s...  19 us
    ppermute x4, waiting for transfers between devices, seq_sum(): received = lax.ppermute(result.astype(jnp.bfloat16), 'seq', pairs)  16.7 us
  transfers between devices with their start and end apart: 41, of which 11 were waited for; matrix products, arithmetic and copies ran while one was open for 9% of the time, Pallas kernels for 63%

profile of v1, /device:TPU:0, one launch (start us, length us, event | category | flops | bytes accessed | tf_op | source)
XLA Modules:
  0.0 683.7 jit_solution(946007766896846180)
XLA Ops:
  3.7 3.0 collective-permute-start
  10.4 7.3 %shard_map.468.own_ref = bf16[2,80,640]{2,1,0:T(8,128)(2,1)} custom-call(s32[1]{0:T(128)} %bitcast.2.side_ref, bf16[80,640]{1,0:T(8,128)(2,1)} %get-tuple-element.76.own_ref, bf16[80,640]{1,0:T(8,128)(2,1)} %copy-done.60), custom_call_target="tpu_custom_call" | custom-call | tf_op jit(solution)/shard_map/pallas_call | solution.py:435
  20.5 3.8 collective-permute-done.1.received_ref.refs_1_
  24.9 13.5 %shard_map.469.own_ref = bf16[2,2,80,640]{3,2,1,0:T(8,128)(2,1)} custom-call(s32[1]{0:T(128)} %bitcast.1.side_ref, bf16[2,80,640]{2,1,0:T(8,128)(2,1)} %shard_map.468.own_ref, bf16[2,80,640]{2,1,0:T(8,128)(2,1)} %copy-done.37), custom_call_target="tpu_custom_call" | custom-call | tf_op jit(solution)/shard_map/pallas_call | solution.py:435
  41.0 11.0 %shard_map.472.own_ref = bf16[2,128,640]{2,1,0:T(8,128)(2,1)} custom-call(s32[1]{0:T(128)} %bitcast.1.side_ref, bf16[128,640]{1,0:T(8,128)(2,1)} %get-tuple-element.78.own_ref, bf16[128,640]{1,0:T(8,128)(2,1)} %copy-done.59), custom_call_target="tpu_custom_call" | custom-call | tf_op jit(solution)/shard_map/pallas_call | solution.py:435
  53.4 2.7 multiply_sine_fusion
  56.1 6.3 collective-permute-done.4.received_ref.refs_0_
  63.1 21.0 %shard_map.473.own_ref = bf16[2,2,128,640]{3,2,1,0:T(8,128)(2,1)} custom-call(s32[1]{0:T(128)} %bitcast.2.side_ref, bf16[2,128,640]{2,1,0:T(8,128)(2,1)} %shard_map.472.own_ref, bf16[2,128,640]{2,1,0:T(8,128)(2,1)} %copy-done.30), custom_call_target="tpu_custom_call" | custom-call | tf_op jit(solution)/shard_map/pallas_call | solution.py:435
  84.2 2.6 shard_map.475
  90.3 25.9 %shard_map.470 = bf16[2,2,2,80,640]{4,3,2,1,0:T(8,128)(2,1)} custom-call(s32[1]{0:T(128)} %bitcast.side_ref, bf16[2,2,80,640]{3,2,1,0:T(8,128)(2,1)} %shard_map.469.own_ref, bf16[2,2,80,640]{3,2,1,0:T(8,128)(2,1)} %copy-done.49), custom_call_target="tpu_custom_call" | custom-call | tf_op jit(solution)/shard_map/pallas_call | solution.py:435
  118.3 2.0 fusion.43
  120.2 4.9 shard_map.471
  125.1 3.5 collective-permute-start.7
  129.5 40.8 %shard_map.474 = bf16[2,2,2,128,640]{4,3,2,1,0:T(8,128)(2,1)} custom-call(s32[1]{0:T(128)} %bitcast.side_ref, bf16[2,2,128,640]{3,2,1,0:T(8,128)(2,1)} %shard_map.473.own_ref, bf16[2,2,128,640]{3,2,1,0:T(8,128)(2,1)} %copy-done.46), custom_call_target="tpu_custom_call" | custom-call | tf_op jit(solution)/shard_map/pallas_call | solution.py:435
  171.1 5.7 shard_map.476
  177.7 40.8 %shard_map.478.refs_1_.own_ref = bf16[2,512,640]{2,1,0:T(8,128)(2,1)} custom-call(s32[1]{0:T(128)} %bitcast.1.side_ref, bf16[512,640]{1,0:T(8,128)(2,1)} %get-tuple-element.82.own_ref, bf16[512,640]{1,0:T(8,128)(2,1)} %copy-done.40, bf16[3,2,640,256]{3,2,1,0:T(8,128)(2,1)} %get-tuple-element.80.refs_0_.q_ref), custom_call_target="tpu_custom_call" | custom-call | tf_op jit(solution)/shard_map/pallas_call | solution.py:435
  219.1 30.9 %shard_map.477.refs_0_.own_ref = bf16[2,80,3072]{2,1,0:T(8,128)(2,1)} custom-call(s32[1]{0:T(128)} %bitcast.2.side_ref, bf16[80,3072]{1,0:T(8,128)(2,1)} %get-tuple-element.79.own_ref, bf16[80,3072]{1,0:T(8,128)(2,1)} %copy-done.48, bf16[3,2,640,256]{3,2,1,0:T(8,128)(2,1)} %get-tuple-element.80.refs_0_.q_ref), custom_call_target="tpu_custom_call" | custom-call | tf_op jit(solution)/shard_map/pallas_call | solution.py:435
  250.9 19.0 %shard_map.479 = bf16[3,192,512]{2,1,0:T(8,128)(2,1)} custom-call(bf16[3,320,512]{2,1,0:T(8,128)(2,1)} %copy-done.36, bf16[2,80,3072]{2,1,0:T(8,128)(2,1)} %shard_map.477.refs_0_.own_ref, bf16[2,512,640]{2,1,0:T(8,128)(2,1)} %shard_map.478.refs_1_.own_ref), custom_call_target="tpu_custom_call" | custom-call | tf_op jit(solution)/shard_map/pallas_call | solution.py:688
  273.4 80.5 %shard_map.481 = bf16[2,2,512,640]{3,2,1,0:T(8,128)(2,1)} custom-call(s32[1]{0:T(128)} %bitcast.2.side_ref, bf16[2,512,640]{2,1,0:T(8,128)(2,1)} %shard_map.478.refs_1_.own_ref, bf16[2,512,640]{2,1,0:T(8,128)(2,1)} %copy-done.27, bf16[3,192,512]{2,1,0:T(8,128)(2,1)} %copy-done.17), custom_call_target="tpu_custom_call" | custom-call | tf_op jit(solution)/shard_map/pallas_call | solution.py:435
  354.0 60.7 %shard_map.482 = bf16[2,2,80,3072]{3,2,1,0:T(8,128)(2,1)} custom-call(s32[1]{0:T(128)} %bitcast.1.side_ref, bf16[2,80,3072]{2,1,0:T(8,128)(2,1)} %shard_map.477.refs_0_.own_ref, bf16[2,80,3072]{2,1,0:T(8,128)(2,1)} %collective-permute-done.12.received_ref, bf16[3,192,512]{2,1,0:T(8,128)(2,1)} %copy-done.17), custom_call_target="tpu_custom_call" | custom-call | tf_op jit(solution)/shard_map/pallas_call | solution.py:435
  415.2 7.8 %shard_map.480.mixed_ref = bf16[3,320,1024]{2,1,0:T(8,128)(2,1)} custom-call(bf16[3,2,640,256]{3,2,1,0:T(8,128)(2,1)} %get-tuple-element.80.refs_0_.q_ref, bf16[3,192,512]{2,1,0:T(8,128)(2,1)} %copy-done.17, bf16[3,320,512]{2,1,0:T(8,128)(2,1)} %copy-done.36, bf16[3,320,512]{2,1,0:T(8,128)(2,1)} %get-tuple-element.81.own_ref, ...), custom_call_target="tpu_custom_call" | custom-call | flops 5284823040 | bytes 16000000 | tf_op jit(solution)/shard_map/pallas_call | solution.py:709
  424.3 38.0 %shard_map.483 = (bf16[3,320,640]{2,1,0:T(8,128)(2,1)}, bf16[3,320,640]{2,1,0:T(8,128)(2,1)}, bf16[3,320,2048]{2,1,0:T(8,128)(2,1)}, bf16[3,320,640]{2,1,0:T(8,1...) custom-call(s32[1]{0:T(128)} %bitcast.side_ref, ...), custom_call_target="tpu_custom_call" | custom-call | flops 17616076800 | bytes 40000000 | tf_op jit(solution)/shard_map/pallas_call | solution.py:730
  462.3 10.3 %shard_map.484 = (bf16[4,80,3072]{2,1,0:T(8,128)(2,1)}, bf16[4,80,3072]{2,1,0:T(8,128)(2,1)}) custom-call(s32[1]{0:T(128)} %bitcast.side_ref, bf16[960,2048]{1,0:T(8,128)(2,1)} %bitcast.173, bf16[960,1024]{1,0:T(8,128)(2,1)} %bitcast.174, bf16[960,640]{1,0:T(8,128)(2,1)} %bitcast.176, bf16[960,640]{1,0:T(8,128)(2,1)} %bitcast.177), custom_call_target="tpu_custom_call" | custom-call | flops 3774873600 | bytes 13000000 | tf_op jit(solution)/shard_map/pallas_call | solution.py:805
  472.7 12.6 %shard_map.485 = (bf16[4,640,512]{2,1,0:T(8,128)(2,1)}, bf16[4,640,512]{2,1,0:T(8,128)(2,1)}) custom-call(s32[1]{0:T(128)} %bitcast.side_ref, bf16[960,2048]{1,0:T(8,128)(2,1)} %bitcast.171, bf16[960,2048]{1,0:T(8,128)(2,1)} %bitcast.172, bf16[960,640]{1,0:T(8,128)(2,1)} %bitcast.175, bf16[4,80,3072]{2,1,0:T(8,128)(2,1)} %get-tuple-element.92.after_ref), custom_call_target="tpu_custom_call" | custom-call | flops 5033164800 | bytes 14000000 | tf_op jit(solution)/shard_map/pallas_call | solution.py:841
  485.7 2.5 fusion.6.refs_1_
  488.2 9.1 %shard_map.486 = (bf16[1,192,512]{2,1,0:T(8,128)(2,1)}, f32[1,320,512]{2,1,0:T(8,128)}, f32[1,320,512]{2,1,0:T(8,128)}, bf16[3,320,1024]{2,1,0:T(8,128)(2,1)}, f32[1,1,256]{2,1,0:T(1,128)}) custom-call(bf16[3,2,640,256]{3,2,1,0:T(8,128)(2,1)} %get-tuple-element.80.refs_0_.q_ref, bf16[3,2,640,256]{3,2,1,0:T(8,128)(2,1)} %get-tuple-element.84.qraw_ref, ...), custom_call_target="tpu_custom_call" | custom-call | flops 5284823040 | bytes 8000000 | tf_op jit(solution)/shard_map/pallas_call | solution.py:886
  503.7 2.2 copy.118
  511.1 2.7 fusion.1.refs_1_
  515.4 9.1 %shard_map.487 = (bf16[1,192,512]{2,1,0:T(8,128)(2,1)}, f32[1,320,512]{2,1,0:T(8,128)}, f32[1,320,512]{2,1,0:T(8,128)}, bf16[3,320,1024]{2,1,0:T(8,128)(2,1)}, f32[1,1,256]{2,1,0:T(1,128)}) custom-call(bf16[3,2,640,256]{3,2,1,0:T(8,128)(2,1)} %get-tuple-element.80.refs_0_.q_ref, ...), custom_call_target="tpu_custom_call", output_to_operand_aliasing={{3}: (12, {})} | custom-call | flops 5284823040 | bytes 8000000 | tf_op jit(solution)/shard_map/pallas_call | solution.py:886
  525.8 9.2 %shard_map.488 = (bf16[1,192,512]{2,1,0:T(8,128)(2,1)}, f32[1,320,512]{2,1,0:T(8,128)}, f32[1,320,512]{2,1,0:T(8,128)}, bf16[3,320,1024]{2,1,0:T(8,128)(2,1)}, f32[1,1,256]{2,1,0:T(1,128)}) custom-call(bf16[3,2,640,256]{3,2,1,0:T(8,128)(2,1)} %get-tuple-element.80.refs_0_.q_ref, ...), custom_call_target="tpu_custom_call", output_to_operand_aliasing={{3}: (12, {})} | custom-call | flops 5284823040 | bytes 8000000 | tf_op jit(solution)/shard_map/pallas_call | solution.py:886
  542.7 5.2 shard_map.489.refs_0_
  547.9 4.7 shard_map.490
  552.7 2.4 collective-permute-done.24
  556.5 20.7 %collective-permute-start.31 = (bf16[80,3072]{1,0:T(8,128)(2,1)S(1)}, bf16[80,3072]{1,0:T(8,128)(2,1)S(1)}, u32[]{:S(2)}, u32[]{:S(2)}) collective-permute-start(bf16[80,3072]{1,0:T(8,128)(2,1)S(1)} %fusion.8.refs_2_), channel_id=1, source_target_pairs={{0,1},{3,2},{4,5},{7,6},{8,9},{11,10},{12,13},{15,14},{16,17},{19,... | collective-permute-start | bytes 1474568 | tf_op jit(solution)/shard_map/ppermute | solution.py:518
  579.6 2.6 fusion.4.refs_2_
  582.8 4.0 collective-permute-done.31
  589.1 4.7 shard_map.491
  594.5 4.8 shard_map.492
  599.3 2.2 fusion
  611.1 7.5 %collective-permute-start.35 = (bf16[640,256]{1,0:T(8,128)(2,1)S(1)}, bf16[640,256]{1,0:T(8,128)(2,1)S(1)}, u32[]{:S(2)}, u32[]{:S(2)}) collective-permute-start(bf16[640,256]{1,0:T(8,128)(2,1)S(1)} %get-tuple-element.240), channel_id=1, source_target_pairs={{0,1},{3,2},{4,5},{7,6},{8,9},{11,10},{12,13},{15,14},{16,17},{19,... | collective-permute-start | bytes 983048 | tf_op jit(solution)/shard_map/ppermute | solution.py:518
  620.7 5.3 collective-permute-done.33
  627.3 5.3 collective-permute-done.38
  636.7 4.9 collective-permute-done.27
  641.9 8.5 %collective-permute-start.28 = (bf16[208,640]{1,0:T(8,128)(2,1)S(1)}, bf16[208,640]{1,0:T(8,128)(2,1)S(1)}, u32[]{:S(2)}, u32[]{:S(2)}) collective-permute-start(bf16[208,640]{1,0:T(8,128)(2,1)S(1)} %fusion.21), channel_id=1, source_target_pairs={{0,1},{3,2},{4,5},{7,6},{8,9},{11,10},{12,13},{15,14},{16,17},{19,... | collective-permute-start | bytes 798728 | tf_op jit(solution)/shard_map/ppermute | solution.py:518
  658.6 4.5 collective-permute-done.37
  663.1 6.8 collective-permute-done.40
  670.0 2.1 multiply_subtract_fusion.1
  672.1 2.2 copy.123
  (302 shorter events, 93.5 us)
Async XLA Ops:
  0.7 37.9 %copy-start.65 = (s32[3,1280]{1,0:T(4,128)S(1)}, s32[3,1280]{1,0:T(4,128)}, u32[]{:S(2)}) copy-start(s32[3,1280]{1,0:T(4,128)} %param.30) | copy-start | bytes 46084
  0.7 39.6 %copy-start.68 = (s32[3,320]{1,0:T(4,128)S(1)}, s32[3,320]{1,0:T(4,128)}, u32[]{:S(2)}) copy-start(s32[3,320]{1,0:T(4,128)} %param.31) | copy-start | bytes 11524
  3.7 6.1 collective-permute-start
  6.7 33.6 %collective-permute-start.3 = (bf16[128,640]{1,0:T(8,128)(2,1)}, bf16[128,640]{1,0:T(8,128)(2,1)S(1)}, u32[]{:S(2)}, u32[]{:S(2)}) collective-permute-start(bf16[128,640]{1,0:T(8,128)(2,1)} %get-tuple-element.78.own_ref), channel_id=1, source_target_pairs={{0,8},{4,12},{8,0},{12,4},{16,24},{20,28},{24,16},{28,20},{1,9},{5... | collective-permute-start | bytes 491528 | tf_op jit(solution)/shard_map/ppermute | solution.py:447
  17.7 6.5 collective-permute-start.1
  38.5 51.1 %collective-permute-start.2 = (bf16[2,2,80,640]{3,2,1,0:T(8,128)(2,1)}, bf16[2,2,80,640]{3,2,1,0:T(8,128)(2,1)S(1)}, u32[]{:S(2)}, u32[]{:S(2)}) collective-permute-start(bf16[2,2,80,640]{3,2,1,0:T(8,128)(2,1)} %shard_map.469.own_ref), channel_id=1, source_target_pairs={{0,4},{4,0},{8,12},{12,8},{16,20},{20,16},{24,28},{28,24},{1,5},{5... | collective-permute-start | bytes 1228808 | tf_op jit(solution)/shard_map/ppermute | solution.py:447
  52.0 10.4 %collective-permute-start.4 = (bf16[2,128,640]{2,1,0:T(8,128)(2,1)}, bf16[2,128,640]{2,1,0:T(8,128)(2,1)S(1)}, u32[]{:S(2)}, u32[]{:S(2)}) collective-permute-start(bf16[2,128,640]{2,1,0:T(8,128)(2,1)} %shard_map.472.own_ref), channel_id=1, source_target_pairs={{0,16},{4,20},{8,24},{12,28},{16,0},{20,4},{24,8},{28,12},{1,17},{... | collective-permute-start | bytes 983048 | tf_op jit(solution)/shard_map/ppermute | solution.py:447
  84.1 44.6 %collective-permute-start.5 = (bf16[2,2,128,640]{3,2,1,0:T(8,128)(2,1)}, bf16[2,2,128,640]{3,2,1,0:T(8,128)(2,1)S(1)}, u32[]{:S(2)}, u32[]{:S(2)}) collective-permute-start(bf16[2,2,128,640]{3,2,1,0:T(8,128)(2,1)} %shard_map.473.own_ref), channel_id=1, source_target_pairs={{0,4},{4,0},{8,12},{12,8},{16,20},{20,16},{24,28},{28,24},{1,5},{5... | collective-permute-start | bytes 1966088 | tf_op jit(solution)/shard_map/ppermute | solution.py:447
  86.8 83.5 %collective-permute-start.6 = (bf16[80,3072]{1,0:T(8,128)(2,1)}, bf16[80,3072]{1,0:T(8,128)(2,1)S(1)}, u32[]{:S(2)}, u32[]{:S(2)}) collective-permute-start(bf16[80,3072]{1,0:T(8,128)(2,1)} %get-tuple-element.79.own_ref), channel_id=1, source_target_pairs={{0,16},{4,20},{8,24},{12,28},{16,0},{20,4},{24,8},{28,12},{1,17},{... | collective-permute-start | bytes 1474568 | tf_op jit(solution)/shard_map/ppermute | solution.py:657
  88.1 88.8 %collective-permute-start.8 = (bf16[512,640]{1,0:T(8,128)(2,1)}, bf16[512,640]{1,0:T(8,128)(2,1)S(1)}, u32[]{:S(2)}, u32[]{:S(2)}) collective-permute-start(bf16[512,640]{1,0:T(8,128)(2,1)} %get-tuple-element.82.own_ref), channel_id=1, source_target_pairs={{0,8},{4,12},{8,0},{12,4},{16,24},{20,28},{24,16},{28,20},{1,9},{5... | collective-permute-start | bytes 1966088 | tf_op jit(solution)/shard_map/ppermute | solution.py:683
  125.1 124.9 %collective-permute-start.7 = (bf16[3,320,512]{2,1,0:T(8,128)(2,1)}, bf16[3,320,512]{2,1,0:T(8,128)(2,1)S(1)}, u32[]{:S(2)}, u32[]{:S(2)}) collective-permute-start(bf16[3,320,512]{2,1,0:T(8,128)(2,1)} %get-tuple-element.81.own_ref), channel_id=1, source_target_pairs={{0,1},{1,2},{2,3},{4,5},{5,6},{6,7},{8,9},{9,10},{10,11},{12,13},{... | collective-permute-start | bytes 2949128 | tf_op jit(solution)/shard_map/ppermute | solution.py:676
  218.5 53.0 %collective-permute-start.10 = (bf16[2,512,640]{2,1,0:T(8,128)(2,1)}, bf16[2,512,640]{2,1,0:T(8,128)(2,1)S(1)}, u32[]{:S(2)}, u32[]{:S(2)}) collective-permute-start(bf16[2,512,640]{2,1,0:T(8,128)(2,1)} %shard_map.478.refs_1_.own_ref), channel_id=1, source_target_pairs={{0,16},{4,20},{8,24},{12,28},{16,0},{20,4},{24,8},{28,12},{1,17},{... | collective-permute-start | bytes 3932168 | tf_op jit(solution)/shard_map/ppermute | solution.py:683
  250.0 20.9 %copy-start.3 = (bf16[2,80,3072]{2,1,0:T(8,128)(2,1)S(1)}, bf16[2,80,3072]{2,1,0:T(8,128)(2,1)}, u32[]{:S(2)}) copy-start(bf16[2,80,3072]{2,1,0:T(8,128)(2,1)} %shard_map.477.refs_0_.own_ref) | copy-start | bytes 2949124
  269.9 1.5 collective-permute-start.9
  270.9 83.1 %collective-permute-start.12 = (bf16[2,80,3072]{2,1,0:T(8,128)(2,1)S(1)}, bf16[2,80,3072]{2,1,0:T(8,128)(2,1)}, u32[]{:S(2)}, u32[]{:S(2)}) collective-permute-start(bf16[2,80,3072]{2,1,0:T(8,128)(2,1)S(1)} %copy-done.3), channel_id=1, source_target_pairs={{0,8},{4,12},{8,0},{12,4},{16,24},{20,28},{24,16},{28,20},{1,9},{5... | collective-permute-start | bytes 2949128 | tf_op jit(solution)/shard_map/ppermute | solution.py:682
  353.9 69.1 %collective-permute-start.11 = (bf16[4,512,640]{2,1,0:T(8,128)(2,1)}, bf16[4,512,640]{2,1,0:T(8,128)(2,1)}, u32[]{:S(2)}, u32[]{:S(2)}) collective-permute-start(bf16[4,512,640]{2,1,0:T(8,128)(2,1)} %bitcast.151), channel_id=1, source_target_pairs={{0,4},{4,0},{8,12},{12,8},{16,20},{20,16},{24,28},{28,24},{1,5},{5... | collective-permute-start | bytes 7864328 | tf_op jit(solution)/shard_map/ppermute | solution.py:699
  414.7 8.3 %collective-permute-start.13 = (bf16[4,80,3072]{2,1,0:T(8,128)(2,1)}, bf16[4,80,3072]{2,1,0:T(8,128)(2,1)S(1)}, u32[]{:S(2)}, u32[]{:S(2)}) collective-permute-start(bf16[4,80,3072]{2,1,0:T(8,128)(2,1)} %bitcast.156), channel_id=1, source_target_pairs={{0,4},{4,0},{8,12},{12,8},{16,20},{20,16},{24,28},{28,24},{1,5},{5... | collective-permute-start | bytes 5898248 | tf_op jit(solution)/shard_map/ppermute | solution.py:698
  472.7 13.1 %collective-permute-start.14 = (bf16[4,80,3072]{2,1,0:T(8,128)(2,1)}, bf16[4,80,3072]{2,1,0:T(8,128)(2,1)}, u32[]{:S(2)}, u32[]{:S(2)}) collective-permute-start(bf16[4,80,3072]{2,1,0:T(8,128)(2,1)} %get-tuple-element.92.after_ref), channel_id=1, source_target_pairs={{0,4},{4,0},{8,12},{12,8},{16,20},{20,16},{24,28},{28,24},{1,5},{5... | collective-permute-start | bytes 5898248 | tf_op jit(solution)/shard_map/ppermute | solution.py:469
  485.3 25.8 %collective-permute-start.15 = (bf16[4,640,512]{2,1,0:T(8,128)(2,1)}, bf16[4,640,512]{2,1,0:T(8,128)(2,1)}, u32[]{:S(2)}, u32[]{:S(2)}) collective-permute-start(bf16[4,640,512]{2,1,0:T(8,128)(2,1)} %get-tuple-element.93.refs_0_), channel_id=1, source_target_pairs={{0,4},{4,0},{8,12},{12,8},{16,20},{20,16},{24,28},{28,24},{1,5},{5... | collective-permute-start | bytes 7864328 | tf_op jit(solution)/shard_map/ppermute | solution.py:469
  497.4 10.1 %collective-permute-start.16 = (bf16[1,192,512]{2,1,0:T(8,128)(2,1)}, bf16[1,192,512]{2,1,0:T(8,128)(2,1)S(1)}, u32[]{:S(2)}, u32[]{:S(2)}) collective-permute-start(bf16[1,192,512]{2,1,0:T(8,128)(2,1)} %get-tuple-element.99), channel_id=1, source_target_pairs={{2,1},{3,2},{6,5},{7,6},{10,9},{11,10},{14,13},{15,14},{18,17},{19... | collective-permute-start | bytes 589832 | tf_op jit(solution)/shard_map/ppermute | solution.py:961
  505.9 30.6 %collective-permute-start.22 = (bf16[2,80,3072]{2,1,0:T(8,128)(2,1)}, bf16[2,80,3072]{2,1,0:T(8,128)(2,1)S(1)}, u32[]{:S(2)}, u32[]{:S(2)}) collective-permute-start(bf16[2,80,3072]{2,1,0:T(8,128)(2,1)} %fusion.6.refs_1_), channel_id=1, source_target_pairs={{0,16},{4,20},{8,24},{12,28},{16,0},{20,4},{24,8},{28,12},{1,17},{... | collective-permute-start | bytes 2949128 | tf_op jit(solution)/shard_map/ppermute | solution.py:500
  509.4 38.6 %collective-permute-start.21 = (bf16[1,320,512]{2,1,0:T(8,128)(2,1)S(1)}, bf16[1,320,512]{2,1,0:T(8,128)(2,1)}, u32[]{:S(2)}, u32[]{:S(2)}) collective-permute-start(bf16[1,320,512]{2,1,0:T(8,128)(2,1)S(1)} %add_convert_fusion.4.refs_1_), channel_id=1, source_target_pairs={{1,0},{2,1},{3,2},{5,4},{6,5},{7,6},{9,8},{10,9},{11,10},{13,12},{... | collective-permute-start | bytes 983048 | tf_op jit(solution)/shard_map/ppermute | solution.py:969
  513.9 65.7 %collective-permute-start.23 = (bf16[2,640,512]{2,1,0:T(8,128)(2,1)}, bf16[2,640,512]{2,1,0:T(8,128)(2,1)S(1)}, u32[]{:S(2)}, u32[]{:S(2)}) collective-permute-start(bf16[2,640,512]{2,1,0:T(8,128)(2,1)} %fusion.1.refs_1_), channel_id=1, source_target_pairs={{0,8},{4,12},{8,0},{12,4},{16,24},{20,28},{24,16},{28,20},{1,9},{5... | collective-permute-start | bytes 3932168 | tf_op jit(solution)/shard_map/ppermute | solution.py:500
  524.4 14.3 %collective-permute-start.19 = (bf16[1,192,512]{2,1,0:T(8,128)(2,1)}, bf16[1,192,512]{2,1,0:T(8,128)(2,1)}, u32[]{:S(2)}, u32[]{:S(2)}) collective-permute-start(bf16[1,192,512]{2,1,0:T(8,128)(2,1)} %get-tuple-element.108), channel_id=1, source_target_pairs={{2,1},{3,2},{6,5},{7,6},{10,9},{11,10},{14,13},{15,14},{18,17},{19... | collective-permute-start | bytes 589832 | tf_op jit(solution)/shard_map/ppermute | solution.py:961
  535.0 6.1 collective-permute-start.17
  538.1 17.0 %collective-permute-start.24 = (bf16[80,3072]{1,0:T(8,128)(2,1)S(1)}, bf16[80,3072]{1,0:T(8,128)(2,1)S(1)}, u32[]{:S(2)}, u32[]{:S(2)}) collective-permute-start(bf16[80,3072]{1,0:T(8,128)(2,1)S(1)} %fusion.9.refs_1_), channel_id=1, source_target_pairs={{0,8},{4,12},{8,0},{12,4},{16,24},{20,28},{24,16},{28,20},{1,9},{5... | collective-permute-start | bytes 1474568 | tf_op jit(solution)/shard_map/ppermute | solution.py:500
  539.8 49.3 %collective-permute-start.20 = (bf16[1,320,512]{2,1,0:T(8,128)(2,1)S(1)}, bf16[1,320,512]{2,1,0:T(8,128)(2,1)}, u32[]{:S(2)}, u32[]{:S(2)}) collective-permute-start(bf16[1,320,512]{2,1,0:T(8,128)(2,1)S(1)} %add_convert_fusion.2.refs_0_), channel_id=1, source_target_pairs={{1,0},{2,1},{3,2},{5,4},{6,5},{7,6},{9,8},{10,9},{11,10},{13,12},{... | collective-permute-start | bytes 983048 | tf_op jit(solution)/shard_map/ppermute | solution.py:969
  541.2 52.6 %collective-permute-start.18 = (bf16[1,320,512]{2,1,0:T(8,128)(2,1)S(1)}, bf16[1,320,512]{2,1,0:T(8,128)(2,1)S(1)}, u32[]{:S(2)}, u32[]{:S(2)}) collective-permute-start(bf16[1,320,512]{2,1,0:T(8,128)(2,1)S(1)} %add_convert_fusion.3.refs_1_), channel_id=1, source_target_pairs={{1,0},{2,1},{3,2},{5,4},{6,5},{7,6},{9,8},{10,9},{11,10},{13,12},{... | collective-permute-start | bytes 983048 | tf_op jit(solution)/shard_map/ppermute | solution.py:969
  552.7 24.6 %copy-start.2 = (bf16[1024,640]{1,0:T(8,128)(2,1)S(1)}, bf16[1024,640]{1,0:T(8,128)(2,1)}, u32[]{:S(2)}) copy-start(bf16[1024,640]{1,0:T(8,128)(2,1)} %shard_map.489.refs_0_) | copy-start | bytes 3932164
  556.5 30.2 %copy-start = (bf16[80,3072]{1,0:T(8,128)(2,1)}, bf16[80,3072]{1,0:T(8,128)(2,1)S(1)}, u32[]{:S(2)}) copy-start(bf16[80,3072]{1,0:T(8,128)(2,1)S(1)} %fusion.8.refs_2_) | copy-start | bytes 1474564
  556.5 30.2 %collective-permute-start.31 = (bf16[80,3072]{1,0:T(8,128)(2,1)S(1)}, bf16[80,3072]{1,0:T(8,128)(2,1)S(1)}, u32[]{:S(2)}, u32[]{:S(2)}) collective-permute-start(bf16[80,3072]{1,0:T(8,128)(2,1)S(1)} %fusion.8.refs_2_), channel_id=1, source_target_pairs={{0,1},{3,2},{4,5},{7,6},{8,9},{11,10},{12,13},{15,14},{16,17},{19,... | collective-permute-start | bytes 1474568 | tf_op jit(solution)/shard_map/ppermute | solution.py:518
  582.2 27.1 %collective-permute-start.34 = (bf16[640,512]{1,0:T(8,128)(2,1)}, bf16[640,512]{1,0:T(8,128)(2,1)}, u32[]{:S(2)}, u32[]{:S(2)}) collective-permute-start(bf16[640,512]{1,0:T(8,128)(2,1)} %fusion.4.refs_2_), channel_id=1, source_target_pairs={{0,16},{4,20},{8,24},{12,28},{16,0},{20,4},{24,8},{28,12},{1,17},{... | collective-permute-start | bytes 1966088 | tf_op jit(solution)/shard_map/ppermute | solution.py:500
  587.6 19.0 %collective-permute-start.32 = (bf16[80,3072]{1,0:T(8,128)(2,1)}, bf16[80,3072]{1,0:T(8,128)(2,1)}, u32[]{:S(2)}, u32[]{:S(2)}) collective-permute-start(bf16[80,3072]{1,0:T(8,128)(2,1)} %fusion.10), channel_id=1, source_target_pairs={{1,2},{2,1},{5,6},{6,5},{9,10},{10,9},{13,14},{14,13},{17,18},{18,... | collective-permute-start | bytes 1474568 | tf_op jit(solution)/shard_map/ppermute | solution.py:520
  605.7 14.3 %collective-permute-start.25 = (bf16[2,2,208,640]{3,2,1,0:T(8,128)(2,1)S(1)}, bf16[2,2,208,640]{3,2,1,0:T(8,128)(2,1)S(1)}, u32[]{:S(2)}, u32[]{:S(2)}) collective-permute-start(bf16[2,2,208,640]{3,2,1,0:T(8,128)(2,1)S(1)} %pad_maximum_fusion), channel_id=1, source_target_pairs={{0,4},{4,0},{8,12},{12,8},{16,20},{20,16},{24,28},{28,24},{1,5},{5... | collective-permute-start | bytes 3194888 | tf_op jit(solution)/shard_map/ppermute | solution.py:500
  608.1 18.0 %collective-permute-start.33 = (bf16[80,3072]{1,0:T(8,128)(2,1)S(1)}, bf16[80,3072]{1,0:T(8,128)(2,1)S(1)}, u32[]{:S(2)}, u32[]{:S(2)}) collective-permute-start(bf16[80,3072]{1,0:T(8,128)(2,1)S(1)} %fusion.16), channel_id=1, source_target_pairs={{1,0},{2,3},{5,4},{6,7},{9,8},{10,11},{13,12},{14,15},{17,16},{18,... | collective-permute-start | bytes 1474568 | tf_op jit(solution)/shard_map/ppermute | solution.py:524
  611.1 16.2 %collective-permute-start.35 = (bf16[640,256]{1,0:T(8,128)(2,1)S(1)}, bf16[640,256]{1,0:T(8,128)(2,1)S(1)}, u32[]{:S(2)}, u32[]{:S(2)}) collective-permute-start(bf16[640,256]{1,0:T(8,128)(2,1)S(1)} %get-tuple-element.240), channel_id=1, source_target_pairs={{0,1},{3,2},{4,5},{7,6},{8,9},{11,10},{12,13},{15,14},{16,17},{19,... | collective-permute-start | bytes 983048 | tf_op jit(solution)/shard_map/ppermute | solution.py:518
  618.6 14.0 %collective-permute-start.38 = (bf16[640,256]{1,0:T(8,128)(2,1)S(1)}, bf16[640,256]{1,0:T(8,128)(2,1)S(1)}, u32[]{:S(2)}, u32[]{:S(2)}) collective-permute-start(bf16[640,256]{1,0:T(8,128)(2,1)S(1)} %get-tuple-element.239), channel_id=1, source_target_pairs={{0,1},{3,2},{4,5},{7,6},{8,9},{11,10},{12,13},{15,14},{16,17},{19,... | collective-permute-start | bytes 983048 | tf_op jit(solution)/shard_map/ppermute | solution.py:518
  620.1 14.1 %collective-permute-start.26 = (bf16[2,208,640]{2,1,0:T(8,128)(2,1)S(1)}, bf16[2,208,640]{2,1,0:T(8,128)(2,1)S(1)}, u32[]{:S(2)}, u32[]{:S(2)}) collective-permute-start(bf16[2,208,640]{2,1,0:T(8,128)(2,1)S(1)} %fusion.5), channel_id=1, source_target_pairs={{0,16},{4,20},{8,24},{12,28},{16,0},{20,4},{24,8},{28,12},{1,17},{... | collective-permute-start | bytes 1597448 | tf_op jit(solution)/shard_map/ppermute | solution.py:500
  632.8 17.6 %collective-permute-start.36 = (bf16[640,256]{1,0:T(8,128)(2,1)S(1)}, bf16[640,256]{1,0:T(8,128)(2,1)S(1)}, u32[]{:S(2)}, u32[]{:S(2)}) collective-permute-start(bf16[640,256]{1,0:T(8,128)(2,1)S(1)} %get-tuple-element.238), channel_id=1, source_target_pairs={{1,2},{2,1},{5,6},{6,5},{9,10},{10,9},{13,14},{14,13},{17,18},{18,... | collective-permute-start | bytes 983048 | tf_op jit(solution)/shard_map/ppermute | solution.py:520
  633.5 16.9 %collective-permute-start.39 = (bf16[640,256]{1,0:T(8,128)(2,1)S(1)}, bf16[640,256]{1,0:T(8,128)(2,1)S(1)}, u32[]{:S(2)}, u32[]{:S(2)}) collective-permute-start(bf16[640,256]{1,0:T(8,128)(2,1)S(1)} %get-tuple-element.237), channel_id=1, source_target_pairs={{1,2},{2,1},{5,6},{6,5},{9,10},{10,9},{13,14},{14,13},{17,18},{18,... | collective-permute-start | bytes 983048 | tf_op jit(solution)/shard_map/ppermute | solution.py:520
  634.3 7.3 %collective-permute-start.27 = (bf16[208,640]{1,0:T(8,128)(2,1)S(1)}, bf16[208,640]{1,0:T(8,128)(2,1)S(1)}, u32[]{:S(2)}, u32[]{:S(2)}) collective-permute-start(bf16[208,640]{1,0:T(8,128)(2,1)S(1)} %fusion.19), channel_id=1, source_target_pairs={{0,8},{4,12},{8,0},{12,4},{16,24},{20,28},{24,16},{28,20},{1,9},{5... | collective-permute-start | bytes 798728 | tf_op jit(solution)/shard_map/ppermute | solution.py:500
  641.9 12.4 %collective-permute-start.28 = (bf16[208,640]{1,0:T(8,128)(2,1)S(1)}, bf16[208,640]{1,0:T(8,128)(2,1)S(1)}, u32[]{:S(2)}, u32[]{:S(2)}) collective-permute-start(bf16[208,640]{1,0:T(8,128)(2,1)S(1)} %fusion.21), channel_id=1, source_target_pairs={{0,1},{3,2},{4,5},{7,6},{8,9},{11,10},{12,13},{15,14},{16,17},{19,... | collective-permute-start | bytes 798728 | tf_op jit(solution)/shard_map/ppermute | solution.py:518
  650.6 12.5 %collective-permute-start.37 = (bf16[640,256]{1,0:T(8,128)(2,1)S(1)}, bf16[640,256]{1,0:T(8,128)(2,1)S(1)}, u32[]{:S(2)}, u32[]{:S(2)}) collective-permute-start(bf16[640,256]{1,0:T(8,128)(2,1)S(1)} %get-tuple-element.236), channel_id=1, source_target_pairs={{1,0},{2,3},{5,4},{6,7},{9,8},{10,11},{13,12},{14,15},{17,16},{18,... | collective-permute-start | bytes 983048 | tf_op jit(solution)/shard_map/ppermute | solution.py:524
  651.9 18.1 %collective-permute-start.40 = (bf16[640,256]{1,0:T(8,128)(2,1)S(1)}, bf16[640,256]{1,0:T(8,128)(2,1)S(1)}, u32[]{:S(2)}, u32[]{:S(2)}) collective-permute-start(bf16[640,256]{1,0:T(8,128)(2,1)S(1)} %get-tuple-element.235), channel_id=1, source_target_pairs={{1,0},{2,3},{5,4},{6,7},{9,8},{10,11},{13,12},{14,15},{17,16},{18,... | collective-permute-start | bytes 983048 | tf_op jit(solution)/shard_map/ppermute | solution.py:524
  654.2 15.8 %copy-start.14 = (f32[256,640]{0,1:T(8,128)S(1)}, f32[256,640]{0,1:T(8,128)}, u32[]{:S(2)}) copy-start(f32[256,640]{0,1:T(8,128)} %copy.118) | copy-start | bytes 1966084
  654.3 15.7 %copy-start.9 = (f32[256,640]{0,1:T(8,128)S(1)}, f32[256,640]{0,1:T(8,128)}, u32[]{:S(2)}) copy-start(f32[256,640]{0,1:T(8,128)} %copy.120) | copy-start | bytes 1966084
  654.3 2.0 collective-permute-start.29
  657.1 22.5 %collective-permute-start.30 = (bf16[208,640]{1,0:T(8,128)(2,1)}, bf16[208,640]{1,0:T(8,128)(2,1)}, u32[]{:S(2)}, u32[]{:S(2)}) collective-permute-start(bf16[208,640]{1,0:T(8,128)(2,1)} %fusion.23), channel_id=1, source_target_pairs={{1,0},{2,3},{5,4},{6,7},{9,8},{10,11},{13,12},{14,15},{17,16},{18,... | collective-permute-start | bytes 798728 | tf_op jit(solution)/shard_map/ppermute | solution.py:524
  (73 other events, 313.8 us)

commit v2 on v1

--- a/solution.py
+++ b/solution.py
@@ -120,46 +120,50 @@
 
 
 def stack_kernel(axis, waits, side_ref, own_ref, received_ref, *refs):
-    out_ref, sems = refs[waits:]
+    out_ref = refs[waits]
     upper = side_ref[0]
     lead = (slice(None),) * axis
-    mine = pltpu.make_async_copy(own_ref, out_ref.at[lead + (upper,)], sems.at[0])
-    other = pltpu.make_async_copy(received_ref, out_ref.at[lead + (1 - upper,)], sems.at[1])
-    mine.start()
-    other.start()
-    mine.wait()
-    other.wait()
+    out_ref[lead + (upper,)] = own_ref[...]
+    out_ref[lead + (1 - upper,)] = received_ref[...]
 
 
 def tail_rows_kernel(waits, near_ref, *refs):
-    out_ref, sem = refs[waits:]
-    rows = out_ref.shape[1]
-    copy = pltpu.make_async_copy(near_ref.at[:, near_ref.shape[1] - rows :], out_ref, sem)
-    copy.start()
-    copy.wait()
-
-
-def gate_up_grad_kernel(side_ref, dgate_ref, dup_ref, pre_ref, after_ref, send_ref, keep_ref, turned_ref):
+    out_ref = refs[waits]
+    out_ref[...] = near_ref[:, near_ref.shape[1] - out_ref.shape[1] :]
+
+
+def near_sum_kernel(waits, near_ref, far_ref, *refs):
+    out_ref = refs[waits]
+    keep = near_ref.shape[1] - far_ref.shape[1]
+    out_ref[0, :keep] = near_ref[0, :keep].astype(jnp.bfloat16)
+    total = near_ref[0, keep:] + far_ref[0].astype(jnp.float32)
+    out_ref[0, keep:] = total.astype(jnp.bfloat16)
+
+
+def sum_kernel(count, index_ref, *refs):
+    total = refs[0][0].astype(jnp.float32)
+    for ref in refs[1:count]:
+        total += ref[0].astype(jnp.float32)
+    refs[-1][0] = total.astype(jnp.bfloat16)
+
+
+def gate_up_grad_kernel(side_ref, dgate_ref, dup_ref, pre_ref, after_ref, send_ref, keep_ref):
     step = pl.program_id(0)
     half = pl.num_programs(0) // 2
     rows = dgate_ref.shape[1]
 
-    @pl.when(step == 0)
-    def _():
-        turned_ref[...] = pre_ref[...].T
-
-    gate = dot_nn(turned_ref[...], dgate_ref[...]).astype(jnp.bfloat16)
-    up = dot_nn(turned_ref[...], dup_ref[...]).astype(jnp.bfloat16)
+    gate = dot_tn(dgate_ref[...], pre_ref[...]).astype(jnp.bfloat16)
+    up = dot_tn(dup_ref[...], pre_ref[...]).astype(jnp.bfloat16)
 
     @pl.when(step < half)
     def _():
-        send_ref[0, :, :rows] = gate
-        send_ref[0, :, rows:] = up
+        send_ref[0, :rows, :] = gate
+        send_ref[0, rows:, :] = up
 
     @pl.when(step >= half)
     def _():
-        keep_ref[0, :, :rows] = gate
-        keep_ref[0, :, rows:] = up
+        keep_ref[0, :rows, :] = gate
+        keep_ref[0, rows:, :] = up
 
 
 def pair_grad_kernel(
@@ -431,13 +435,16 @@
 def stack_step(own, received, bit, done, arrived=()):
     axis = sum(1 for other in done if other > bit)
     anywhere = pl.BlockSpec(memory_space=pl.ANY)
+    block = pl.BlockSpec(memory_space=pltpu.VMEM)
     arrived = list(arrived)
     return pl.pallas_call(
         functools.partial(stack_kernel, axis, len(arrived)),
         out_shape=jax.ShapeDtypeStruct(own.shape[:axis] + (2,) + own.shape[axis:], own.dtype),
-        in_specs=[pl.BlockSpec(memory_space=pltpu.SMEM)] + [anywhere] * (2 + len(arrived)),
-        out_specs=anywhere,
-        scratch_shapes=[pltpu.SemaphoreType.DMA((2,))],
+        in_specs=[pl.BlockSpec(memory_space=pltpu.SMEM)]
+        + [block] * 2
+        + [anywhere] * len(arrived),
+        out_specs=block,
+        compiler_params=pltpu.CompilerParams(vmem_limit_bytes=VMEM_BYTES),
     )(side(bit)[None].astype(jnp.int32), own, received, *arrived)
 
 
@@ -484,6 +491,53 @@
             value += self.pick(part, bits, picks).astype(jnp.float32)
         return value.astype(jnp.bfloat16)
 
+    def ordered_total(self, after, other=None):
+        picks = dict(self.chosen)
+        if other is not None:
+            picks[other] = 1 - side(other)
+        left = [b for b in range(len(self.order) - 1, -1, -1) if b not in picks]
+        places = jnp.arange(2 ** len(left), dtype=jnp.int32)
+        terms = self.terms + self.received
+        index = []
+        for part, bits in terms:
+            flat = jnp.zeros_like(places)
+            for bit in bits:
+                if bit in picks:
+                    value = picks[bit]
+                else:
+                    value = (places >> (len(left) - 1 - left.index(bit))) & 1
+                flat = 2 * flat + value
+            index.append(flat)
+        block = terms[0][0].shape[-2:]
+        anywhere = pl.BlockSpec(memory_space=pl.ANY)
+
+        def spec(k):
+            return pl.BlockSpec((1,) + block, lambda g, index: (index[k, g], 0, 0))
+
+        out = pl.pallas_call(
+            functools.partial(sum_kernel, len(terms)),
+            out_shape=jax.ShapeDtypeStruct((len(places),) + block, jnp.bfloat16),
+            grid_spec=pltpu.PrefetchScalarGridSpec(
+                num_scalar_prefetch=1,
+                grid=(len(places),),
+                in_specs=[spec(k) for k in range(len(terms))] + [anywhere] * len(after),
+                out_specs=pl.BlockSpec((1,) + block, lambda g, index: (g, 0, 0)),
+            ),
+            compiler_params=kernel_params(),
+        )(jnp.stack(index), *[part.reshape((-1,) + block) for part, _ in terms], *after)
+        return out.reshape((2,) * len(left) + block)
+
+    def ordered_step(self, bit, after):
+        self.sent = self.ordered_total(after, bit)
+        self.receive(bit)
+
+    def receive(self, bit):
+        received = lax.ppermute(self.sent, "dp", flips(bit))
+        self.chosen[bit] = side(bit)
+        left = [b for b in range(len(self.order) - 1, -1, -1) if b not in self.chosen]
+        self.received.append((received, left))
+        return received
+
     def pick(self, part, bits, picks):
         bits = list(bits)
         for bit, where in picks.items():
@@ -497,11 +551,8 @@
         return self.sent
 
     def step(self, bit):
-        received = lax.ppermute(self.send(bit), "dp", flips(bit))
-        self.chosen[bit] = side(bit)
-        left = [b for b in range(len(self.order) - 1, -1, -1) if b not in self.chosen]
-        self.received.append((received, left))
-        return received
+        self.send(bit)
+        return self.receive(bit)
 
 
 def seq_sum(part):
@@ -688,9 +739,9 @@
             far_send = pl.pallas_call(
                 functools.partial(tail_rows_kernel, 2),
                 out_shape=array((seqs, far, 2 * size), low),
-                in_specs=[anywhere] * 3,
-                out_specs=anywhere,
-                scratch_shapes=[pltpu.SemaphoreType.DMA],
+                in_specs=[block, anywhere, anywhere],
+                out_specs=block,
+                compiler_params=pltpu.CompilerParams(vmem_limit_bytes=VMEM_BYTES),
             )(pair_near, pair_half, gate_up_half)
             pair_far = lax.ppermute(far_send, "seq", upward[1:])
     pair_half = pair_half.reshape((count // 2,) + pair_shard.shape)
@@ -836,8 +887,8 @@
         def shard_of(g, side):
             return (0, 2 * (g % half) + jnp.where(g < half, 1 - side[0], side[0]))
 
-        block_shape = (1, width, 2 * shard_units)
-        half_shape = array((half, width, 2 * shard_units), low)
+        block_shape = (1, 2 * shard_units, width)
+        half_shape = array((half, 2 * shard_units, width), low)
         gate_up_send, gate_up_keep = pl.pallas_call(
             gate_up_grad_kernel,
             out_shape=[half_shape, half_shape],
@@ -854,7 +905,6 @@
                     pl.BlockSpec(block_shape, lambda g, side: (jnp.minimum(g, half - 1), 0, 0)),
                     pl.BlockSpec(block_shape, lambda g, side: (jnp.maximum(g - half, 0), 0, 0)),
                 ],
-                scratch_shapes=[pltpu.VMEM((width, tokens_all), low)],
             ),
             compiler_params=kernel_params(),
             cost_estimate=pl.CostEstimate(
@@ -863,20 +913,15 @@
         )(core_side, flat(grad_gate_low), flat(grad_up_low), flat(pre_low), pair_send)
         gate_up_sum = RowSum.from_halves(gate_up_keep, gate_up_send, back_a)
     else:
-        down_out_sum = RowSum(
-            [grad_blocks(grad_down_low, product_low), grad_blocks(grad_attended_low, mixed)],
-            back_b,
-            -1,
+        pair_blocks = jnp.concatenate(
+            [grad_blocks(grad_down_low, product_low), grad_blocks(grad_attended_low, mixed)], axis=-1
         )
+        down_out_sum = RowSum([pair_blocks], back_b, -1)
         down_out_sum.step(0)
-
-        def turned_blocks(gradient):
-            product = weight_grad(flat(pre_low), flat(gradient)).astype(low)
-            return product.reshape(width, count, shard_units).transpose(1, 0, 2)
-
-        gate_up_sum = RowSum(
-            [turned_blocks(grad_gate_low), turned_blocks(grad_up_low)], back_a, -1
+        gate_up_blocks = jnp.concatenate(
+            [grad_blocks(grad_gate_low, pre_low), grad_blocks(grad_up_low, pre_low)], axis=-2
         )
+        gate_up_sum = RowSum([gate_up_blocks], back_a, -2)
         gate_up_sum.step(0)
 
     def at_seq(s, *tail):
@@ -951,9 +996,17 @@
 
     downward = [(i + 1, i) for i in range(shards - 1)]
     grad_query_low = None
-    down_out_sum.step(back_b[1])
-    arrived = [gate_up_sum.sent, down_out_sum.sent]
-    own_parts, query_gains, near_sums, from_near = [], [], [], []
+    arrived = [gate_up_sum.sent]
+
+    def near_total(grad_near, from_far, after):
+        return pl.pallas_call(
+            functools.partial(near_sum_kernel, len(after)),
+            out_shape=array(grad_near.shape, low),
+            in_specs=[block] * 2 + [anywhere] * len(after),
+            out_specs=block,
+        )(grad_near, from_far, *after)
+
+    own_parts, query_gains, near_sums, far_parts, near_parts = [], [], [], [], []
     for s in range(seqs):
         grad_far, grad_near, grad_own, grad_query_low, g_part = attend_back(
             s, grad_query_low, arrived
@@ -961,19 +1014,18 @@
         from_far = lax.ppermute(grad_far, "seq", downward[1:])
         own_parts.append(grad_own)
         query_gains.append(g_part)
-        near_sum = (
-            grad_near
-            + jnp.pad(from_far.astype(f32), ((0, 0), (rows - far, 0), (0, 0)))
-        ).astype(low)
-        near_sums.append(near_sum)
-        from_near.append(lax.ppermute(near_sum, "seq", downward))
+        far_parts.append(from_far)
+        near_parts.append(grad_near)
         if s == 0:
-            gate_up_sum.step(back_a[1])
+            down_out_sum.ordered_step(back_b[1], [grad_own])
+            gate_up_sum.ordered_step(back_a[1], [down_out_sum.sent])
             arrived = [gate_up_sum.sent]
         elif s == 1:
+            near_sums.append(near_total(near_parts[0], far_parts[0], [grad_own]))
             arrived = [near_sums[0]]
     for bit in back_b[2:]:
-        down_out_sum.step(bit)
+        down_out_sum.ordered_step(bit, [own_parts[-1]])
+    near_sums.append(near_total(near_parts[1], far_parts[1], [down_out_sum.sent]))
     query_columns = heads * size
     grad_w_query = pl.pallas_call(
         functools.partial(query_grad_kernel, 2),
@@ -991,9 +1043,10 @@
             flops=2 * tokens_all * width * query_columns, bytes_accessed=5_000_000, transcendentals=0
         ),
     )(flat(grad_query_low), flat(normed), near_sums[1], down_out_sum.sent)
+    near_sums.append(near_total(near_parts[2], far_parts[2], [grad_w_query]))
+    from_near = [lax.ppermute(near_sum, "seq", downward) for near_sum in near_sums]
     for bit in back_a[2:]:
-        gate_up_sum.step(bit)
-    down_out_part = down_out_sum.total()
+        gate_up_sum.ordered_step(bit, [near_sums[2]])
 
     def input_back(s, buffers, arrived):
         kinds = [
@@ -1045,14 +1098,16 @@
 
     buffers = []
     input_gains, key_gains = [], []
-    waits = [[grad_w_query, near_sums[-1]], [gate_up_sum.sent], [down_out_part]]
-    waits += [[]] * seqs
     for s in range(seqs):
-        *buffers, g_part, g_key_part = input_back(s, buffers, waits[s])
+        waits = [gate_up_sum.sent]
+        if s == seqs - 1:
+            down_out_part = down_out_sum.ordered_total([buffers[0]])
+            waits = [down_out_part]
+        *buffers, g_part, g_key_part = input_back(s, buffers, waits)
         input_gains.append(g_part)
         key_gains.append(g_key_part)
     input_grad, grad_pair_low = buffers
-    pair_blocks = grad_blocks(grad_pair_low, normed).reshape(2, count, key_rows, width)
+    key_value_blocks = grad_blocks(grad_pair_low, normed).reshape(2, count, key_rows, width)
     grad_gains = jnp.concatenate(
         [
             sum(input_gains).reshape(-1),
@@ -1067,16 +1122,21 @@
     )
     query_rows = query_weight.shape[0]
     rest_sum = RowSum(
-        [grad_w_query.reshape(count, query_rows, width), pair_blocks[0], pair_blocks[1], gain_block],
+        [
+            grad_w_query.reshape(count, query_rows, width),
+            key_value_blocks[0],
+            key_value_blocks[1],
+            gain_block,
+        ],
         back_b,
         -2,
     )
     for bit in back_b:
         rest_sum.step(bit)
     down_out_total = seq_sum(down_out_part)
-    gate_up_part = gate_up_sum.total()
-    gate_total = seq_sum(gate_up_part[:, :shard_units]).T
-    up_total = seq_sum(gate_up_part[:, shard_units:]).T
+    gate_up_part = gate_up_sum.ordered_total([input_grad])
+    gate_total = seq_sum(gate_up_part[:shard_units])
+    up_total = seq_sum(gate_up_part[shard_units:])
     rest_total = seq_sum(rest_sum.total())
     query_total = rest_total[:query_rows]
     rest_total = rest_total[query_rows:]

time: 689 us -> 368 us (0.53)
  Pallas kernels: 482 us -> 181 us
  waiting for transfers between devices: 46.1 us -> 64.1 us
  other arithmetic: 32.2 us -> 15.5 us
  starting transfers between devices: 77.3 us -> 63.2 us
  local copies, waits for them, and re-layouts: 41.8 us -> 32.7 us
    pallas_call x10, Pallas kernels: 333 us -> 22.6 us  [stack_step(): pl.pallas_call(functools.partial(stack_kernel, axis, len(arrived)), out_s...]
    pallas_call x0 -> x9, Pallas kernels: none -> 25.2 us  [the longest x6 19.5 us: ordered_total(): pl.pallas_call(functools.partial(sum_kernel, len(terms)), out_shape=jax.S...]
    ppermute x2, waiting for transfers between devices: 0.01 us -> 17.9 us  [body(): gate_up_received = lax.ppermute(gate_up_half, 'dp', flips(order_a[i]))]
    pallas_call x1, Pallas kernels: 19 us -> 2.05 us  [body(): pl.pallas_call(functools.partial(tail_rows_kernel, 2), out_shape=array((s...]
    convert_element_type x9 -> x3, other arithmetic: 13 us -> 0.43 us  [total(): return value.astype(jnp.bfloat16)]
    ppermute x4, starting transfers between devices: 38 us -> 27 us  [seq_sum(): terms.append(lax.ppermute(total().astype(jnp.bfloat16), 'seq', pairs))]
    unnamed x175 -> x131, local copies, waits for them, and re-layouts: 27.5 us -> 18.8 us
  transfers between devices with their start and end apart: 41 -> 41, of which waited for: 11 -> 14; matrix products, arithmetic and copies ran while one was open for 9% -> 8% of each run, Pallas kernels for 63% -> 33%
where the time goes in v2:
time: 368 us; the launch traced here: 362 us
  Pallas kernels  181 us (49%)
  waiting for transfers between devices  64.1 us (17%)
  starting transfers between devices  63.2 us (17%)
  local copies, waits for them, and re-layouts  32.7 us (9%)
  other arithmetic  15.5 us (4%)
    pallas_call x6, Pallas kernels, seq_call(): pl.pallas_call(kernel, grid=(1,), out_shape=outs, in_specs=in_specs, out_...  41.4 us
    pallas_call x1, Pallas kernels, body(): call(functools.partial(middle_kernel, heads, 512), [array((seqs, rows, wi...  38 us
    ppermute x4, starting transfers between devices, seq_sum(): terms.append(lax.ppermute(total().astype(jnp.bfloat16), 'seq', pairs))  27 us
    pallas_call x10, Pallas kernels, stack_step(): pl.pallas_call(functools.partial(stack_kernel, axis, len(arrived)), out_s...  22.6 us
    ppermute x4, waiting for transfers between devices, seq_sum(): received = lax.ppermute(result.astype(jnp.bfloat16), 'seq', pairs)  20.8 us
    pallas_call x6, Pallas kernels, ordered_total(): pl.pallas_call(functools.partial(sum_kernel, len(terms)), out_shape=jax.S...  19.5 us
    unnamed x131, local copies, waits for them, and re-layouts  18.8 us
    ppermute x2, waiting for transfers between devices, body(): gate_up_received = lax.ppermute(gate_up_half, 'dp', flips(order_a[i]))  17.9 us
  transfers between devices with their start and end apart: 41, of which 14 were waited for; matrix products, arithmetic and copies ran while one was open for 8% of the time, Pallas kernels for 33%

profile of v2, /device:TPU:0, one launch (start us, length us, event | category | flops | bytes accessed | tf_op | source)
XLA Modules:
  0.0 361.5 jit_solution(13189361550747639490)
XLA Ops:
  3.7 3.0 collective-permute-start
  14.7 3.8 %collective-permute-done.1.received_ref.refs_1_ = bf16[2,80,640]{2,1,0:T(8,128)(2,1)S(1)} collective-permute-done((bf16[2,80,640]{2,1,0:T(8,128)(2,1)}, bf16[2,80,640]{2,1,0:T(8,128)(2,1)S(1)}, u32[]{:S(2)}, u32[]{:S(2)}) %collective-permute-start.1) | collective-permute-done | bytes 204832 | tf_op jit(solution)/shard_map/ppermute | solution.py:454
  26.4 2.7 multiply_sine_fusion
  29.2 6.3 %collective-permute-done.4.received_ref.refs_0_ = bf16[2,128,640]{2,1,0:T(8,128)(2,1)S(1)} collective-permute-done((bf16[2,128,640]{2,1,0:T(8,128)(2,1)}, bf16[2,128,640]{2,1,0:T(8,128)(2,1)S(1)}, u32[]{:S(2)}, u32[]{:S(2)}) %collective-permute-start.4) | collective-permute-done | bytes 327712 | tf_op jit(solution)/shard_map/ppermute | solution.py:454
  36.2 2.0 shard_map.473.own_ref
  38.2 2.6 shard_map.475
  44.3 2.1 shard_map.470
  48.4 2.0 fusion.32
  50.4 4.9 %shard_map.471 = (bf16[3,320,640]{2,1,0:T(8,128)(2,1)}, bf16[3,320,512]{2,1,0:T(8,128)(2,1)}, bf16[3,320,256]{2,1,0:T(8,128)(2,1)}) custom-call(bf16[3,320,640]{2,1,0:T(8,128)(2,1)} %x_ref.9, f32[3,320,128]{2,1,0:T(8,128)} %get-tuple-element.177.cos_ref, f32[3,320,128]{2,1,0:T(8,128)} %get-tuple-element.176.sin_ref, bf16[256,640]{1,0:T(8,128)(2,1)} %bitcast.143, ...), custom_call_target="tpu_custom_call" | custom-call | flops 629145600 | bytes 6000000 | tf_op jit(solution)/shard_map/pallas_call | solution.py:685
  55.2 3.5 collective-permute-start.7
  59.6 2.5 shard_map.474
  62.9 5.7 %shard_map.476 = (bf16[3,2,640,256]{3,2,1,0:T(8,128)(2,1)}, bf16[3,2,640,256]{3,2,1,0:T(8,128)(2,1)}) custom-call(bf16[3,320,640]{2,1,0:T(8,128)(2,1)} %get-tuple-element.77.normed_ref, f32[3,320,128]{2,1,0:T(8,128)} %get-tuple-element.177.cos_ref, f32[3,320,128]{2,1,0:T(8,128)} %get-tuple-element.176.sin_ref, bf16[1024,640]{1,0:T(8,128)(2,1)} %bitcast.130, ...), custom_call_target="tpu_custom_call" | custom-call | flops 1258291200 | bytes 8000000 | tf_op jit(solution)/shard_map/pallas_call | solution.py:709
  69.4 2.4 shard_map.478.refs_1_.own_ref
  72.4 2.2 shard_map.477.refs_0_.own_ref
  74.6 5.6 %collective-permute-done.7.near_ref = bf16[3,320,512]{2,1,0:T(8,128)(2,1)S(1)} collective-permute-done((bf16[3,320,512]{2,1,0:T(8,128)(2,1)}, bf16[3,320,512]{2,1,0:T(8,128)(2,1)S(1)}, u32[]{:S(2)}, u32[]{:S(2)}) %collective-permute-start.7) | collective-permute-done | bytes 983072 | tf_op jit(solution)/shard_map/ppermute | solution.py:727
  81.1 2.1 shard_map.479
  84.5 17.9 %collective-permute-done.10.received_ref = bf16[2,512,640]{2,1,0:T(8,128)(2,1)S(1)} collective-permute-done((bf16[2,512,640]{2,1,0:T(8,128)(2,1)}, bf16[2,512,640]{2,1,0:T(8,128)(2,1)S(1)}, u32[]{:S(2)}, u32[]{:S(2)}) %collective-permute-start.10) | collective-permute-done | bytes 1310752 | tf_op jit(solution)/shard_map/ppermute | solution.py:734
  103.5 3.4 shard_map.481
  107.9 2.9 shard_map.482
  111.3 8.0 %shard_map.480.mixed_ref = bf16[3,320,1024]{2,1,0:T(8,128)(2,1)} custom-call(bf16[3,2,640,256]{3,2,1,0:T(8,128)(2,1)} %get-tuple-element.80.refs_0_.q_ref, bf16[3,192,512]{2,1,0:T(8,128)(2,1)} %copy-done.9, bf16[3,320,512]{2,1,0:T(8,128)(2,1)} %copy-done.17, bf16[3,320,512]{2,1,0:T(8,128)(2,1)} %get-tuple-element.81.own_ref, ...), custom_call_target="tpu_custom_call" | custom-call | flops 5284823040 | bytes 16000000 | tf_op jit(solution)/shard_map/pallas_call | solution.py:760
  121.5 38.0 %shard_map.483 = (bf16[3,320,640]{2,1,0:T(8,128)(2,1)}, bf16[3,320,640]{2,1,0:T(8,128)(2,1)}, bf16[3,320,2048]{2,1,0:T(8,128)(2,1)}, bf16[3,320,640]{2,1,0:T(8,1...) custom-call(s32[1]{0:T(128)} %bitcast.side_ref, ...), custom_call_target="tpu_custom_call" | custom-call | flops 17616076800 | bytes 40000000 | tf_op jit(solution)/shard_map/pallas_call | solution.py:781
  159.5 10.3 %shard_map.484 = (bf16[4,80,3072]{2,1,0:T(8,128)(2,1)}, bf16[4,80,3072]{2,1,0:T(8,128)(2,1)}) custom-call(s32[1]{0:T(128)} %bitcast.side_ref, bf16[960,2048]{1,0:T(8,128)(2,1)} %bitcast.175, bf16[960,1024]{1,0:T(8,128)(2,1)} %bitcast.176, bf16[960,640]{1,0:T(8,128)(2,1)} %bitcast.178, bf16[960,640]{1,0:T(8,128)(2,1)} %bitcast.179), custom_call_target="tpu_custom_call" | custom-call | flops 3774873600 | bytes 13000000 | tf_op jit(solution)/shard_map/pallas_call | solution.py:856
  169.8 13.1 %shard_map.485 = (bf16[4,512,640]{2,1,0:T(8,128)(2,1)}, bf16[4,512,640]{2,1,0:T(8,128)(2,1)}) custom-call(s32[1]{0:T(128)} %bitcast.side_ref, bf16[960,2048]{1,0:T(8,128)(2,1)} %bitcast.173, bf16[960,2048]{1,0:T(8,128)(2,1)} %bitcast.174, bf16[960,640]{1,0:T(8,128)(2,1)} %bitcast.177, bf16[4,80,3072]{2,1,0:T(8,128)(2,1)} %get-tuple-element.92.after_ref), custom_call_target="tpu_custom_call" | custom-call | flops 5033164800 | bytes 14000000 | tf_op jit(solution)/shard_map/pallas_call | solution.py:892
  187.5 9.1 %shard_map.486 = (bf16[1,192,512]{2,1,0:T(8,128)(2,1)}, f32[1,320,512]{2,1,0:T(8,128)}, f32[1,320,512]{2,1,0:T(8,128)}, bf16[3,320,1024]{2,1,0:T(8,128)(2,1)}, f32[1,1,256]{2,1,0:T(1,128)}) custom-call(bf16[3,2,640,256]{3,2,1,0:T(8,128)(2,1)} %get-tuple-element.80.refs_0_.q_ref, bf16[3,2,640,256]{3,2,1,0:T(8,128)(2,1)} %get-tuple-element.84.qraw_ref, ...), custom_call_target="tpu_custom_call" | custom-call | flops 5284823040 | bytes 8000000 | tf_op jit(solution)/shard_map/pallas_call | solution.py:931
  197.4 3.2 shard_map.487.refs_2_
  202.5 3.4 shard_map.488.refs_1_
  206.5 9.1 %shard_map.489 = (bf16[1,192,512]{2,1,0:T(8,128)(2,1)}, f32[1,320,512]{2,1,0:T(8,128)}, f32[1,320,512]{2,1,0:T(8,128)}, bf16[3,320,1024]{2,1,0:T(8,128)(2,1)}, f32[1,1,256]{2,1,0:T(1,128)}) custom-call(bf16[3,2,640,256]{3,2,1,0:T(8,128)(2,1)} %get-tuple-element.80.refs_0_.q_ref, ...), custom_call_target="tpu_custom_call", output_to_operand_aliasing={{3}: (12, {})} | custom-call | flops 5284823040 | bytes 8000000 | tf_op jit(solution)/shard_map/pallas_call | solution.py:931
  216.9 1.9 shard_map.490.refs_1_
  220.1 9.1 %shard_map.491 = (bf16[1,192,512]{2,1,0:T(8,128)(2,1)}, f32[1,320,512]{2,1,0:T(8,128)}, f32[1,320,512]{2,1,0:T(8,128)}, bf16[3,320,1024]{2,1,0:T(8,128)(2,1)}, f32[1,1,256]{2,1,0:T(1,128)}) custom-call(bf16[3,2,640,256]{3,2,1,0:T(8,128)(2,1)} %get-tuple-element.80.refs_0_.q_ref, ...), custom_call_target="tpu_custom_call", output_to_operand_aliasing={{3}: (12, {})} | custom-call | flops 5284823040 | bytes 8000000 | tf_op jit(solution)/shard_map/pallas_call | solution.py:931
  230.6 3.0 shard_map.492
  235.8 1.9 shard_map.493.refs_0_
  238.9 5.4 %shard_map.494.refs_0_ = bf16[1024,640]{1,0:T(8,128)(2,1)} custom-call(bf16[960,1024]{1,0:T(8,128)(2,1)} %bitcast.129, bf16[960,640]{1,0:T(8,128)(2,1)} %bitcast.165, bf16[1,320,512]{2,1,0:T(8,128)(2,1)} %shard_map.493.refs_0_, bf16[80,3072]{1,0:T(8,128)(2,1)} %bitcast.152), custom_call_target="tpu_custom_call" | custom-call | flops 1258291200 | bytes 5000000 | tf_op jit(solution)/shard_map/pallas_call | solution.py:1030
  245.0 1.9 shard_map.495.refs_3_
  250.9 3.2 shard_map.496
  255.7 4.7 %shard_map.497 = (f32[3,320,640]{2,1,0:T(8,128)}, bf16[3,320,512]{2,1,0:T(8,128)(2,1)}, f32[1,1,640]{2,1,0:T(1,128)}, f32[1,1,256]{2,1,0:T(1,128)}) custom-call(f32[1,320,512]{2,1,0:T(8,128)} %get-tuple-element.97.refs_2_.own_ref, bf16[1,320,512]{2,1,0:T(8,128)(2,1)} %collective-permute-done.22.recv_ref, bf16[3,320,256]{2,1,0:T(8,128)(2,1)} %get-tuple-element.108.kraw_ref, ...), custom_call_target="tpu_custom_call" | custom-call | flops 629145600 | bytes 8000000 | tf_op jit(solution)/shard_map/pallas_call | solution.py:931
  260.4 4.7 %shard_map.498 = (f32[3,320,640]{2,1,0:T(8,128)}, bf16[3,320,512]{2,1,0:T(8,128)(2,1)}, f32[1,1,640]{2,1,0:T(1,128)}, f32[1,1,256]{2,1,0:T(1,128)}) custom-call(f32[1,320,512]{2,1,0:T(8,128)} %get-tuple-element.101.refs_0_.own_ref, bf16[1,320,512]{2,1,0:T(8,128)(2,1)} %collective-permute-done.21.recv_ref, ...), custom_call_target="tpu_custom_call", output_to_operand_aliasing={{0}: (13, {}), {1}: (14, {})} | custom-call | flops 629145600 | bytes 8000000 | tf_op jit(solution)/shard_map/pallas_call | solution.py:931
  265.1 3.2 shard_map.499
  268.3 9.9 %collective-permute-start.31 = (bf16[80,3072]{1,0:T(8,128)(2,1)}, bf16[80,3072]{1,0:T(8,128)(2,1)S(1)}, u32[]{:S(2)}, u32[]{:S(2)}) collective-permute-start(bf16[80,3072]{1,0:T(8,128)(2,1)} %bitcast.134), channel_id=1, source_target_pairs={{0,1},{3,2},{4,5},{7,6},{8,9},{11,10},{12,13},{15,14},{16,17},{19,... | collective-permute-start | bytes 1474568 | tf_op jit(solution)/shard_map/ppermute | solution.py:569
  278.9 4.8 %shard_map.500 = (f32[3,320,640]{2,1,0:T(8,128)}, bf16[3,320,512]{2,1,0:T(8,128)(2,1)}, f32[1,1,640]{2,1,0:T(1,128)}, f32[1,1,256]{2,1,0:T(1,128)}) custom-call(f32[1,320,512]{2,1,0:T(8,128)} %get-tuple-element.102.refs_3_.own_ref, bf16[1,320,512]{2,1,0:T(8,128)(2,1)} %copy-done.32, ...), custom_call_target="tpu_custom_call", output_to_operand_aliasing={{0}: (13, {}), {1}: (14, {})} | custom-call | flops 629145600 | bytes 8000000 | tf_op jit(solution)/shard_map/pallas_call | solution.py:931
  283.8 3.1 fusion
  290.7 3.5 shard_map.501
  295.4 8.6 %collective-permute-start.38 = (bf16[256,640]{1,0:T(8,128)(2,1)S(1)}, bf16[256,640]{1,0:T(8,128)(2,1)S(1)}, u32[]{:S(2)}, u32[]{:S(2)}) collective-permute-start(bf16[256,640]{1,0:T(8,128)(2,1)S(1)} %get-tuple-element.155), channel_id=1, source_target_pairs={{0,1},{3,2},{4,5},{7,6},{8,9},{11,10},{12,13},{15,14},{16,17},{19,... | collective-permute-start | bytes 983048 | tf_op jit(solution)/shard_map/ppermute | solution.py:569
  304.4 4.6 %collective-permute-done.38 = bf16[256,640]{1,0:T(8,128)(2,1)S(1)} collective-permute-done((bf16[256,640]{1,0:T(8,128)(2,1)S(1)}, bf16[256,640]{1,0:T(8,128)(2,1)S(1)}, u32[]{:S(2)}, u32[]{:S(2)}) %collective-permute-start.38) | collective-permute-done | bytes 327712 | tf_op jit(solution)/shard_map/ppermute | solution.py:569
  311.5 6.0 %collective-permute-start.35 = (bf16[256,640]{1,0:T(8,128)(2,1)S(1)}, bf16[256,640]{1,0:T(8,128)(2,1)S(1)}, u32[]{:S(2)}, u32[]{:S(2)}) collective-permute-start(bf16[256,640]{1,0:T(8,128)(2,1)S(1)} %get-tuple-element.156), channel_id=1, source_target_pairs={{0,1},{3,2},{4,5},{7,6},{8,9},{11,10},{12,13},{15,14},{16,17},{19,... | collective-permute-start | bytes 983048 | tf_op jit(solution)/shard_map/ppermute | solution.py:569
  319.8 7.5 %collective-permute-done.33 = bf16[80,3072]{1,0:T(8,128)(2,1)S(1)} collective-permute-done((bf16[80,3072]{1,0:T(8,128)(2,1)S(1)}, bf16[80,3072]{1,0:T(8,128)(2,1)S(1)}, u32[]{:S(2)}, u32[]{:S(2)}) %collective-permute-start.33) | collective-permute-done | bytes 491552 | tf_op jit(solution)/shard_map/ppermute | solution.py:575
  335.1 2.6 collective-permute-start.28
  345.1 3.5 collective-permute-done.37
  350.4 8.1 %collective-permute-done.30 = bf16[208,640]{1,0:T(8,128)(2,1)S(1)} collective-permute-done((bf16[208,640]{1,0:T(8,128)(2,1)S(1)}, bf16[208,640]{1,0:T(8,128)(2,1)S(1)}, u32[]{:S(2)}, u32[]{:S(2)}) %collective-permute-start.30) | collective-permute-done | bytes 266272 | tf_op jit(solution)/shard_map/ppermute | solution.py:575
  (272 shorter events, 86.9 us)
Async XLA Ops:
  0.7 20.3 %copy-start.48 = (s32[3,1280]{1,0:T(4,128)S(1)}, s32[3,1280]{1,0:T(4,128)}, u32[]{:S(2)}) copy-start(s32[3,1280]{1,0:T(4,128)} %param.30) | copy-start | bytes 46084
  0.7 22.0 %copy-start.51 = (s32[3,320]{1,0:T(4,128)S(1)}, s32[3,320]{1,0:T(4,128)}, u32[]{:S(2)}) copy-start(s32[3,320]{1,0:T(4,128)} %param.31) | copy-start | bytes 11524
  3.7 6.1 %collective-permute-start = (bf16[80,640]{1,0:T(8,128)(2,1)}, bf16[80,640]{1,0:T(8,128)(2,1)S(1)}, u32[]{:S(2)}, u32[]{:S(2)}) collective-permute-start(bf16[80,640]{1,0:T(8,128)(2,1)} %get-tuple-element.76.own_ref), channel_id=1, source_target_pairs={{0,16},{4,20},{8,24},{12,28},{16,0},{20,4},{24,8},{28,12},{1,17},{... | collective-permute-start | bytes 307208 | tf_op jit(solution)/shard_map/ppermute | solution.py:454
  6.7 16.1 %collective-permute-start.3 = (bf16[128,640]{1,0:T(8,128)(2,1)}, bf16[128,640]{1,0:T(8,128)(2,1)S(1)}, u32[]{:S(2)}, u32[]{:S(2)}) collective-permute-start(bf16[128,640]{1,0:T(8,128)(2,1)} %get-tuple-element.78.own_ref), channel_id=1, source_target_pairs={{0,8},{4,12},{8,0},{12,4},{16,24},{20,28},{24,16},{28,20},{1,9},{5... | collective-permute-start | bytes 491528 | tf_op jit(solution)/shard_map/ppermute | solution.py:454
  12.0 6.5 %collective-permute-start.1 = (bf16[2,80,640]{2,1,0:T(8,128)(2,1)}, bf16[2,80,640]{2,1,0:T(8,128)(2,1)S(1)}, u32[]{:S(2)}, u32[]{:S(2)}) collective-permute-start(bf16[2,80,640]{2,1,0:T(8,128)(2,1)} %shard_map.468.own_ref), channel_id=1, source_target_pairs={{0,8},{4,12},{8,0},{12,4},{16,24},{20,28},{24,16},{28,20},{1,9},{5... | collective-permute-start | bytes 614408 | tf_op jit(solution)/shard_map/ppermute | solution.py:454
  21.0 22.6 %collective-permute-start.2 = (bf16[2,2,80,640]{3,2,1,0:T(8,128)(2,1)}, bf16[2,2,80,640]{3,2,1,0:T(8,128)(2,1)S(1)}, u32[]{:S(2)}, u32[]{:S(2)}) collective-permute-start(bf16[2,2,80,640]{3,2,1,0:T(8,128)(2,1)} %shard_map.469.own_ref), channel_id=1, source_target_pairs={{0,4},{4,0},{8,12},{12,8},{16,20},{20,16},{24,28},{28,24},{1,5},{5... | collective-permute-start | bytes 1228808 | tf_op jit(solution)/shard_map/ppermute | solution.py:454
  25.1 10.3 %collective-permute-start.4 = (bf16[2,128,640]{2,1,0:T(8,128)(2,1)}, bf16[2,128,640]{2,1,0:T(8,128)(2,1)S(1)}, u32[]{:S(2)}, u32[]{:S(2)}) collective-permute-start(bf16[2,128,640]{2,1,0:T(8,128)(2,1)} %shard_map.472.own_ref), channel_id=1, source_target_pairs={{0,16},{4,20},{8,24},{12,28},{16,0},{20,4},{24,8},{28,12},{1,17},{... | collective-permute-start | bytes 983048 | tf_op jit(solution)/shard_map/ppermute | solution.py:454
  38.2 20.6 %collective-permute-start.5 = (bf16[2,2,128,640]{3,2,1,0:T(8,128)(2,1)}, bf16[2,2,128,640]{3,2,1,0:T(8,128)(2,1)S(1)}, u32[]{:S(2)}, u32[]{:S(2)}) collective-permute-start(bf16[2,2,128,640]{3,2,1,0:T(8,128)(2,1)} %shard_map.473.own_ref), channel_id=1, source_target_pairs={{0,4},{4,0},{8,12},{12,8},{16,20},{20,16},{24,28},{28,24},{1,5},{5... | collective-permute-start | bytes 1966088 | tf_op jit(solution)/shard_map/ppermute | solution.py:454
  40.8 21.3 %collective-permute-start.6 = (bf16[80,3072]{1,0:T(8,128)(2,1)}, bf16[80,3072]{1,0:T(8,128)(2,1)S(1)}, u32[]{:S(2)}, u32[]{:S(2)}) collective-permute-start(bf16[80,3072]{1,0:T(8,128)(2,1)} %get-tuple-element.79.own_ref), channel_id=1, source_target_pairs={{0,16},{4,20},{8,24},{12,28},{16,0},{20,4},{24,8},{28,12},{1,17},{... | collective-permute-start | bytes 1474568 | tf_op jit(solution)/shard_map/ppermute | solution.py:708
  42.1 26.5 %collective-permute-start.8 = (bf16[512,640]{1,0:T(8,128)(2,1)}, bf16[512,640]{1,0:T(8,128)(2,1)S(1)}, u32[]{:S(2)}, u32[]{:S(2)}) collective-permute-start(bf16[512,640]{1,0:T(8,128)(2,1)} %get-tuple-element.82.own_ref), channel_id=1, source_target_pairs={{0,8},{4,12},{8,0},{12,4},{16,24},{20,28},{24,16},{28,20},{1,9},{5... | collective-permute-start | bytes 1966088 | tf_op jit(solution)/shard_map/ppermute | solution.py:734
  55.2 24.9 %collective-permute-start.7 = (bf16[3,320,512]{2,1,0:T(8,128)(2,1)}, bf16[3,320,512]{2,1,0:T(8,128)(2,1)S(1)}, u32[]{:S(2)}, u32[]{:S(2)}) collective-permute-start(bf16[3,320,512]{2,1,0:T(8,128)(2,1)} %get-tuple-element.81.own_ref), channel_id=1, source_target_pairs={{0,1},{1,2},{2,3},{4,5},{5,6},{6,7},{8,9},{9,10},{10,11},{12,13},{... | collective-permute-start | bytes 2949128 | tf_op jit(solution)/shard_map/ppermute | solution.py:727
  71.9 30.6 %collective-permute-start.10 = (bf16[2,512,640]{2,1,0:T(8,128)(2,1)}, bf16[2,512,640]{2,1,0:T(8,128)(2,1)S(1)}, u32[]{:S(2)}, u32[]{:S(2)}) collective-permute-start(bf16[2,512,640]{2,1,0:T(8,128)(2,1)} %shard_map.478.refs_1_.own_ref), channel_id=1, source_target_pairs={{0,16},{4,20},{8,24},{12,28},{16,0},{20,4},{24,8},{28,12},{1,17},{... | collective-permute-start | bytes 3932168 | tf_op jit(solution)/shard_map/ppermute | solution.py:734
  83.2 1.3 collective-permute-start.9
  83.9 23.0 %collective-permute-start.12 = (bf16[2,80,3072]{2,1,0:T(8,128)(2,1)S(1)}, bf16[2,80,3072]{2,1,0:T(8,128)(2,1)S(1)}, u32[]{:S(2)}, u32[]{:S(2)}) collective-permute-start(bf16[2,80,3072]{2,1,0:T(8,128)(2,1)S(1)} %copy-done.4), channel_id=1, source_target_pairs={{0,8},{4,12},{8,0},{12,4},{16,24},{20,28},{24,16},{28,20},{1,9},{5... | collective-permute-start | bytes 2949128 | tf_op jit(solution)/shard_map/ppermute | solution.py:733
  84.5 17.9 %copy-start.9 = (bf16[3,192,512]{2,1,0:T(8,128)(2,1)}, bf16[3,192,512]{2,1,0:T(8,128)(2,1)S(1)}, u32[]{:S(2)}) copy-start(bf16[3,192,512]{2,1,0:T(8,128)(2,1)S(1)} %collective-permute-done.9.far_ref.refs_0_) | copy-start | bytes 1769476
  106.9 12.4 %collective-permute-start.11 = (bf16[4,512,640]{2,1,0:T(8,128)(2,1)}, bf16[4,512,640]{2,1,0:T(8,128)(2,1)S(1)}, u32[]{:S(2)}, u32[]{:S(2)}) collective-permute-start(bf16[4,512,640]{2,1,0:T(8,128)(2,1)} %bitcast.155), channel_id=1, source_target_pairs={{0,4},{4,0},{8,12},{12,8},{16,20},{20,16},{24,28},{28,24},{1,5},{5... | collective-permute-start | bytes 7864328 | tf_op jit(solution)/shard_map/ppermute | solution.py:750
  110.8 8.5 %collective-permute-start.13 = (bf16[4,80,3072]{2,1,0:T(8,128)(2,1)}, bf16[4,80,3072]{2,1,0:T(8,128)(2,1)S(1)}, u32[]{:S(2)}, u32[]{:S(2)}) collective-permute-start(bf16[4,80,3072]{2,1,0:T(8,128)(2,1)} %bitcast.157), channel_id=1, source_target_pairs={{0,4},{4,0},{8,12},{12,8},{16,20},{20,16},{24,28},{28,24},{1,5},{5... | collective-permute-start | bytes 5898248 | tf_op jit(solution)/shard_map/ppermute | solution.py:749
  182.9 18.1 %collective-permute-start.14 = (bf16[4,512,640]{2,1,0:T(8,128)(2,1)}, bf16[4,512,640]{2,1,0:T(8,128)(2,1)S(1)}, u32[]{:S(2)}, u32[]{:S(2)}) collective-permute-start(bf16[4,512,640]{2,1,0:T(8,128)(2,1)} %get-tuple-element.93.refs_0_), channel_id=1, source_target_pairs={{0,4},{4,0},{8,12},{12,8},{16,20},{20,16},{24,28},{28,24},{1,5},{5... | collective-permute-start | bytes 7864328 | tf_op jit(solution)/shard_map/ppermute | solution.py:476
  182.9 14.4 %collective-permute-start.15 = (bf16[4,80,3072]{2,1,0:T(8,128)(2,1)}, bf16[4,80,3072]{2,1,0:T(8,128)(2,1)}, u32[]{:S(2)}, u32[]{:S(2)}) collective-permute-start(bf16[4,80,3072]{2,1,0:T(8,128)(2,1)} %get-tuple-element.92.after_ref), channel_id=1, source_target_pairs={{0,4},{4,0},{8,12},{12,8},{16,20},{20,16},{24,28},{28,24},{1,5},{5... | collective-permute-start | bytes 5898248 | tf_op jit(solution)/shard_map/ppermute | solution.py:476
  196.6 19.6 %collective-permute-start.16 = (bf16[1,192,512]{2,1,0:T(8,128)(2,1)}, bf16[1,192,512]{2,1,0:T(8,128)(2,1)S(1)}, u32[]{:S(2)}, u32[]{:S(2)}) collective-permute-start(bf16[1,192,512]{2,1,0:T(8,128)(2,1)} %get-tuple-element.100), channel_id=1, source_target_pairs={{2,1},{3,2},{6,5},{7,6},{10,9},{11,10},{14,13},{15,14},{18,17},{19... | collective-permute-start | bytes 589832 | tf_op jit(solution)/shard_map/ppermute | solution.py:1014
  200.5 30.1 %collective-permute-start.19 = (bf16[2,80,3072]{2,1,0:T(8,128)(2,1)}, bf16[2,80,3072]{2,1,0:T(8,128)(2,1)}, u32[]{:S(2)}, u32[]{:S(2)}) collective-permute-start(bf16[2,80,3072]{2,1,0:T(8,128)(2,1)} %shard_map.487.refs_2_), channel_id=1, source_target_pairs={{0,16},{4,20},{8,24},{12,28},{16,0},{20,4},{24,8},{28,12},{1,17},{... | collective-permute-start | bytes 2949128 | tf_op jit(solution)/shard_map/ppermute | solution.py:535
  205.9 43.8 %collective-permute-start.23 = (bf16[2,512,640]{2,1,0:T(8,128)(2,1)}, bf16[2,512,640]{2,1,0:T(8,128)(2,1)S(1)}, u32[]{:S(2)}, u32[]{:S(2)}) collective-permute-start(bf16[2,512,640]{2,1,0:T(8,128)(2,1)} %shard_map.488.refs_1_), channel_id=1, source_target_pairs={{0,8},{4,12},{8,0},{12,4},{16,24},{20,28},{24,16},{28,20},{1,9},{5... | collective-permute-start | bytes 3932168 | tf_op jit(solution)/shard_map/ppermute | solution.py:535
  215.6 19.5 %collective-permute-start.18 = (bf16[1,192,512]{2,1,0:T(8,128)(2,1)}, bf16[1,192,512]{2,1,0:T(8,128)(2,1)S(1)}, u32[]{:S(2)}, u32[]{:S(2)}) collective-permute-start(bf16[1,192,512]{2,1,0:T(8,128)(2,1)} %get-tuple-element.107), channel_id=1, source_target_pairs={{2,1},{3,2},{6,5},{7,6},{10,9},{11,10},{14,13},{15,14},{18,17},{19... | collective-permute-start | bytes 589832 | tf_op jit(solution)/shard_map/ppermute | solution.py:1014
  218.8 36.9 %collective-permute-start.22 = (bf16[1,320,512]{2,1,0:T(8,128)(2,1)}, bf16[1,320,512]{2,1,0:T(8,128)(2,1)}, u32[]{:S(2)}, u32[]{:S(2)}) collective-permute-start(bf16[1,320,512]{2,1,0:T(8,128)(2,1)} %shard_map.490.refs_1_), channel_id=1, source_target_pairs={{1,0},{2,1},{3,2},{5,4},{6,5},{7,6},{9,8},{10,9},{11,10},{13,12},{... | collective-permute-start | bytes 983048 | tf_op jit(solution)/shard_map/ppermute | solution.py:1047
  229.2 15.1 %collective-permute-start.17 = (bf16[1,192,512]{2,1,0:T(8,128)(2,1)}, bf16[1,192,512]{2,1,0:T(8,128)(2,1)S(1)}, u32[]{:S(2)}, u32[]{:S(2)}) collective-permute-start(bf16[1,192,512]{2,1,0:T(8,128)(2,1)} %get-tuple-element.104), channel_id=1, source_target_pairs={{2,1},{3,2},{6,5},{7,6},{10,9},{11,10},{14,13},{15,14},{18,17},{19... | collective-permute-start | bytes 589832 | tf_op jit(solution)/shard_map/ppermute | solution.py:1014
  233.6 31.5 %collective-permute-start.24 = (bf16[80,3072]{1,0:T(8,128)(2,1)}, bf16[80,3072]{1,0:T(8,128)(2,1)}, u32[]{:S(2)}, u32[]{:S(2)}) collective-permute-start(bf16[80,3072]{1,0:T(8,128)(2,1)} %bitcast.150), channel_id=1, source_target_pairs={{0,8},{4,12},{8,0},{12,4},{16,24},{20,28},{24,16},{28,20},{1,9},{5... | collective-permute-start | bytes 1474568 | tf_op jit(solution)/shard_map/ppermute | solution.py:535
  237.7 22.8 %collective-permute-start.21 = (bf16[1,320,512]{2,1,0:T(8,128)(2,1)}, bf16[1,320,512]{2,1,0:T(8,128)(2,1)}, u32[]{:S(2)}, u32[]{:S(2)}) collective-permute-start(bf16[1,320,512]{2,1,0:T(8,128)(2,1)} %shard_map.493.refs_0_), channel_id=1, source_target_pairs={{1,0},{2,1},{3,2},{5,4},{6,5},{7,6},{9,8},{10,9},{11,10},{13,12},{... | collective-permute-start | bytes 983048 | tf_op jit(solution)/shard_map/ppermute | solution.py:1047
  246.9 31.3 %collective-permute-start.20 = (bf16[1,320,512]{2,1,0:T(8,128)(2,1)}, bf16[1,320,512]{2,1,0:T(8,128)(2,1)S(1)}, u32[]{:S(2)}, u32[]{:S(2)}) collective-permute-start(bf16[1,320,512]{2,1,0:T(8,128)(2,1)} %shard_map.495.refs_3_), channel_id=1, source_target_pairs={{1,0},{2,1},{3,2},{5,4},{6,5},{7,6},{9,8},{10,9},{11,10},{13,12},{... | collective-permute-start | bytes 983048 | tf_op jit(solution)/shard_map/ppermute | solution.py:1047
  254.2 35.7 %collective-permute-start.34 = (bf16[512,640]{1,0:T(8,128)(2,1)}, bf16[512,640]{1,0:T(8,128)(2,1)S(1)}, u32[]{:S(2)}, u32[]{:S(2)}) collective-permute-start(bf16[512,640]{1,0:T(8,128)(2,1)} %bitcast.147), channel_id=1, source_target_pairs={{0,16},{4,20},{8,24},{12,28},{16,0},{20,4},{24,8},{28,12},{1,17},{... | collective-permute-start | bytes 1966088 | tf_op jit(solution)/shard_map/ppermute | solution.py:535
  268.3 20.2 %collective-permute-start.31 = (bf16[80,3072]{1,0:T(8,128)(2,1)}, bf16[80,3072]{1,0:T(8,128)(2,1)S(1)}, u32[]{:S(2)}, u32[]{:S(2)}) collective-permute-start(bf16[80,3072]{1,0:T(8,128)(2,1)} %bitcast.134), channel_id=1, source_target_pairs={{0,1},{3,2},{4,5},{7,6},{8,9},{11,10},{12,13},{15,14},{16,17},{19,... | collective-permute-start | bytes 1474568 | tf_op jit(solution)/shard_map/ppermute | solution.py:569
  289.2 20.8 %collective-permute-start.32 = (bf16[80,3072]{1,0:T(8,128)(2,1)S(1)}, bf16[80,3072]{1,0:T(8,128)(2,1)S(1)}, u32[]{:S(2)}, u32[]{:S(2)}) collective-permute-start(bf16[80,3072]{1,0:T(8,128)(2,1)S(1)} %fusion.2), channel_id=1, source_target_pairs={{1,2},{2,1},{5,6},{6,5},{9,10},{10,9},{13,14},{14,13},{17,18},{18,... | collective-permute-start | bytes 1474568 | tf_op jit(solution)/shard_map/ppermute | solution.py:571
  294.2 14.8 %copy-start.1 = (bf16[1,512,640]{2,1,0:T(8,128)(2,1)S(1)}, bf16[1,512,640]{2,1,0:T(8,128)(2,1)}, u32[]{:S(2)}) copy-start(bf16[1,512,640]{2,1,0:T(8,128)(2,1)} %shard_map.501) | copy-start | bytes 1966084
  295.4 13.6 %collective-permute-start.38 = (bf16[256,640]{1,0:T(8,128)(2,1)S(1)}, bf16[256,640]{1,0:T(8,128)(2,1)S(1)}, u32[]{:S(2)}, u32[]{:S(2)}) collective-permute-start(bf16[256,640]{1,0:T(8,128)(2,1)S(1)} %get-tuple-element.155), channel_id=1, source_target_pairs={{0,1},{3,2},{4,5},{7,6},{8,9},{11,10},{12,13},{15,14},{16,17},{19,... | collective-permute-start | bytes 983048 | tf_op jit(solution)/shard_map/ppermute | solution.py:569
  304.1 13.3 %collective-permute-start.25 = (bf16[2,2,208,640]{3,2,1,0:T(8,128)(2,1)S(1)}, bf16[2,2,208,640]{3,2,1,0:T(8,128)(2,1)S(1)}, u32[]{:S(2)}, u32[]{:S(2)}) collective-permute-start(bf16[2,2,208,640]{3,2,1,0:T(8,128)(2,1)S(1)} %pad_maximum_fusion), channel_id=1, source_target_pairs={{0,4},{4,0},{8,12},{12,8},{16,20},{20,16},{24,28},{28,24},{1,5},{5... | collective-permute-start | bytes 3194888 | tf_op jit(solution)/shard_map/ppermute | solution.py:535
  309.1 9.1 %collective-permute-start.39 = (bf16[256,640]{1,0:T(8,128)(2,1)S(1)}, bf16[256,640]{1,0:T(8,128)(2,1)S(1)}, u32[]{:S(2)}, u32[]{:S(2)}) collective-permute-start(bf16[256,640]{1,0:T(8,128)(2,1)S(1)} %fusion.8), channel_id=1, source_target_pairs={{1,2},{2,1},{5,6},{6,5},{9,10},{10,9},{13,14},{14,13},{17,18},{18,... | collective-permute-start | bytes 983048 | tf_op jit(solution)/shard_map/ppermute | solution.py:571
  310.1 17.1 %collective-permute-start.33 = (bf16[80,3072]{1,0:T(8,128)(2,1)S(1)}, bf16[80,3072]{1,0:T(8,128)(2,1)S(1)}, u32[]{:S(2)}, u32[]{:S(2)}) collective-permute-start(bf16[80,3072]{1,0:T(8,128)(2,1)S(1)} %fusion.6), channel_id=1, source_target_pairs={{1,0},{2,3},{5,4},{6,7},{9,8},{10,11},{13,12},{14,15},{17,16},{18,... | collective-permute-start | bytes 1474568 | tf_op jit(solution)/shard_map/ppermute | solution.py:575
  311.5 17.6 %collective-permute-start.35 = (bf16[256,640]{1,0:T(8,128)(2,1)S(1)}, bf16[256,640]{1,0:T(8,128)(2,1)S(1)}, u32[]{:S(2)}, u32[]{:S(2)}) collective-permute-start(bf16[256,640]{1,0:T(8,128)(2,1)S(1)} %get-tuple-element.156), channel_id=1, source_target_pairs={{0,1},{3,2},{4,5},{7,6},{8,9},{11,10},{12,13},{15,14},{16,17},{19,... | collective-permute-start | bytes 983048 | tf_op jit(solution)/shard_map/ppermute | solution.py:569
  317.6 10.7 %collective-permute-start.26 = (bf16[2,208,640]{2,1,0:T(8,128)(2,1)S(1)}, bf16[2,208,640]{2,1,0:T(8,128)(2,1)S(1)}, u32[]{:S(2)}, u32[]{:S(2)}) collective-permute-start(bf16[2,208,640]{2,1,0:T(8,128)(2,1)S(1)} %fusion.1), channel_id=1, source_target_pairs={{0,16},{4,20},{8,24},{12,28},{16,0},{20,4},{24,8},{28,12},{1,17},{... | collective-permute-start | bytes 1597448 | tf_op jit(solution)/shard_map/ppermute | solution.py:535
  318.3 12.5 %copy-start.6 = (f32[256,640]{1,0:T(8,128)S(1)}, f32[256,640]{1,0:T(8,128)}, u32[]{:S(2)}) copy-start(f32[256,640]{1,0:T(8,128)} %wu_ref.1) | copy-start | bytes 1966084
  318.3 12.5 %copy-start.20 = (f32[256,640]{1,0:T(8,128)S(1)}, f32[256,640]{1,0:T(8,128)}, u32[]{:S(2)}) copy-start(f32[256,640]{1,0:T(8,128)} %param.53) | copy-start | bytes 1966084
  318.3 12.4 %copy-start.21 = (f32[256,640]{1,0:T(8,128)S(1)}, f32[256,640]{1,0:T(8,128)}, u32[]{:S(2)}) copy-start(f32[256,640]{1,0:T(8,128)} %param.45) | copy-start | bytes 1966084
  318.3 12.4 %collective-permute-start.40 = (bf16[256,640]{1,0:T(8,128)(2,1)S(1)}, bf16[256,640]{1,0:T(8,128)(2,1)S(1)}, u32[]{:S(2)}, u32[]{:S(2)}) collective-permute-start(bf16[256,640]{1,0:T(8,128)(2,1)S(1)} %fusion.17), channel_id=1, source_target_pairs={{1,0},{2,3},{5,4},{6,7},{9,8},{10,11},{13,12},{14,15},{17,16},{18,... | collective-permute-start | bytes 983048 | tf_op jit(solution)/shard_map/ppermute | solution.py:575
  328.5 6.5 %collective-permute-start.27 = (bf16[208,640]{1,0:T(8,128)(2,1)S(1)}, bf16[208,640]{1,0:T(8,128)(2,1)S(1)}, u32[]{:S(2)}, u32[]{:S(2)}) collective-permute-start(bf16[208,640]{1,0:T(8,128)(2,1)S(1)} %fusion.9), channel_id=1, source_target_pairs={{0,8},{4,12},{8,0},{12,4},{16,24},{20,28},{24,16},{28,20},{1,9},{5... | collective-permute-start | bytes 798728 | tf_op jit(solution)/shard_map/ppermute | solution.py:535
  332.6 6.8 %collective-permute-start.36 = (bf16[256,640]{1,0:T(8,128)(2,1)S(1)}, bf16[256,640]{1,0:T(8,128)(2,1)S(1)}, u32[]{:S(2)}, u32[]{:S(2)}) collective-permute-start(bf16[256,640]{1,0:T(8,128)(2,1)S(1)} %get-tuple-element.154), channel_id=1, source_target_pairs={{1,2},{2,1},{5,6},{6,5},{9,10},{10,9},{13,14},{14,13},{17,18},{18,... | collective-permute-start | bytes 983048 | tf_op jit(solution)/shard_map/ppermute | solution.py:571
  335.1 6.5 %collective-permute-start.28 = (bf16[208,640]{1,0:T(8,128)(2,1)S(1)}, bf16[208,640]{1,0:T(8,128)(2,1)S(1)}, u32[]{:S(2)}, u32[]{:S(2)}) collective-permute-start(bf16[208,640]{1,0:T(8,128)(2,1)S(1)} %fusion.11), channel_id=1, source_target_pairs={{0,1},{3,2},{4,5},{7,6},{8,9},{11,10},{12,13},{15,14},{16,17},{19,... | collective-permute-start | bytes 798728 | tf_op jit(solution)/shard_map/ppermute | solution.py:569
  339.5 9.1 %collective-permute-start.37 = (bf16[256,640]{1,0:T(8,128)(2,1)S(1)}, bf16[256,640]{1,0:T(8,128)(2,1)S(1)}, u32[]{:S(2)}, u32[]{:S(2)}) collective-permute-start(bf16[256,640]{1,0:T(8,128)(2,1)S(1)} %fusion.16), channel_id=1, source_target_pairs={{1,0},{2,3},{5,4},{6,7},{9,8},{10,11},{13,12},{14,15},{17,16},{18,... | collective-permute-start | bytes 983048 | tf_op jit(solution)/shard_map/ppermute | solution.py:575
  341.7 1.9 collective-permute-start.29
  343.8 14.6 %collective-permute-start.30 = (bf16[208,640]{1,0:T(8,128)(2,1)S(1)}, bf16[208,640]{1,0:T(8,128)(2,1)S(1)}, u32[]{:S(2)}, u32[]{:S(2)}) collective-permute-start(bf16[208,640]{1,0:T(8,128)(2,1)S(1)} %fusion.13), channel_id=1, source_target_pairs={{1,0},{2,3},{5,4},{6,7},{9,8},{10,11},{13,12},{14,15},{17,16},{18,... | collective-permute-start | bytes 798728 | tf_op jit(solution)/shard_map/ppermute | solution.py:575
  (57 other events, 189.3 us)

commit v3 on v2

--- a/solution.py
+++ b/solution.py
@@ -98,33 +98,36 @@
     return jnp.concatenate([values] * heads, axis=0)
 
 
-def cast_first_kernel(wq_ref, wk_ref, wv_ref, gain_ref, q_ref, rest_ref):
-    q_ref[...] = wq_ref[...].astype(jnp.bfloat16)
+def cast_first_kernel(wq_ref, wk_ref, wv_ref, gain_ref, out_ref):
     width = wq_ref.shape[1]
     gains = gain_ref[...]
     tail = width - gains.shape[1]
     block = jnp.broadcast_to(gains, (16, gains.shape[1]))
     if tail:
         block = jnp.concatenate([block, jnp.zeros((16, tail), jnp.float32)], axis=1)
-    rest_ref[...] = jnp.concatenate([wk_ref[...], wv_ref[...], block], axis=0).astype(jnp.bfloat16)
+    parts = [wq_ref[...], wk_ref[...], wv_ref[...], block]
+    out_ref[...] = jnp.concatenate(parts, axis=0).astype(jnp.bfloat16)
 
 
 def cast_rest_kernel(waits, wg_ref, wu_ref, wd_ref, wo_ref, *refs):
-    out_ref, pair_ref = refs[waits:]
-    rows = wg_ref.shape[0]
-    units = wd_ref.shape[1]
-    out_ref[:rows, :] = wg_ref[...].astype(jnp.bfloat16)
-    out_ref[rows:, :] = wu_ref[...].astype(jnp.bfloat16)
-    pair_ref[:, :units] = wd_ref[...].astype(jnp.bfloat16)
-    pair_ref[:, units:] = wo_ref[...].astype(jnp.bfloat16)
-
-
-def stack_kernel(axis, waits, side_ref, own_ref, received_ref, *refs):
-    out_ref = refs[waits]
-    upper = side_ref[0]
-    lead = (slice(None),) * axis
-    out_ref[lead + (upper,)] = own_ref[...]
-    out_ref[lead + (1 - upper,)] = received_ref[...]
+    gate_ref, up_ref, first_ref, second_ref = refs[waits:]
+    cut = first_ref.shape[1]
+    rest = wd_ref.shape[1] - cut
+    gate_ref[...] = wg_ref[...].astype(jnp.bfloat16)
+    up_ref[...] = wu_ref[...].astype(jnp.bfloat16)
+    first_ref[...] = wd_ref[:, :cut].astype(jnp.bfloat16)
+    second_ref[:, :rest] = wd_ref[:, cut:].astype(jnp.bfloat16)
+    second_ref[:, rest:] = wo_ref[...].astype(jnp.bfloat16)
+
+
+def stack_kernel(bits, axes, waits, index_ref, *refs):
+    count = len(bits)
+    outs = refs[2 * count + waits :]
+    for i in range(count):
+        upper = (index_ref[0] >> bits[i]) & 1
+        lead = (slice(None),) * axes[i]
+        outs[i][lead + (upper,)] = refs[2 * i][...]
+        outs[i][lead + (1 - upper,)] = refs[2 * i + 1][...]
 
 
 def tail_rows_kernel(waits, near_ref, *refs):
@@ -269,7 +272,8 @@
 
 
 def middle_kernel(
-    heads, chunk, side_ref, mixed_ref, x_ref, cot_ref, gu_own_ref, gu_got_ref, do_own_ref, do_got_ref, ga_ref, gp_ref, gf_ref,
+    heads, chunk, side_ref, mixed_ref, x_ref, cot_ref, gate_own_ref, gate_got_ref, up_own_ref, up_got_ref,
+    first_own_ref, first_got_ref, second_own_ref, second_got_ref, ga_ref, gp_ref, gf_ref,
     out_ref, pre_ref, product_ref, ddown_ref, dgate_ref, dup_ref, datt_ref, dhid_ref, dmix_ref, dg_ref,
     act_ref, slope_ref, wgu_ref, wdo_blocks_ref, sems,
 ):
@@ -277,11 +281,24 @@
     def _():
         upper = side_ref[0]
         copies = []
-        for i, (source, target) in enumerate(
-            [(do_own_ref, wdo_blocks_ref), (do_got_ref, wdo_blocks_ref), (gu_own_ref, wgu_ref), (gu_got_ref, wgu_ref)]
-        ):
-            place = upper if i % 2 == 0 else 1 - upper
-            copies.append(pltpu.make_async_copy(source, target.at[:, place], sems.at[i]))
+        shard = gate_own_ref.shape[1]
+        cut = first_own_ref.shape[2]
+        places = [
+            (slice(None, cut), first_own_ref, first_got_ref),
+            (slice(cut, None), second_own_ref, second_got_ref),
+        ]
+        for lanes, own, got in places:
+            for place, source in ((upper, own), (1 - upper, got)):
+                target = wdo_blocks_ref.at[:, place, :, lanes]
+                copies.append(pltpu.make_async_copy(source, target, sems.at[len(copies)]))
+        places = [
+            (slice(None, shard), gate_own_ref, gate_got_ref),
+            (slice(shard, None), up_own_ref, up_got_ref),
+        ]
+        for lines, own, got in places:
+            for place, source in ((upper, own), (1 - upper, got)):
+                target = wgu_ref.at[:, place, lines, :]
+                copies.append(pltpu.make_async_copy(source, target, sems.at[len(copies)]))
         for copy in copies:
             copy.start()
         for copy in copies:
@@ -428,33 +445,31 @@
     return [(i, i ^ (1 << bit)) for i in range(lax.axis_size("dp"))]
 
 
+def device_index():
+    return lax.axis_index("dp")[None].astype(jnp.int32)
+
+
 def side(bit):
     return (lax.axis_index("dp") >> bit) & 1
 
 
-def stack_step(own, received, bit, done, arrived=()):
-    axis = sum(1 for other in done if other > bit)
+def stack_step(pairs, bits, done, arrived=()):
+    axes = [sum(1 for other in before if other > bit) for bit, before in zip(bits, done)]
     anywhere = pl.BlockSpec(memory_space=pl.ANY)
     block = pl.BlockSpec(memory_space=pltpu.VMEM)
     arrived = list(arrived)
+    shapes = [
+        own.shape[:axis] + (2,) + own.shape[axis:] for (own, _), axis in zip(pairs, axes)
+    ]
     return pl.pallas_call(
-        functools.partial(stack_kernel, axis, len(arrived)),
-        out_shape=jax.ShapeDtypeStruct(own.shape[:axis] + (2,) + own.shape[axis:], own.dtype),
+        functools.partial(stack_kernel, bits, axes, len(arrived)),
+        out_shape=[jax.ShapeDtypeStruct(shape, jnp.bfloat16) for shape in shapes],
         in_specs=[pl.BlockSpec(memory_space=pltpu.SMEM)]
-        + [block] * 2
+        + [block] * (2 * len(pairs))
         + [anywhere] * len(arrived),
-        out_specs=block,
+        out_specs=[block] * len(pairs),
         compiler_params=pltpu.CompilerParams(vmem_limit_bytes=VMEM_BYTES),
-    )(side(bit)[None].astype(jnp.int32), own, received, *arrived)
-
-
-def gather_rows(shard, order):
-    current, steps = shard, []
-    for i, bit in enumerate(order):
-        received = lax.ppermute(current, "dp", flips(bit))
-        steps.append(received)
-        current = stack_step(current, received, bit, order[:i])
-    return current.reshape((lax.axis_size("dp"),) + shard.shape), steps
+    )(device_index(), *[array for pair in pairs for array in pair], *arrived)
 
 
 class RowSum:
@@ -492,39 +507,38 @@
         return value.astype(jnp.bfloat16)
 
     def ordered_total(self, after, other=None):
-        picks = dict(self.chosen)
-        if other is not None:
-            picks[other] = 1 - side(other)
-        left = [b for b in range(len(self.order) - 1, -1, -1) if b not in picks]
-        places = jnp.arange(2 ** len(left), dtype=jnp.int32)
+        gone = set(self.chosen) | ({other} if other is not None else set())
+        left = [b for b in range(len(self.order) - 1, -1, -1) if b not in gone]
         terms = self.terms + self.received
-        index = []
-        for part, bits in terms:
-            flat = jnp.zeros_like(places)
-            for bit in bits:
-                if bit in picks:
-                    value = picks[bit]
-                else:
-                    value = (places >> (len(left) - 1 - left.index(bit))) & 1
-                flat = 2 * flat + value
-            index.append(flat)
         block = terms[0][0].shape[-2:]
         anywhere = pl.BlockSpec(memory_space=pl.ANY)
 
-        def spec(k):
-            return pl.BlockSpec((1,) + block, lambda g, index: (index[k, g], 0, 0))
-
+        def spec(bits):
+            def place(g, index):
+                flat = 0
+                for bit in bits:
+                    if bit in gone:
+                        value = (index[0] >> bit) & 1
+                        value = 1 - value if bit == other else value
+                    else:
+                        value = (g >> (len(left) - 1 - left.index(bit))) & 1
+                    flat = 2 * flat + value
+                return (flat, 0, 0)
+
+            return pl.BlockSpec((1,) + block, place)
+
+        count = 2 ** len(left)
         out = pl.pallas_call(
             functools.partial(sum_kernel, len(terms)),
-            out_shape=jax.ShapeDtypeStruct((len(places),) + block, jnp.bfloat16),
+            out_shape=jax.ShapeDtypeStruct((count,) + block, jnp.bfloat16),
             grid_spec=pltpu.PrefetchScalarGridSpec(
                 num_scalar_prefetch=1,
-                grid=(len(places),),
-                in_specs=[spec(k) for k in range(len(terms))] + [anywhere] * len(after),
+                grid=(count,),
+                in_specs=[spec(bits) for _, bits in terms] + [anywhere] * len(after),
                 out_specs=pl.BlockSpec((1,) + block, lambda g, index: (g, 0, 0)),
             ),
             compiler_params=kernel_params(),
-        )(jnp.stack(index), *[part.reshape((-1,) + block) for part, _ in terms], *after)
+        )(device_index(), *[part.reshape((-1,) + block) for part, _ in terms], *after)
         return out.reshape((2,) * len(left) + block)
 
     def ordered_step(self, bit, after):
@@ -622,28 +636,54 @@
     def array(shape, kind):
         return jax.ShapeDtypeStruct(shape, kind)
 
-    query_shard, rest_shard = pl.pallas_call(
+    query_rows = query_weight.shape[0]
+    first_shard = pl.pallas_call(
         cast_first_kernel,
-        out_shape=[array(query_weight.shape, low), array((rest_rows, width), low)],
+        out_shape=array((query_rows + rest_rows, width), low),
     )(query_weight, key_weight, value_weight, norm_gains[None])
-    query_all, query_steps = gather_rows(query_shard, order_a)
-    rest_all, rest_steps = gather_rows(rest_shard, order_b)
-    w_query = query_all.reshape(-1, width)
-    w_key = rest_all[:, :key_rows].reshape(-1, width)
-    w_value = rest_all[:, key_rows : 2 * key_rows].reshape(-1, width)
-    gains_all = rest_all[:, 2 * key_rows, :gain_rows].reshape(-1)
     block = pl.BlockSpec(memory_space=pltpu.VMEM)
     anywhere = pl.BlockSpec(memory_space=pl.ANY)
-    arrived = [query_steps[-2], rest_steps[-2]]
-    gate_up_shard, pair_shard = pl.pallas_call(
-        functools.partial(cast_rest_kernel, len(arrived)),
+    first_received = lax.ppermute(first_shard, "dp", flips(order_b[0]))
+    pair_width = down_weight.shape[1] + output_weight.shape[1]
+    pair_half_shape = array((down_weight.shape[0], pair_width // 2), low)
+    shards_low = pl.pallas_call(
+        functools.partial(cast_rest_kernel, 1),
         out_shape=[
-            array((2 * gate_weight.shape[0], width), low),
-            array((down_weight.shape[0], down_weight.shape[1] + output_weight.shape[1]), low),
+            array(gate_weight.shape, low),
+            array(up_weight.shape, low),
+            pair_half_shape,
+            pair_half_shape,
         ],
-        in_specs=[block] * 4 + [anywhere] * len(arrived),
-    )(gate_weight, up_weight, down_weight, output_weight, *arrived)
-
+        in_specs=[block] * 4 + [anywhere],
+    )(gate_weight, up_weight, down_weight, output_weight, first_received)
+    rest_orders = [order_a, order_b, order_a, order_b]
+
+    def rest_step(blocks, i):
+        return [
+            lax.ppermute(own, "dp", flips(order[i])) for own, order in zip(blocks, rest_orders)
+        ]
+
+    def rest_stack(blocks, received, i, arrived):
+        return stack_step(
+            list(zip(blocks, received)),
+            [order[i] for order in rest_orders],
+            [order[:i] for order in rest_orders],
+            arrived,
+        )
+
+    (first_all,) = stack_step([(first_shard, first_received)], [order_b[0]], [[]])
+    for i in range(1, bits):
+        first_received = lax.ppermute(first_all, "dp", flips(order_b[i]))
+        (first_all,) = stack_step(
+            [(first_all, first_received)], [order_b[i]], [order_b[:i]], shards_low[:1]
+        )
+    first_all = first_all.reshape((count,) + first_shard.shape)
+    rest_received = rest_step(shards_low, 0)
+    key_start = query_rows + key_rows
+    w_query = first_all[:, :query_rows].reshape(-1, width)
+    w_key = first_all[:, query_rows:key_start].reshape(-1, width)
+    w_value = first_all[:, key_start : key_start + key_rows].reshape(-1, width)
+    gains_all = first_all[:, key_start + key_rows, :gain_rows].reshape(-1)
     seqs, rows, _ = tokens.shape
     size = w_key.shape[0]
     heads = w_query.shape[0] // size
@@ -683,7 +723,7 @@
     head_block = per_seq(2, heads * part, size)
     q_shape = (seqs, 2, heads * part, size)
     normed, pair_own, key_raw = call(
-        functools.partial(project_pair_kernel, 2),
+        functools.partial(project_pair_kernel, 6),
         [
             array((seqs, rows, width), low),
             array((seqs, rows, 2 * size), low),
@@ -698,14 +738,17 @@
             whole(*w_value.shape),
             whole(1, width),
             whole(1, size),
-            anywhere,
-            anywhere,
-        ],
+        ]
+        + [anywhere] * 6,
         [],
         4 * tokens_all * width * size,
         6_000_000,
-    )(tokens, cosine, sine, w_key, w_value, g_input, g_key, query_ids, key_ids)
-    pair_first = lax.ppermute(pair_shard, "dp", flips(order_b[0]))
+    )(
+        tokens, cosine, sine, w_key, w_value, g_input, g_key, query_ids, key_ids, *rest_received
+    )
+    upward = [(i, i + 1) for i in range(shards - 1)]
+    pair_near = lax.ppermute(pair_own, "seq", upward)
+    rest_blocks = rest_stack(shards_low, rest_received, 0, [pair_own])
     query, query_raw = call(
         functools.partial(project_query_kernel, heads, 1),
         [array(q_shape, low), array(q_shape, low)],
@@ -721,33 +764,23 @@
         [],
         2 * tokens_all * width * heads * size,
         8_000_000,
-    )(normed, cosine, sine, w_query, g_query, pair_first)
-
-    upward = [(i, i + 1) for i in range(shards - 1)]
-    pair_near = lax.ppermute(pair_own, "seq", upward)
-    gate_up_half, pair_half = gate_up_shard, pair_shard
-    pair_far = None
-    for i in range(bits - 1):
-        pair_received = pair_first
-        if i:
-            pair_received = lax.ppermute(pair_half, "dp", flips(order_b[i]))
-        gate_up_received = lax.ppermute(gate_up_half, "dp", flips(order_a[i]))
-        waits = [query] if i == 0 else [pair_far]
-        pair_half = stack_step(pair_half, pair_received, order_b[i], order_b[:i], waits)
-        gate_up_half = stack_step(gate_up_half, gate_up_received, order_a[i], order_a[:i], waits)
-        if i == 0:
-            far_send = pl.pallas_call(
-                functools.partial(tail_rows_kernel, 2),
-                out_shape=array((seqs, far, 2 * size), low),
-                in_specs=[block, anywhere, anywhere],
-                out_specs=block,
-                compiler_params=pltpu.CompilerParams(vmem_limit_bytes=VMEM_BYTES),
-            )(pair_near, pair_half, gate_up_half)
-            pair_far = lax.ppermute(far_send, "seq", upward[1:])
-    pair_half = pair_half.reshape((count // 2,) + pair_shard.shape)
-    gate_up_half = gate_up_half.reshape((count // 2,) + gate_up_shard.shape)
-    pair_received = lax.ppermute(pair_half, "dp", flips(0))
-    gate_up_received = lax.ppermute(gate_up_half, "dp", flips(0))
+    )(normed, cosine, sine, w_query, g_query, rest_blocks[0])
+
+    far_send = pl.pallas_call(
+        functools.partial(tail_rows_kernel, 1),
+        out_shape=array((seqs, far, 2 * size), low),
+        in_specs=[block, anywhere],
+        out_specs=block,
+        compiler_params=pltpu.CompilerParams(vmem_limit_bytes=VMEM_BYTES),
+    )(pair_near, query)
+    pair_far = lax.ppermute(far_send, "seq", upward[1:])
+    for i in range(1, bits - 1):
+        rest_blocks = rest_stack(rest_blocks, rest_step(rest_blocks, i), i, [pair_far])
+    rest_blocks = [
+        blocks.reshape((count // 2,) + blocks.shape[-2:]) for blocks in rest_blocks
+    ]
+    rest_received = [lax.ppermute(blocks, "dp", flips(0)) for blocks in rest_blocks]
+    rest_operands = [array for pair in zip(rest_blocks, rest_received) for array in pair]
 
     window_specs = [
         per_seq(far, 2 * size),
@@ -813,6 +846,10 @@
             anywhere,
             anywhere,
             anywhere,
+            anywhere,
+            anywhere,
+            anywhere,
+            anywhere,
             whole(1, width),
             whole(1, width),
             whole(1, width),
@@ -820,15 +857,14 @@
         [
             pltpu.VMEM((rows, units), f32),
             pltpu.VMEM((rows, units), f32),
-            pltpu.VMEM((count // 2, 2) + gate_up_shard.shape, low),
-            pltpu.VMEM((count // 2, 2) + pair_shard.shape, low),
-            pltpu.SemaphoreType.DMA((4,)),
+            pltpu.VMEM((count // 2, 2, 2 * gate_weight.shape[0], width), low),
+            pltpu.VMEM((count // 2, 2, down_weight.shape[0], pair_width), low),
+            pltpu.SemaphoreType.DMA((8,)),
         ],
         4 * tokens_all * width * (heads * size + 3 * units),
         40_000_000,
     )(
-        core_side, mixed, tokens, cotangent, gate_up_half, gate_up_received, pair_half, pair_received,
-        g_attn, g_pre, g_ffn,
+        core_side, mixed, tokens, cotangent, *rest_operands, g_attn, g_pre, g_ffn,
     )
 
     def flat(values):
@@ -1120,7 +1156,6 @@
         grad_gains.astype(low).reshape(count, 1, gain_rows),
         ((0, 0), (0, 15), (0, width - gain_rows)),
     )
-    query_rows = query_weight.shape[0]
     rest_sum = RowSum(
         [
             grad_w_query.reshape(count, query_rows, width),
@@ -1131,10 +1166,11 @@
         back_b,
         -2,
     )
-    for bit in back_b:
+    rest_sum.step(back_b[0])
+    gate_up_part = gate_up_sum.ordered_total([rest_sum.sent])
+    for bit in back_b[1:]:
         rest_sum.step(bit)
     down_out_total = seq_sum(down_out_part)
-    gate_up_part = gate_up_sum.ordered_total([input_grad])
     gate_total = seq_sum(gate_up_part[:shard_units])
     up_total = seq_sum(gate_up_part[shard_units:])
     rest_total = seq_sum(rest_sum.total())

time: 368 us -> 356 us (0.967)
  Pallas kernels: 181 us -> 169 us
  local copies, waits for them, and re-layouts: 32.7 us -> 27.2 us
  waiting for transfers between devices: 64.1 us -> 68.1 us
    pallas_call x14 -> x9, Pallas kernels: 33.9 us -> 26.5 us  [the longest x5 15 us: stack_step(): pl.pallas_call(functools.partial(stack_kernel, bits, axes, len(arrived)),...]
    pallas_call x6, Pallas kernels: 19.5 us -> 15.3 us  [ordered_total(): pl.pallas_call(functools.partial(sum_kernel, len(terms)), out_shape=jax.S...]
    unnamed x131 -> x143, local copies, waits for them, and re-layouts: 18.8 us -> 14.9 us
    ppermute x12 -> x15, starting transfers between devices: 11.9 us -> 14.1 us  [the longest x8 8.36 us: rest_step(): lax.ppermute(own, 'dp', flips(order[i]))]
    ppermute x12 -> x15, waiting for transfers between devices: 29.7 us -> 30.8 us  [the longest x8 15 us: rest_step(): lax.ppermute(own, 'dp', flips(order[i]))]
  transfers between devices with their start and end apart: 41 -> 44, of which waited for: 14 -> 15; matrix products, arithmetic and copies ran while one was open for 8% -> 7% of each run, Pallas kernels for 33% -> 26%
where the time goes in v3:
time: 356 us; the launch traced here: 349 us
  Pallas kernels  169 us (47%)
  waiting for transfers between devices  68.1 us (19%)
  starting transfers between devices  65.8 us (18%)
  local copies, waits for them, and re-layouts  27.2 us (8%)
  other arithmetic  14.1 us (4%)
    pallas_call x6, Pallas kernels, seq_call(): pl.pallas_call(kernel, grid=(1,), out_shape=outs, in_specs=in_specs, out_...  41.4 us
    pallas_call x1, Pallas kernels, body(): call(functools.partial(middle_kernel, heads, 512), [array((seqs, rows, wi...  38.1 us
    ppermute x4, starting transfers between devices, seq_sum(): terms.append(lax.ppermute(total().astype(jnp.bfloat16), 'seq', pairs))  27.1 us
    ppermute x4, waiting for transfers between devices, seq_sum(): received = lax.ppermute(result.astype(jnp.bfloat16), 'seq', pairs)  20.5 us
    pallas_call x6, Pallas kernels, ordered_total(): pl.pallas_call(functools.partial(sum_kernel, len(terms)), out_shape=jax.S...  15.3 us
    ppermute x8, waiting for transfers between devices, rest_step(): lax.ppermute(own, 'dp', flips(order[i]))  15 us
    pallas_call x5, Pallas kernels, stack_step(): pl.pallas_call(functools.partial(stack_kernel, bits, axes, len(arrived)),...  15 us
    unnamed x143, local copies, waits for them, and re-layouts  14.9 us
  transfers between devices with their start and end apart: 44, of which 15 were waited for; matrix products, arithmetic and copies ran while one was open for 7% of the time, Pallas kernels for 26%

profile of v3, /device:TPU:0, one launch (start us, length us, event | category | flops | bytes accessed | tf_op | source)
XLA Modules:
  0.0 349.5 jit_solution(10836608740360031673)
XLA Ops:
  3.7 3.0 collective-permute-start
  6.6 6.6 %collective-permute-done.refs_1_.refs_0_ = bf16[208,640]{1,0:T(8,128)(2,1)S(1)} collective-permute-done((bf16[208,640]{1,0:T(8,128)(2,1)}, bf16[208,640]{1,0:T(8,128)(2,1)S(1)}, u32[]{:S(2)}, u32[]{:S(2)}) %collective-permute-start) | collective-permute-done | bytes 266272 | tf_op jit(solution)/shard_map/ppermute | solution.py:646
  13.9 1.9 shard_map.468.refs_0_
  17.5 2.6 shard_map.469
  20.1 9.2 %collective-permute-done.1.refs_1_ = bf16[2,208,640]{2,1,0:T(8,128)(2,1)S(1)} collective-permute-done((bf16[2,208,640]{2,1,0:T(8,128)(2,1)}, bf16[2,208,640]{2,1,0:T(8,128)(2,1)S(1)}, u32[]{:S(2)}, u32[]{:S(2)}) %collective-permute-start.1) | collective-permute-done | bytes 532512 | tf_op jit(solution)/shard_map/ppermute | solution.py:676
  30.1 2.3 shard_map.470.refs_0_
  34.4 2.8 multiply_sine_fusion
  42.2 3.0 shard_map.471
  47.3 2.0 fusion.31
  49.2 3.3 collective-permute-done.5.refs_4_.refs_5_
  54.5 5.0 %shard_map.472 = (bf16[3,320,640]{2,1,0:T(8,128)(2,1)}, bf16[3,320,512]{2,1,0:T(8,128)(2,1)}, bf16[3,320,256]{2,1,0:T(8,128)(2,1)}) custom-call(bf16[3,320,640]{2,1,0:T(8,128)(2,1)} %x_ref.9, f32[3,320,128]{2,1,0:T(8,128)} %get-tuple-element.193.cos_ref, f32[3,320,128]{2,1,0:T(8,128)} %get-tuple-element.192.sin_ref, bf16[256,640]{1,0:T(8,128)(2,1)} %bitcast.136, ...), custom_call_target="tpu_custom_call" | custom-call | flops 629145600 | bytes 6000000 | tf_op jit(solution)/shard_map/pallas_call | solution.py:725
  59.6 3.5 %collective-permute-start.7 = (bf16[3,320,512]{2,1,0:T(8,128)(2,1)}, bf16[3,320,512]{2,1,0:T(8,128)(2,1)S(1)}, u32[]{:S(2)}, u32[]{:S(2)}) collective-permute-start(bf16[3,320,512]{2,1,0:T(8,128)(2,1)} %get-tuple-element.89.refs_8_.own_ref), channel_id=1, source_target_pairs={{0,1},{1,2},{2,3},{4,5},{5,6},{6,7},{8,9},{9,10},{10,11},{12,13},{... | collective-permute-start | bytes 2949128 | tf_op jit(solution)/shard_map/ppermute | solution.py:750
  64.3 3.0 shard_map.473
  69.4 5.7 %shard_map.474 = (bf16[3,2,640,256]{3,2,1,0:T(8,128)(2,1)}, bf16[3,2,640,256]{3,2,1,0:T(8,128)(2,1)}) custom-call(bf16[3,320,640]{2,1,0:T(8,128)(2,1)} %get-tuple-element.88.normed_ref, f32[3,320,128]{2,1,0:T(8,128)} %get-tuple-element.193.cos_ref, f32[3,320,128]{2,1,0:T(8,128)} %get-tuple-element.192.sin_ref, bf16[1024,640]{1,0:T(8,128)(2,1)} %bitcast.123, ...), custom_call_target="tpu_custom_call" | custom-call | flops 1258291200 | bytes 8000000 | tf_op jit(solution)/shard_map/pallas_call | solution.py:752
  75.1 8.8 %collective-permute-done.7.near_ref = bf16[3,320,512]{2,1,0:T(8,128)(2,1)S(1)} collective-permute-done((bf16[3,320,512]{2,1,0:T(8,128)(2,1)}, bf16[3,320,512]{2,1,0:T(8,128)(2,1)S(1)}, u32[]{:S(2)}, u32[]{:S(2)}) %collective-permute-start.7) | collective-permute-done | bytes 983072 | tf_op jit(solution)/shard_map/ppermute | solution.py:750
  84.8 2.1 shard_map.475
  90.0 9.4 %collective-permute-done.11.refs_5_ = bf16[2,80,1536]{2,1,0:T(8,128)(2,1)S(1)} collective-permute-done((bf16[2,80,1536]{2,1,0:T(8,128)(2,1)S(1)}, bf16[2,80,1536]{2,1,0:T(8,128)(2,1)S(1)}, u32[]{:S(2)}, u32[]{:S(2)}) %collective-permute-start.11) | collective-permute-done | bytes 491552 | tf_op jit(solution)/shard_map/ppermute | solution.py:663
  102.6 4.7 %shard_map.477 = (bf16[2,2,256,640]{3,2,1,0:T(8,128)(2,1)}, bf16[2,2,256,640]{3,2,1,0:T(8,128)(2,1)}, bf16[2,2,80,1536]{3,2,1,0:T(8,128)(2,1)}, bf16[2,2,80,1536]{3,2,1,0:T(8,128)(2,1)}) custom-call(s32[1]{0:T(128)} %bitcast.1.index_ref, bf16[2,256,640]{2,1,0:T(8,128)(2,1)} %get-tuple-element.90.refs_0_, bf16[2,256,640]{2,1,0:T(8,128)(2,1)} %copy-done.31, ...), custom_call_target="tpu_custom_call" | custom-call | tf_op jit(solution)/shard_map/pallas_call | solution.py:464
  108.3 7.9 %shard_map.476.mixed_ref = bf16[3,320,1024]{2,1,0:T(8,128)(2,1)} custom-call(bf16[3,2,640,256]{3,2,1,0:T(8,128)(2,1)} %get-tuple-element.91.refs_0_.q_ref, bf16[3,192,512]{2,1,0:T(8,128)(2,1)} %copy-done.32, bf16[3,320,512]{2,1,0:T(8,128)(2,1)} %copy-done.19, bf16[3,320,512]{2,1,0:T(8,128)(2,1)} %get-tuple-element.89.refs_8_.own_ref, ...), custom_call_target="tpu_custom_call" | custom-call | flops 5284823040 | bytes 16000000 | tf_op jit(solution)/shard_map/pallas_call | solution.py:793
  117.8 38.1 %shard_map.478 = (bf16[3,320,640]{2,1,0:T(8,128)(2,1)}, bf16[3,320,640]{2,1,0:T(8,128)(2,1)}, bf16[3,320,2048]{2,1,0:T(8,128)(2,1)}, bf16[3,320,640]{2,1,0:T(8,1...) custom-call(s32[1]{0:T(128)} %bitcast.side_ref, ...), custom_call_target="tpu_custom_call" | custom-call | flops 17616076800 | bytes 40000000 | tf_op jit(solution)/shard_map/pallas_call | solution.py:814
  155.9 10.3 %shard_map.479 = (bf16[4,80,3072]{2,1,0:T(8,128)(2,1)}, bf16[4,80,3072]{2,1,0:T(8,128)(2,1)}) custom-call(s32[1]{0:T(128)} %bitcast.side_ref, bf16[960,2048]{1,0:T(8,128)(2,1)} %bitcast.172, bf16[960,1024]{1,0:T(8,128)(2,1)} %bitcast.173, bf16[960,640]{1,0:T(8,128)(2,1)} %bitcast.175, bf16[960,640]{1,0:T(8,128)(2,1)} %bitcast.176), custom_call_target="tpu_custom_call" | custom-call | flops 3774873600 | bytes 13000000 | tf_op jit(solution)/shard_map/pallas_call | solution.py:892
  166.2 13.1 %shard_map.480 = (bf16[4,512,640]{2,1,0:T(8,128)(2,1)}, bf16[4,512,640]{2,1,0:T(8,128)(2,1)}) custom-call(s32[1]{0:T(128)} %bitcast.side_ref, bf16[960,2048]{1,0:T(8,128)(2,1)} %bitcast.170, bf16[960,2048]{1,0:T(8,128)(2,1)} %bitcast.171, bf16[960,640]{1,0:T(8,128)(2,1)} %bitcast.174, bf16[4,80,3072]{2,1,0:T(8,128)(2,1)} %get-tuple-element.108.after_ref), custom_call_target="tpu_custom_call" | custom-call | flops 5033164800 | bytes 14000000 | tf_op jit(solution)/shard_map/pallas_call | solution.py:928
  179.8 9.1 %shard_map.481 = (bf16[1,192,512]{2,1,0:T(8,128)(2,1)}, f32[1,320,512]{2,1,0:T(8,128)}, f32[1,320,512]{2,1,0:T(8,128)}, bf16[3,320,1024]{2,1,0:T(8,128)(2,1)}, f32[1,1,256]{2,1,0:T(1,128)}) custom-call(bf16[3,2,640,256]{3,2,1,0:T(8,128)(2,1)} %get-tuple-element.91.refs_0_.q_ref, bf16[3,2,640,256]{3,2,1,0:T(8,128)(2,1)} %get-tuple-element.100.qraw_ref, ...), custom_call_target="tpu_custom_call" | custom-call | flops 5284823040 | bytes 8000000 | tf_op jit(solution)/shard_map/pallas_call | solution.py:967
  189.6 2.4 shard_map.482.refs_2_
  194.0 2.7 shard_map.483.refs_1_
  197.5 9.1 %shard_map.484 = (bf16[1,192,512]{2,1,0:T(8,128)(2,1)}, f32[1,320,512]{2,1,0:T(8,128)}, f32[1,320,512]{2,1,0:T(8,128)}, bf16[3,320,1024]{2,1,0:T(8,128)(2,1)}, f32[1,1,256]{2,1,0:T(1,128)}) custom-call(bf16[3,2,640,256]{3,2,1,0:T(8,128)(2,1)} %get-tuple-element.91.refs_0_.q_ref, ...), custom_call_target="tpu_custom_call", output_to_operand_aliasing={{3}: (12, {})} | custom-call | flops 5284823040 | bytes 8000000 | tf_op jit(solution)/shard_map/pallas_call | solution.py:967
  208.0 1.9 shard_map.485.refs_1_
  211.2 9.0 %shard_map.486 = (bf16[1,192,512]{2,1,0:T(8,128)(2,1)}, f32[1,320,512]{2,1,0:T(8,128)}, f32[1,320,512]{2,1,0:T(8,128)}, bf16[3,320,1024]{2,1,0:T(8,128)(2,1)}, f32[1,1,256]{2,1,0:T(1,128)}) custom-call(bf16[3,2,640,256]{3,2,1,0:T(8,128)(2,1)} %get-tuple-element.91.refs_0_.q_ref, ...), custom_call_target="tpu_custom_call", output_to_operand_aliasing={{3}: (12, {})} | custom-call | flops 5284823040 | bytes 8000000 | tf_op jit(solution)/shard_map/pallas_call | solution.py:967
  221.6 2.3 shard_map.487
  225.8 1.9 shard_map.488.refs_0_
  229.0 5.4 %shard_map.489.refs_0_ = bf16[1024,640]{1,0:T(8,128)(2,1)} custom-call(bf16[960,1024]{1,0:T(8,128)(2,1)} %bitcast.122, bf16[960,640]{1,0:T(8,128)(2,1)} %bitcast.155, bf16[1,320,512]{2,1,0:T(8,128)(2,1)} %shard_map.488.refs_0_, bf16[80,3072]{1,0:T(8,128)(2,1)} %bitcast.148), custom_call_target="tpu_custom_call" | custom-call | flops 1258291200 | bytes 5000000 | tf_op jit(solution)/shard_map/pallas_call | solution.py:1066
  235.1 1.9 shard_map.490.refs_3_
  240.8 2.6 shard_map.491
  244.9 4.7 %shard_map.492 = (f32[3,320,640]{2,1,0:T(8,128)}, bf16[3,320,512]{2,1,0:T(8,128)(2,1)}, f32[1,1,640]{2,1,0:T(1,128)}, f32[1,1,256]{2,1,0:T(1,128)}) custom-call(f32[1,320,512]{2,1,0:T(8,128)} %get-tuple-element.113.refs_2_.own_ref, bf16[1,320,512]{2,1,0:T(8,128)(2,1)} %collective-permute-done.25.recv_ref, bf16[3,320,256]{2,1,0:T(8,128)(2,1)} %get-tuple-element.124.kraw_ref, ...), custom_call_target="tpu_custom_call" | custom-call | flops 629145600 | bytes 8000000 | tf_op jit(solution)/shard_map/pallas_call | solution.py:967
  249.6 4.7 %shard_map.493 = (f32[3,320,640]{2,1,0:T(8,128)}, bf16[3,320,512]{2,1,0:T(8,128)(2,1)}, f32[1,1,640]{2,1,0:T(1,128)}, f32[1,1,256]{2,1,0:T(1,128)}) custom-call(f32[1,320,512]{2,1,0:T(8,128)} %get-tuple-element.117.refs_0_.own_ref, bf16[1,320,512]{2,1,0:T(8,128)(2,1)} %collective-permute-done.24.recv_ref, ...), custom_call_target="tpu_custom_call", output_to_operand_aliasing={{0}: (13, {}), {1}: (14, {})} | custom-call | flops 629145600 | bytes 8000000 | tf_op jit(solution)/shard_map/pallas_call | solution.py:967
  254.3 2.5 shard_map.494
  256.8 10.6 %collective-permute-start.34 = (bf16[80,3072]{1,0:T(8,128)(2,1)}, bf16[80,3072]{1,0:T(8,128)(2,1)S(1)}, u32[]{:S(2)}, u32[]{:S(2)}) collective-permute-start(bf16[80,3072]{1,0:T(8,128)(2,1)} %bitcast.127), channel_id=1, source_target_pairs={{0,1},{3,2},{4,5},{7,6},{8,9},{11,10},{12,13},{15,14},{16,17},{19,... | collective-permute-start | bytes 1474568 | tf_op jit(solution)/shard_map/ppermute | solution.py:583
  268.1 4.8 %shard_map.495 = (f32[3,320,640]{2,1,0:T(8,128)}, bf16[3,320,512]{2,1,0:T(8,128)(2,1)}, f32[1,1,640]{2,1,0:T(1,128)}, f32[1,1,256]{2,1,0:T(1,128)}) custom-call(f32[1,320,512]{2,1,0:T(8,128)} %get-tuple-element.118.refs_3_.own_ref, bf16[1,320,512]{2,1,0:T(8,128)(2,1)} %copy-done.38, ...), custom_call_target="tpu_custom_call", output_to_operand_aliasing={{0}: (13, {}), {1}: (14, {})} | custom-call | flops 629145600 | bytes 8000000 | tf_op jit(solution)/shard_map/pallas_call | solution.py:967
  273.0 3.1 fusion
  280.1 2.8 shard_map.496
  284.1 8.0 %collective-permute-start.41 = (bf16[256,640]{1,0:T(8,128)(2,1)S(1)}, bf16[256,640]{1,0:T(8,128)(2,1)S(1)}, u32[]{:S(2)}, u32[]{:S(2)}) collective-permute-start(bf16[256,640]{1,0:T(8,128)(2,1)S(1)} %get-tuple-element.171), channel_id=1, source_target_pairs={{0,1},{3,2},{4,5},{7,6},{8,9},{11,10},{12,13},{15,14},{16,17},{19,... | collective-permute-start | bytes 983048 | tf_op jit(solution)/shard_map/ppermute | solution.py:583
  292.2 4.9 %collective-permute-done.41 = bf16[256,640]{1,0:T(8,128)(2,1)S(1)} collective-permute-done((bf16[256,640]{1,0:T(8,128)(2,1)S(1)}, bf16[256,640]{1,0:T(8,128)(2,1)S(1)}, u32[]{:S(2)}, u32[]{:S(2)}) %collective-permute-start.41) | collective-permute-done | bytes 327712 | tf_op jit(solution)/shard_map/ppermute | solution.py:583
  299.4 6.0 %collective-permute-start.38 = (bf16[256,640]{1,0:T(8,128)(2,1)S(1)}, bf16[256,640]{1,0:T(8,128)(2,1)S(1)}, u32[]{:S(2)}, u32[]{:S(2)}) collective-permute-start(bf16[256,640]{1,0:T(8,128)(2,1)S(1)} %get-tuple-element.172), channel_id=1, source_target_pairs={{0,1},{3,2},{4,5},{7,6},{8,9},{11,10},{12,13},{15,14},{16,17},{19,... | collective-permute-start | bytes 983048 | tf_op jit(solution)/shard_map/ppermute | solution.py:583
  307.7 7.5 %collective-permute-done.36 = bf16[80,3072]{1,0:T(8,128)(2,1)S(1)} collective-permute-done((bf16[80,3072]{1,0:T(8,128)(2,1)S(1)}, bf16[80,3072]{1,0:T(8,128)(2,1)S(1)}, u32[]{:S(2)}, u32[]{:S(2)}) %collective-permute-start.36) | collective-permute-done | bytes 491552 | tf_op jit(solution)/shard_map/ppermute | solution.py:589
  318.7 1.8 multiply_subtract_fusion.1
  323.0 2.6 collective-permute-start.31
  333.0 3.5 %collective-permute-done.40 = bf16[256,640]{1,0:T(8,128)(2,1)S(1)} collective-permute-done((bf16[256,640]{1,0:T(8,128)(2,1)S(1)}, bf16[256,640]{1,0:T(8,128)(2,1)S(1)}, u32[]{:S(2)}, u32[]{:S(2)}) %collective-permute-start.40) | collective-permute-done | bytes 327712 | tf_op jit(solution)/shard_map/ppermute | solution.py:589
  338.3 8.1 %collective-permute-done.33 = bf16[208,640]{1,0:T(8,128)(2,1)S(1)} collective-permute-done((bf16[208,640]{1,0:T(8,128)(2,1)S(1)}, bf16[208,640]{1,0:T(8,128)(2,1)S(1)}, u32[]{:S(2)}, u32[]{:S(2)}) %collective-permute-start.33) | collective-permute-done | bytes 266272 | tf_op jit(solution)/shard_map/ppermute | solution.py:589
  (271 shorter events, 75.6 us)
Async XLA Ops:
  3.7 9.6 %collective-permute-start = (bf16[208,640]{1,0:T(8,128)(2,1)}, bf16[208,640]{1,0:T(8,128)(2,1)S(1)}, u32[]{:S(2)}, u32[]{:S(2)}) collective-permute-start(bf16[208,640]{1,0:T(8,128)(2,1)} %shard_map.467.refs_0_), channel_id=1, source_target_pairs={{0,16},{4,20},{8,24},{12,28},{16,0},{20,4},{24,8},{28,12},{1,17},{... | collective-permute-start | bytes 798728 | tf_op jit(solution)/shard_map/ppermute | solution.py:646
  15.8 13.5 %collective-permute-start.1 = (bf16[2,208,640]{2,1,0:T(8,128)(2,1)}, bf16[2,208,640]{2,1,0:T(8,128)(2,1)S(1)}, u32[]{:S(2)}, u32[]{:S(2)}) collective-permute-start(bf16[2,208,640]{2,1,0:T(8,128)(2,1)} %shard_map.468.refs_0_), channel_id=1, source_target_pairs={{0,8},{4,12},{8,0},{12,4},{16,24},{20,28},{24,16},{28,20},{1,9},{5... | collective-permute-start | bytes 1597448 | tf_op jit(solution)/shard_map/ppermute | solution.py:676
  32.4 8.8 %collective-permute-start.2 = (bf16[2,2,208,640]{3,2,1,0:T(8,128)(2,1)}, bf16[2,2,208,640]{3,2,1,0:T(8,128)(2,1)S(1)}, u32[]{:S(2)}, u32[]{:S(2)}) collective-permute-start(bf16[2,2,208,640]{3,2,1,0:T(8,128)(2,1)} %shard_map.470.refs_0_), channel_id=1, source_target_pairs={{0,4},{4,0},{8,12},{12,8},{16,20},{20,16},{24,28},{28,24},{1,5},{5... | collective-permute-start | bytes 3194888 | tf_op jit(solution)/shard_map/ppermute | solution.py:676
  37.2 16.5 %collective-permute-start.3 = (bf16[256,640]{1,0:T(8,128)(2,1)S(1)}, bf16[256,640]{1,0:T(8,128)(2,1)S(1)}, u32[]{:S(2)}, u32[]{:S(2)}) collective-permute-start(bf16[256,640]{1,0:T(8,128)(2,1)S(1)} %copy-done.7), channel_id=1, source_target_pairs={{0,8},{4,12},{8,0},{12,4},{16,24},{20,28},{24,16},{28,20},{1,9},{5... | collective-permute-start | bytes 983048 | tf_op jit(solution)/shard_map/ppermute | solution.py:663
  38.6 15.1 %collective-permute-start.4 = (bf16[256,640]{1,0:T(8,128)(2,1)S(1)}, bf16[256,640]{1,0:T(8,128)(2,1)S(1)}, u32[]{:S(2)}, u32[]{:S(2)}) collective-permute-start(bf16[256,640]{1,0:T(8,128)(2,1)S(1)} %copy-done.45), channel_id=1, source_target_pairs={{0,16},{4,20},{8,24},{12,28},{16,0},{20,4},{24,8},{28,12},{1,17},{... | collective-permute-start | bytes 983048 | tf_op jit(solution)/shard_map/ppermute | solution.py:663
  40.1 12.4 %collective-permute-start.5 = (bf16[80,1536]{1,0:T(8,128)(2,1)S(1)}, bf16[80,1536]{1,0:T(8,128)(2,1)S(1)}, u32[]{:S(2)}, u32[]{:S(2)}) collective-permute-start(bf16[80,1536]{1,0:T(8,128)(2,1)S(1)} %copy-done.46), channel_id=1, source_target_pairs={{0,8},{4,12},{8,0},{12,4},{16,24},{20,28},{24,16},{28,20},{1,9},{5... | collective-permute-start | bytes 737288 | tf_op jit(solution)/shard_map/ppermute | solution.py:663
  40.6 13.0 %collective-permute-start.6 = (bf16[80,1536]{1,0:T(8,128)(2,1)S(1)}, bf16[80,1536]{1,0:T(8,128)(2,1)S(1)}, u32[]{:S(2)}, u32[]{:S(2)}) collective-permute-start(bf16[80,1536]{1,0:T(8,128)(2,1)S(1)} %copy-done.47), channel_id=1, source_target_pairs={{0,16},{4,20},{8,24},{12,28},{16,0},{20,4},{24,8},{28,12},{1,17},{... | collective-permute-start | bytes 737288 | tf_op jit(solution)/shard_map/ppermute | solution.py:663
  59.6 24.3 %collective-permute-start.7 = (bf16[3,320,512]{2,1,0:T(8,128)(2,1)}, bf16[3,320,512]{2,1,0:T(8,128)(2,1)S(1)}, u32[]{:S(2)}, u32[]{:S(2)}) collective-permute-start(bf16[3,320,512]{2,1,0:T(8,128)(2,1)} %get-tuple-element.89.refs_8_.own_ref), channel_id=1, source_target_pairs={{0,1},{1,2},{2,3},{4,5},{5,6},{6,7},{8,9},{9,10},{10,11},{12,13},{... | collective-permute-start | bytes 2949128 | tf_op jit(solution)/shard_map/ppermute | solution.py:750
  67.4 33.2 %collective-permute-start.10 = (bf16[2,256,640]{2,1,0:T(8,128)(2,1)}, bf16[2,256,640]{2,1,0:T(8,128)(2,1)S(1)}, u32[]{:S(2)}, u32[]{:S(2)}) collective-permute-start(bf16[2,256,640]{2,1,0:T(8,128)(2,1)} %get-tuple-element.92.refs_2_), channel_id=1, source_target_pairs={{0,8},{4,12},{8,0},{12,4},{16,24},{20,28},{24,16},{28,20},{1,9},{5... | collective-permute-start | bytes 1966088 | tf_op jit(solution)/shard_map/ppermute | solution.py:663
  67.9 32.7 %collective-permute-start.9 = (bf16[2,256,640]{2,1,0:T(8,128)(2,1)}, bf16[2,256,640]{2,1,0:T(8,128)(2,1)S(1)}, u32[]{:S(2)}, u32[]{:S(2)}) collective-permute-start(bf16[2,256,640]{2,1,0:T(8,128)(2,1)} %get-tuple-element.90.refs_0_), channel_id=1, source_target_pairs={{0,16},{4,20},{8,24},{12,28},{16,0},{20,4},{24,8},{28,12},{1,17},{... | collective-permute-start | bytes 1966088 | tf_op jit(solution)/shard_map/ppermute | solution.py:663
  87.0 13.6 %collective-permute-start.8 = (bf16[3,192,512]{2,1,0:T(8,128)(2,1)}, bf16[3,192,512]{2,1,0:T(8,128)(2,1)S(1)}, u32[]{:S(2)}, u32[]{:S(2)}) collective-permute-start(bf16[3,192,512]{2,1,0:T(8,128)(2,1)} %shard_map.475), channel_id=1, source_target_pairs={{1,2},{2,3},{5,6},{6,7},{9,10},{10,11},{13,14},{14,15},{17,18},{18... | collective-permute-start | bytes 1769480 | tf_op jit(solution)/shard_map/ppermute | solution.py:776
  87.7 11.6 %collective-permute-start.11 = (bf16[2,80,1536]{2,1,0:T(8,128)(2,1)S(1)}, bf16[2,80,1536]{2,1,0:T(8,128)(2,1)S(1)}, u32[]{:S(2)}, u32[]{:S(2)}) collective-permute-start(bf16[2,80,1536]{2,1,0:T(8,128)(2,1)S(1)} %copy-done.34), channel_id=1, source_target_pairs={{0,16},{4,20},{8,24},{12,28},{16,0},{20,4},{24,8},{28,12},{1,17},{... | collective-permute-start | bytes 1474568 | tf_op jit(solution)/shard_map/ppermute | solution.py:663
  89.3 11.3 %collective-permute-start.12 = (bf16[2,80,1536]{2,1,0:T(8,128)(2,1)S(1)}, bf16[2,80,1536]{2,1,0:T(8,128)(2,1)S(1)}, u32[]{:S(2)}, u32[]{:S(2)}) collective-permute-start(bf16[2,80,1536]{2,1,0:T(8,128)(2,1)S(1)} %copy-done.35), channel_id=1, source_target_pairs={{0,8},{4,12},{8,0},{12,4},{16,24},{20,28},{24,16},{28,20},{1,9},{5... | collective-permute-start | bytes 1474568 | tf_op jit(solution)/shard_map/ppermute | solution.py:663
  107.3 9.0 %collective-permute-start.13 = (bf16[4,256,640]{2,1,0:T(8,128)(2,1)}, bf16[4,256,640]{2,1,0:T(8,128)(2,1)S(1)}, u32[]{:S(2)}, u32[]{:S(2)}) collective-permute-start(bf16[4,256,640]{2,1,0:T(8,128)(2,1)} %bitcast.162), channel_id=1, source_target_pairs={{0,4},{4,0},{8,12},{12,8},{16,20},{20,16},{24,28},{28,24},{1,5},{5... | collective-permute-start | bytes 3932168 | tf_op jit(solution)/shard_map/ppermute | solution.py:782
  107.3 9.0 %collective-permute-start.14 = (bf16[4,256,640]{2,1,0:T(8,128)(2,1)}, bf16[4,256,640]{2,1,0:T(8,128)(2,1)S(1)}, u32[]{:S(2)}, u32[]{:S(2)}) collective-permute-start(bf16[4,256,640]{2,1,0:T(8,128)(2,1)} %bitcast.164), channel_id=1, source_target_pairs={{0,4},{4,0},{8,12},{12,8},{16,20},{20,16},{24,28},{28,24},{1,5},{5... | collective-permute-start | bytes 3932168 | tf_op jit(solution)/shard_map/ppermute | solution.py:782
  107.8 8.4 %collective-permute-start.15 = (bf16[4,80,1536]{2,1,0:T(8,128)(2,1)}, bf16[4,80,1536]{2,1,0:T(8,128)(2,1)}, u32[]{:S(2)}, u32[]{:S(2)}) collective-permute-start(bf16[4,80,1536]{2,1,0:T(8,128)(2,1)} %bitcast.166), channel_id=1, source_target_pairs={{0,4},{4,0},{8,12},{12,8},{16,20},{20,16},{24,28},{28,24},{1,5},{5... | collective-permute-start | bytes 2949128 | tf_op jit(solution)/shard_map/ppermute | solution.py:782
  107.8 8.4 %collective-permute-start.16 = (bf16[4,80,1536]{2,1,0:T(8,128)(2,1)}, bf16[4,80,1536]{2,1,0:T(8,128)(2,1)}, u32[]{:S(2)}, u32[]{:S(2)}) collective-permute-start(bf16[4,80,1536]{2,1,0:T(8,128)(2,1)} %bitcast.168), channel_id=1, source_target_pairs={{0,4},{4,0},{8,12},{12,8},{16,20},{20,16},{24,28},{28,24},{1,5},{5... | collective-permute-start | bytes 2949128 | tf_op jit(solution)/shard_map/ppermute | solution.py:782
  179.3 13.3 %collective-permute-start.17 = (bf16[4,512,640]{2,1,0:T(8,128)(2,1)}, bf16[4,512,640]{2,1,0:T(8,128)(2,1)S(1)}, u32[]{:S(2)}, u32[]{:S(2)}) collective-permute-start(bf16[4,512,640]{2,1,0:T(8,128)(2,1)} %get-tuple-element.109.refs_0_), channel_id=1, source_target_pairs={{0,4},{4,0},{8,12},{12,8},{16,20},{20,16},{24,28},{28,24},{1,5},{5... | collective-permute-start | bytes 7864328 | tf_op jit(solution)/shard_map/ppermute | solution.py:491
  179.3 10.3 %collective-permute-start.18 = (bf16[4,80,3072]{2,1,0:T(8,128)(2,1)}, bf16[4,80,3072]{2,1,0:T(8,128)(2,1)}, u32[]{:S(2)}, u32[]{:S(2)}) collective-permute-start(bf16[4,80,3072]{2,1,0:T(8,128)(2,1)} %get-tuple-element.108.after_ref), channel_id=1, source_target_pairs={{0,4},{4,0},{8,12},{12,8},{16,20},{20,16},{24,28},{28,24},{1,5},{5... | collective-permute-start | bytes 5898248 | tf_op jit(solution)/shard_map/ppermute | solution.py:491
  188.9 18.4 %collective-permute-start.19 = (bf16[1,192,512]{2,1,0:T(8,128)(2,1)}, bf16[1,192,512]{2,1,0:T(8,128)(2,1)S(1)}, u32[]{:S(2)}, u32[]{:S(2)}) collective-permute-start(bf16[1,192,512]{2,1,0:T(8,128)(2,1)} %get-tuple-element.116), channel_id=1, source_target_pairs={{2,1},{3,2},{6,5},{7,6},{10,9},{11,10},{14,13},{15,14},{18,17},{19... | collective-permute-start | bytes 589832 | tf_op jit(solution)/shard_map/ppermute | solution.py:1050
  192.0 29.6 %collective-permute-start.22 = (bf16[2,80,3072]{2,1,0:T(8,128)(2,1)}, bf16[2,80,3072]{2,1,0:T(8,128)(2,1)}, u32[]{:S(2)}, u32[]{:S(2)}) collective-permute-start(bf16[2,80,3072]{2,1,0:T(8,128)(2,1)} %shard_map.482.refs_2_), channel_id=1, source_target_pairs={{0,16},{4,20},{8,24},{12,28},{16,0},{20,4},{24,8},{28,12},{1,17},{... | collective-permute-start | bytes 2949128 | tf_op jit(solution)/shard_map/ppermute | solution.py:549
  196.7 43.0 %collective-permute-start.26 = (bf16[2,512,640]{2,1,0:T(8,128)(2,1)}, bf16[2,512,640]{2,1,0:T(8,128)(2,1)S(1)}, u32[]{:S(2)}, u32[]{:S(2)}) collective-permute-start(bf16[2,512,640]{2,1,0:T(8,128)(2,1)} %shard_map.483.refs_1_), channel_id=1, source_target_pairs={{0,8},{4,12},{8,0},{12,4},{16,24},{20,28},{24,16},{28,20},{1,9},{5... | collective-permute-start | bytes 3932168 | tf_op jit(solution)/shard_map/ppermute | solution.py:549
  206.6 18.5 %collective-permute-start.21 = (bf16[1,192,512]{2,1,0:T(8,128)(2,1)}, bf16[1,192,512]{2,1,0:T(8,128)(2,1)S(1)}, u32[]{:S(2)}, u32[]{:S(2)}) collective-permute-start(bf16[1,192,512]{2,1,0:T(8,128)(2,1)} %get-tuple-element.123), channel_id=1, source_target_pairs={{2,1},{3,2},{6,5},{7,6},{10,9},{11,10},{14,13},{15,14},{18,17},{19... | collective-permute-start | bytes 589832 | tf_op jit(solution)/shard_map/ppermute | solution.py:1050
  209.9 35.1 %collective-permute-start.25 = (bf16[1,320,512]{2,1,0:T(8,128)(2,1)}, bf16[1,320,512]{2,1,0:T(8,128)(2,1)}, u32[]{:S(2)}, u32[]{:S(2)}) collective-permute-start(bf16[1,320,512]{2,1,0:T(8,128)(2,1)} %shard_map.485.refs_1_), channel_id=1, source_target_pairs={{1,0},{2,1},{3,2},{5,4},{6,5},{7,6},{9,8},{10,9},{11,10},{13,12},{... | collective-permute-start | bytes 983048 | tf_op jit(solution)/shard_map/ppermute | solution.py:1083
  220.2 14.2 %collective-permute-start.20 = (bf16[1,192,512]{2,1,0:T(8,128)(2,1)}, bf16[1,192,512]{2,1,0:T(8,128)(2,1)S(1)}, u32[]{:S(2)}, u32[]{:S(2)}) collective-permute-start(bf16[1,192,512]{2,1,0:T(8,128)(2,1)} %get-tuple-element.120), channel_id=1, source_target_pairs={{2,1},{3,2},{6,5},{7,6},{10,9},{11,10},{14,13},{15,14},{18,17},{19... | collective-permute-start | bytes 589832 | tf_op jit(solution)/shard_map/ppermute | solution.py:1050
  223.9 30.4 %collective-permute-start.27 = (bf16[80,3072]{1,0:T(8,128)(2,1)}, bf16[80,3072]{1,0:T(8,128)(2,1)}, u32[]{:S(2)}, u32[]{:S(2)}) collective-permute-start(bf16[80,3072]{1,0:T(8,128)(2,1)} %bitcast.146), channel_id=1, source_target_pairs={{0,8},{4,12},{8,0},{12,4},{16,24},{20,28},{24,16},{28,20},{1,9},{5... | collective-permute-start | bytes 1474568 | tf_op jit(solution)/shard_map/ppermute | solution.py:549
  227.7 22.0 %collective-permute-start.24 = (bf16[1,320,512]{2,1,0:T(8,128)(2,1)}, bf16[1,320,512]{2,1,0:T(8,128)(2,1)}, u32[]{:S(2)}, u32[]{:S(2)}) collective-permute-start(bf16[1,320,512]{2,1,0:T(8,128)(2,1)} %shard_map.488.refs_0_), channel_id=1, source_target_pairs={{1,0},{2,1},{3,2},{5,4},{6,5},{7,6},{9,8},{10,9},{11,10},{13,12},{... | collective-permute-start | bytes 983048 | tf_op jit(solution)/shard_map/ppermute | solution.py:1083
  237.0 30.4 %collective-permute-start.23 = (bf16[1,320,512]{2,1,0:T(8,128)(2,1)}, bf16[1,320,512]{2,1,0:T(8,128)(2,1)S(1)}, u32[]{:S(2)}, u32[]{:S(2)}) collective-permute-start(bf16[1,320,512]{2,1,0:T(8,128)(2,1)} %shard_map.490.refs_3_), channel_id=1, source_target_pairs={{1,0},{2,1},{3,2},{5,4},{6,5},{7,6},{9,8},{10,9},{11,10},{13,12},{... | collective-permute-start | bytes 983048 | tf_op jit(solution)/shard_map/ppermute | solution.py:1083
  243.4 35.8 %collective-permute-start.37 = (bf16[512,640]{1,0:T(8,128)(2,1)}, bf16[512,640]{1,0:T(8,128)(2,1)S(1)}, u32[]{:S(2)}, u32[]{:S(2)}) collective-permute-start(bf16[512,640]{1,0:T(8,128)(2,1)} %bitcast.143), channel_id=1, source_target_pairs={{0,16},{4,20},{8,24},{12,28},{16,0},{20,4},{24,8},{28,12},{1,17},{... | collective-permute-start | bytes 1966088 | tf_op jit(solution)/shard_map/ppermute | solution.py:549
  256.8 20.8 %collective-permute-start.34 = (bf16[80,3072]{1,0:T(8,128)(2,1)}, bf16[80,3072]{1,0:T(8,128)(2,1)S(1)}, u32[]{:S(2)}, u32[]{:S(2)}) collective-permute-start(bf16[80,3072]{1,0:T(8,128)(2,1)} %bitcast.127), channel_id=1, source_target_pairs={{0,1},{3,2},{4,5},{7,6},{8,9},{11,10},{12,13},{15,14},{16,17},{19,... | collective-permute-start | bytes 1474568 | tf_op jit(solution)/shard_map/ppermute | solution.py:583
  277.5 27.8 %collective-permute-start.28 = (bf16[2,2,208,640]{3,2,1,0:T(8,128)(2,1)S(1)}, bf16[2,2,208,640]{3,2,1,0:T(8,128)(2,1)S(1)}, u32[]{:S(2)}, u32[]{:S(2)}) collective-permute-start(bf16[2,2,208,640]{3,2,1,0:T(8,128)(2,1)S(1)} %pad_maximum_fusion.refs_4_), channel_id=1, source_target_pairs={{0,4},{4,0},{8,12},{12,8},{16,20},{20,16},{24,28},{28,24},{1,5},{5... | collective-permute-start | bytes 3194888 | tf_op jit(solution)/shard_map/ppermute | solution.py:549
  278.5 19.3 %collective-permute-start.35 = (bf16[80,3072]{1,0:T(8,128)(2,1)S(1)}, bf16[80,3072]{1,0:T(8,128)(2,1)S(1)}, u32[]{:S(2)}, u32[]{:S(2)}) collective-permute-start(bf16[80,3072]{1,0:T(8,128)(2,1)S(1)} %fusion.2), channel_id=1, source_target_pairs={{1,2},{2,1},{5,6},{6,5},{9,10},{10,9},{13,14},{14,13},{17,18},{18,... | collective-permute-start | bytes 1474568 | tf_op jit(solution)/shard_map/ppermute | solution.py:585
  282.9 14.2 %copy-start.1 = (bf16[1,512,640]{2,1,0:T(8,128)(2,1)S(1)}, bf16[1,512,640]{2,1,0:T(8,128)(2,1)}, u32[]{:S(2)}) copy-start(bf16[1,512,640]{2,1,0:T(8,128)(2,1)} %shard_map.496) | copy-start | bytes 1966084
  284.1 13.0 %collective-permute-start.41 = (bf16[256,640]{1,0:T(8,128)(2,1)S(1)}, bf16[256,640]{1,0:T(8,128)(2,1)S(1)}, u32[]{:S(2)}, u32[]{:S(2)}) collective-permute-start(bf16[256,640]{1,0:T(8,128)(2,1)S(1)} %get-tuple-element.171), channel_id=1, source_target_pairs={{0,1},{3,2},{4,5},{7,6},{8,9},{11,10},{12,13},{15,14},{16,17},{19,... | collective-permute-start | bytes 983048 | tf_op jit(solution)/shard_map/ppermute | solution.py:583
  292.2 13.2 %copy-start.15 = (bf16[2,128,640]{2,1,0:T(8,128)(2,1)S(1)}, bf16[2,128,640]{2,1,0:T(8,128)(2,1)}, u32[]{:S(2)}) copy-start(bf16[2,128,640]{2,1,0:T(8,128)(2,1)} %dynamic-slice_bitcast_fusion.1) | copy-start | bytes 983044
  297.2 8.9 %collective-permute-start.42 = (bf16[256,640]{1,0:T(8,128)(2,1)S(1)}, bf16[256,640]{1,0:T(8,128)(2,1)S(1)}, u32[]{:S(2)}, u32[]{:S(2)}) collective-permute-start(bf16[256,640]{1,0:T(8,128)(2,1)S(1)} %fusion.8), channel_id=1, source_target_pairs={{1,2},{2,1},{5,6},{6,5},{9,10},{10,9},{13,14},{14,13},{17,18},{18,... | collective-permute-start | bytes 983048 | tf_op jit(solution)/shard_map/ppermute | solution.py:585
  298.0 17.1 %collective-permute-start.36 = (bf16[80,3072]{1,0:T(8,128)(2,1)S(1)}, bf16[80,3072]{1,0:T(8,128)(2,1)S(1)}, u32[]{:S(2)}, u32[]{:S(2)}) collective-permute-start(bf16[80,3072]{1,0:T(8,128)(2,1)S(1)} %fusion.6), channel_id=1, source_target_pairs={{1,0},{2,3},{5,4},{6,7},{9,8},{10,11},{13,12},{14,15},{17,16},{18,... | collective-permute-start | bytes 1474568 | tf_op jit(solution)/shard_map/ppermute | solution.py:589
  299.4 17.9 %collective-permute-start.38 = (bf16[256,640]{1,0:T(8,128)(2,1)S(1)}, bf16[256,640]{1,0:T(8,128)(2,1)S(1)}, u32[]{:S(2)}, u32[]{:S(2)}) collective-permute-start(bf16[256,640]{1,0:T(8,128)(2,1)S(1)} %get-tuple-element.172), channel_id=1, source_target_pairs={{0,1},{3,2},{4,5},{7,6},{8,9},{11,10},{12,13},{15,14},{16,17},{19,... | collective-permute-start | bytes 983048 | tf_op jit(solution)/shard_map/ppermute | solution.py:583
  305.5 10.8 %collective-permute-start.29 = (bf16[2,208,640]{2,1,0:T(8,128)(2,1)S(1)}, bf16[2,208,640]{2,1,0:T(8,128)(2,1)S(1)}, u32[]{:S(2)}, u32[]{:S(2)}) collective-permute-start(bf16[2,208,640]{2,1,0:T(8,128)(2,1)S(1)} %fusion.1), channel_id=1, source_target_pairs={{0,16},{4,20},{8,24},{12,28},{16,0},{20,4},{24,8},{28,12},{1,17},{... | collective-permute-start | bytes 1597448 | tf_op jit(solution)/shard_map/ppermute | solution.py:549
  306.2 12.5 %copy-start.8 = (f32[256,640]{1,0:T(8,128)S(1)}, f32[256,640]{1,0:T(8,128)}, u32[]{:S(2)}) copy-start(f32[256,640]{1,0:T(8,128)} %wu_ref.1) | copy-start | bytes 1966084
  306.2 12.5 %copy-start.23 = (f32[256,640]{1,0:T(8,128)S(1)}, f32[256,640]{1,0:T(8,128)}, u32[]{:S(2)}) copy-start(f32[256,640]{1,0:T(8,128)} %param.53) | copy-start | bytes 1966084
  306.3 12.4 %collective-permute-start.43 = (bf16[256,640]{1,0:T(8,128)(2,1)S(1)}, bf16[256,640]{1,0:T(8,128)(2,1)S(1)}, u32[]{:S(2)}, u32[]{:S(2)}) collective-permute-start(bf16[256,640]{1,0:T(8,128)(2,1)S(1)} %fusion.17), channel_id=1, source_target_pairs={{1,0},{2,3},{5,4},{6,7},{9,8},{10,11},{13,12},{14,15},{17,16},{18,... | collective-permute-start | bytes 983048 | tf_op jit(solution)/shard_map/ppermute | solution.py:589
  316.4 6.5 %collective-permute-start.30 = (bf16[208,640]{1,0:T(8,128)(2,1)S(1)}, bf16[208,640]{1,0:T(8,128)(2,1)S(1)}, u32[]{:S(2)}, u32[]{:S(2)}) collective-permute-start(bf16[208,640]{1,0:T(8,128)(2,1)S(1)} %fusion.9), channel_id=1, source_target_pairs={{0,8},{4,12},{8,0},{12,4},{16,24},{20,28},{24,16},{28,20},{1,9},{5... | collective-permute-start | bytes 798728 | tf_op jit(solution)/shard_map/ppermute | solution.py:549
  320.5 6.8 %collective-permute-start.39 = (bf16[256,640]{1,0:T(8,128)(2,1)S(1)}, bf16[256,640]{1,0:T(8,128)(2,1)S(1)}, u32[]{:S(2)}, u32[]{:S(2)}) collective-permute-start(bf16[256,640]{1,0:T(8,128)(2,1)S(1)} %get-tuple-element.170), channel_id=1, source_target_pairs={{1,2},{2,1},{5,6},{6,5},{9,10},{10,9},{13,14},{14,13},{17,18},{18,... | collective-permute-start | bytes 983048 | tf_op jit(solution)/shard_map/ppermute | solution.py:585
  323.0 6.5 %collective-permute-start.31 = (bf16[208,640]{1,0:T(8,128)(2,1)S(1)}, bf16[208,640]{1,0:T(8,128)(2,1)S(1)}, u32[]{:S(2)}, u32[]{:S(2)}) collective-permute-start(bf16[208,640]{1,0:T(8,128)(2,1)S(1)} %fusion.11), channel_id=1, source_target_pairs={{0,1},{3,2},{4,5},{7,6},{8,9},{11,10},{12,13},{15,14},{16,17},{19,... | collective-permute-start | bytes 798728 | tf_op jit(solution)/shard_map/ppermute | solution.py:583
  327.4 9.1 %collective-permute-start.40 = (bf16[256,640]{1,0:T(8,128)(2,1)S(1)}, bf16[256,640]{1,0:T(8,128)(2,1)S(1)}, u32[]{:S(2)}, u32[]{:S(2)}) collective-permute-start(bf16[256,640]{1,0:T(8,128)(2,1)S(1)} %fusion.16), channel_id=1, source_target_pairs={{1,0},{2,3},{5,4},{6,7},{9,8},{10,11},{13,12},{14,15},{17,16},{18,... | collective-permute-start | bytes 983048 | tf_op jit(solution)/shard_map/ppermute | solution.py:589
  329.7 1.9 collective-permute-start.32
  331.7 14.6 %collective-permute-start.33 = (bf16[208,640]{1,0:T(8,128)(2,1)S(1)}, bf16[208,640]{1,0:T(8,128)(2,1)S(1)}, u32[]{:S(2)}, u32[]{:S(2)}) collective-permute-start(bf16[208,640]{1,0:T(8,128)(2,1)S(1)} %fusion.13), channel_id=1, source_target_pairs={{1,0},{2,3},{5,4},{6,7},{9,8},{10,11},{13,12},{14,15},{17,16},{18,... | collective-permute-start | bytes 798728 | tf_op jit(solution)/shard_map/ppermute | solution.py:589
  (67 other events, 246.0 us)

commit v4 on v3

--- a/solution.py
+++ b/solution.py
@@ -571,25 +571,14 @@
 
 def seq_sum(part):
     count = lax.axis_size("seq")
-    index = lax.axis_index("seq")
-    half = count // 2
-    terms = [part]
-
-    def total():
-        return sum(term.astype(jnp.float32) for term in terms)
-
-    for t in range(half - 1):
-        pairs = [(t, t + 1), (count - 1 - t, count - 2 - t)]
-        terms.append(lax.ppermute(total().astype(jnp.bfloat16), "seq", pairs))
-    middle = [(half - 1, half), (half, half - 1)]
-    terms.append(lax.ppermute(total().astype(jnp.bfloat16), "seq", middle))
-    result = total()
-    for t in range(half - 2, -1, -1):
-        pairs = [(t + 1, t), (count - 2 - t, count - 1 - t)]
-        received = lax.ppermute(result.astype(jnp.bfloat16), "seq", pairs)
-        outer = (index == t) | (index == count - 1 - t)
-        result = jnp.where(outer, received.astype(jnp.float32), result)
-    return result
+    total = part.astype(jnp.float32)
+    distance = 1
+    while distance < count:
+        pairs = [(i, i ^ distance) for i in range(count)]
+        received = lax.ppermute(total.astype(jnp.bfloat16), "seq", pairs)
+        total = total.astype(jnp.bfloat16).astype(jnp.float32) + received.astype(jnp.float32)
+        distance *= 2
+    return total
 
 
 def body(
@@ -1058,18 +1047,21 @@
             arrived = [gate_up_sum.sent]
         elif s == 1:
             near_sums.append(near_total(near_parts[0], far_parts[0], [grad_own]))
+            from_near = [lax.ppermute(near_sums[0], "seq", downward)]
             arrived = [near_sums[0]]
     for bit in back_b[2:]:
         down_out_sum.ordered_step(bit, [own_parts[-1]])
     near_sums.append(near_total(near_parts[1], far_parts[1], [down_out_sum.sent]))
+    from_near.append(lax.ppermute(near_sums[1], "seq", downward))
     query_columns = heads * size
     grad_w_query = pl.pallas_call(
-        functools.partial(query_grad_kernel, 2),
+        functools.partial(query_grad_kernel, 3),
         grid=(heads,),
         out_shape=array((query_columns, width), low),
         in_specs=[
             pl.BlockSpec((tokens_all, size), lambda i: (0, i)),
             whole(tokens_all, width),
+            anywhere,
             anywhere,
             anywhere,
         ],
@@ -1078,11 +1070,13 @@
         cost_estimate=pl.CostEstimate(
             flops=2 * tokens_all * width * query_columns, bytes_accessed=5_000_000, transcendentals=0
         ),
-    )(flat(grad_query_low), flat(normed), near_sums[1], down_out_sum.sent)
+    )(
+        flat(grad_query_low), flat(normed), near_sums[1], down_out_sum.sent, from_near[0]
+    )
     near_sums.append(near_total(near_parts[2], far_parts[2], [grad_w_query]))
-    from_near = [lax.ppermute(near_sum, "seq", downward) for near_sum in near_sums]
+    from_near.append(lax.ppermute(near_sums[2], "seq", downward))
     for bit in back_a[2:]:
-        gate_up_sum.ordered_step(bit, [near_sums[2]])
+        gate_up_sum.ordered_step(bit, [near_sums[2], from_near[1]])
 
     def input_back(s, buffers, arrived):
         kinds = [
@@ -1137,8 +1131,11 @@
     for s in range(seqs):
         waits = [gate_up_sum.sent]
         if s == seqs - 1:
-            down_out_part = down_out_sum.ordered_total([buffers[0]])
-            waits = [down_out_part]
+            down_out_part = down_out_sum.ordered_total(
+                [buffers[0], from_near[s], gate_up_sum.received[-1][0]]
+            )
+            gate_up_part = gate_up_sum.ordered_total([down_out_part])
+            waits = [gate_up_part]
         *buffers, g_part, g_key_part = input_back(s, buffers, waits)
         input_gains.append(g_part)
         key_gains.append(g_key_part)
@@ -1166,9 +1163,7 @@
         back_b,
         -2,
     )
-    rest_sum.step(back_b[0])
-    gate_up_part = gate_up_sum.ordered_total([rest_sum.sent])
-    for bit in back_b[1:]:
+    for bit in back_b:
         rest_sum.step(bit)
     down_out_total = seq_sum(down_out_part)
     gate_total = seq_sum(gate_up_part[:shard_units])

time: 356 us -> 382 us (1.073)
  waiting for transfers between devices: 68.1 us -> 111 us
  starting transfers between devices: 65.8 us -> 47.7 us
    ppermute x15 -> x11, waiting for transfers between devices: 26.1 us -> 71.5 us  [the longest x8 60.6 us: seq_sum(): received = lax.ppermute(total.astype(jnp.bfloat16), 'seq', pairs)]
    ppermute x15 -> x11, starting transfers between devices: 39.3 us -> 20.6 us  [the longest x8 16.6 us: seq_sum(): received = lax.ppermute(total.astype(jnp.bfloat16), 'seq', pairs)]
    unnamed x143 -> x159, local copies, waits for them, and re-layouts: 14.9 us -> 16.8 us
  transfers between devices with their start and end apart: 44 -> 40, of which waited for: 15 -> 16; matrix products, arithmetic and copies ran while one was open for 7% -> 7% of each run, Pallas kernels for 26% -> 23%
where the time goes in v4:
time: 382 us; the launch traced here: 376 us
  Pallas kernels  169 us (44%)
  waiting for transfers between devices  111 us (29%)
  starting transfers between devices  47.7 us (12%)
  local copies, waits for them, and re-layouts  29.1 us (8%)
  other arithmetic  15 us (4%)
    ppermute x8, waiting for transfers between devices, seq_sum(): received = lax.ppermute(total.astype(jnp.bfloat16), 'seq', pairs)  60.6 us
    pallas_call x6, Pallas kernels, seq_call(): pl.pallas_call(kernel, grid=(1,), out_shape=outs, in_specs=in_specs, out_...  41.4 us
    pallas_call x1, Pallas kernels, body(): call(functools.partial(middle_kernel, heads, 512), [array((seqs, rows, wi...  38.1 us
    unnamed x159, local copies, waits for them, and re-layouts  16.8 us
    ppermute x8, starting transfers between devices, seq_sum(): received = lax.ppermute(total.astype(jnp.bfloat16), 'seq', pairs)  16.6 us
    pallas_call x6, Pallas kernels, ordered_total(): pl.pallas_call(functools.partial(sum_kernel, len(terms)), out_shape=jax.S...  15.2 us
    ppermute x8, waiting for transfers between devices, rest_step(): lax.ppermute(own, 'dp', flips(order[i]))  15 us
    pallas_call x5, Pallas kernels, stack_step(): pl.pallas_call(functools.partial(stack_kernel, bits, axes, len(arrived)),...  14.8 us
  transfers between devices with their start and end apart: 40, of which 16 were waited for; matrix products, arithmetic and copies ran while one was open for 7% of the time, Pallas kernels for 23%

profile of v4, /device:TPU:0, one launch (start us, length us, event | category | flops | bytes accessed | tf_op | source)
XLA Modules:
  0.0 375.9 jit_solution(1537241431557772600)
XLA Ops:
  3.7 3.0 collective-permute-start
  6.6 6.6 %collective-permute-done.refs_1_.refs_0_ = bf16[208,640]{1,0:T(8,128)(2,1)S(1)} collective-permute-done((bf16[208,640]{1,0:T(8,128)(2,1)}, bf16[208,640]{1,0:T(8,128)(2,1)S(1)}, u32[]{:S(2)}, u32[]{:S(2)}) %collective-permute-start) | collective-permute-done | bytes 266272 | tf_op jit(solution)/shard_map/ppermute | solution.py:635
  17.5 2.6 shard_map.469
  20.1 9.2 %collective-permute-done.1.refs_1_ = bf16[2,208,640]{2,1,0:T(8,128)(2,1)S(1)} collective-permute-done((bf16[2,208,640]{2,1,0:T(8,128)(2,1)}, bf16[2,208,640]{2,1,0:T(8,128)(2,1)S(1)}, u32[]{:S(2)}, u32[]{:S(2)}) %collective-permute-start.1) | collective-permute-done | bytes 532512 | tf_op jit(solution)/shard_map/ppermute | solution.py:665
  30.1 2.3 shard_map.470.refs_0_
  34.4 2.8 multiply_sine_fusion
  42.2 3.0 shard_map.471
  49.2 3.3 collective-permute-done.5.refs_4_.refs_5_
  54.5 5.0 %shard_map.472 = (bf16[3,320,640]{2,1,0:T(8,128)(2,1)}, bf16[3,320,512]{2,1,0:T(8,128)(2,1)}, bf16[3,320,256]{2,1,0:T(8,128)(2,1)}) custom-call(bf16[3,320,640]{2,1,0:T(8,128)(2,1)} %x_ref.9, f32[3,320,128]{2,1,0:T(8,128)} %get-tuple-element.194.cos_ref, f32[3,320,128]{2,1,0:T(8,128)} %get-tuple-element.193.sin_ref, bf16[256,640]{1,0:T(8,128)(2,1)} %bitcast.117, ...), custom_call_target="tpu_custom_call" | custom-call | flops 629145600 | bytes 6000000 | tf_op jit(solution)/shard_map/pallas_call | solution.py:714
  59.6 3.5 collective-permute-start.7
  64.3 3.0 shard_map.473
  69.4 5.7 %shard_map.474 = (bf16[3,2,640,256]{3,2,1,0:T(8,128)(2,1)}, bf16[3,2,640,256]{3,2,1,0:T(8,128)(2,1)}) custom-call(bf16[3,320,640]{2,1,0:T(8,128)(2,1)} %get-tuple-element.88.normed_ref, f32[3,320,128]{2,1,0:T(8,128)} %get-tuple-element.194.cos_ref, f32[3,320,128]{2,1,0:T(8,128)} %get-tuple-element.193.sin_ref, bf16[1024,640]{1,0:T(8,128)(2,1)} %bitcast.105, ...), custom_call_target="tpu_custom_call" | custom-call | flops 1258291200 | bytes 8000000 | tf_op jit(solution)/shard_map/pallas_call | solution.py:741
  75.1 8.8 %collective-permute-done.7.near_ref = bf16[3,320,512]{2,1,0:T(8,128)(2,1)S(1)} collective-permute-done((bf16[3,320,512]{2,1,0:T(8,128)(2,1)}, bf16[3,320,512]{2,1,0:T(8,128)(2,1)S(1)}, u32[]{:S(2)}, u32[]{:S(2)}) %collective-permute-start.7) | collective-permute-done | bytes 983072 | tf_op jit(solution)/shard_map/ppermute | solution.py:739
  84.9 2.1 shard_map.475
  90.0 9.4 %collective-permute-done.11.refs_5_ = bf16[2,80,1536]{2,1,0:T(8,128)(2,1)S(1)} collective-permute-done((bf16[2,80,1536]{2,1,0:T(8,128)(2,1)S(1)}, bf16[2,80,1536]{2,1,0:T(8,128)(2,1)S(1)}, u32[]{:S(2)}, u32[]{:S(2)}) %collective-permute-start.11) | collective-permute-done | bytes 491552 | tf_op jit(solution)/shard_map/ppermute | solution.py:652
  102.6 4.6 %shard_map.477 = (bf16[2,2,256,640]{3,2,1,0:T(8,128)(2,1)}, bf16[2,2,256,640]{3,2,1,0:T(8,128)(2,1)}, bf16[2,2,80,1536]{3,2,1,0:T(8,128)(2,1)}, bf16[2,2,80,1536]{3,2,1,0:T(8,128)(2,1)}) custom-call(s32[1]{0:T(128)} %bitcast.1.index_ref, bf16[2,256,640]{2,1,0:T(8,128)(2,1)} %get-tuple-element.90.refs_0_, bf16[2,256,640]{2,1,0:T(8,128)(2,1)} %copy-done.37, ...), custom_call_target="tpu_custom_call" | custom-call | tf_op jit(solution)/shard_map/pallas_call | solution.py:464
  108.2 7.9 %shard_map.476.mixed_ref = bf16[3,320,1024]{2,1,0:T(8,128)(2,1)} custom-call(bf16[3,2,640,256]{3,2,1,0:T(8,128)(2,1)} %get-tuple-element.91.refs_0_.q_ref, bf16[3,192,512]{2,1,0:T(8,128)(2,1)} %copy-done.38, bf16[3,320,512]{2,1,0:T(8,128)(2,1)} %copy-done.25, bf16[3,320,512]{2,1,0:T(8,128)(2,1)} %get-tuple-element.89.refs_8_.own_ref, ...), custom_call_target="tpu_custom_call" | custom-call | flops 5284823040 | bytes 16000000 | tf_op jit(solution)/shard_map/pallas_call | solution.py:782
  117.7 38.1 %shard_map.478 = (bf16[3,320,640]{2,1,0:T(8,128)(2,1)}, bf16[3,320,640]{2,1,0:T(8,128)(2,1)}, bf16[3,320,2048]{2,1,0:T(8,128)(2,1)}, bf16[3,320,640]{2,1,0:T(8,1...) custom-call(s32[1]{0:T(128)} %bitcast.side_ref, ...), custom_call_target="tpu_custom_call" | custom-call | flops 17616076800 | bytes 40000000 | tf_op jit(solution)/shard_map/pallas_call | solution.py:803
  155.8 10.2 %shard_map.479 = (bf16[4,80,3072]{2,1,0:T(8,128)(2,1)}, bf16[4,80,3072]{2,1,0:T(8,128)(2,1)}) custom-call(s32[1]{0:T(128)} %bitcast.side_ref, bf16[960,2048]{1,0:T(8,128)(2,1)} %bitcast.157, bf16[960,1024]{1,0:T(8,128)(2,1)} %bitcast.158, bf16[960,640]{1,0:T(8,128)(2,1)} %bitcast.160, bf16[960,640]{1,0:T(8,128)(2,1)} %bitcast.161), custom_call_target="tpu_custom_call" | custom-call | flops 3774873600 | bytes 13000000 | tf_op jit(solution)/shard_map/pallas_call | solution.py:881
  166.0 12.9 %shard_map.480 = (bf16[4,512,640]{2,1,0:T(8,128)(2,1)}, bf16[4,512,640]{2,1,0:T(8,128)(2,1)}) custom-call(s32[1]{0:T(128)} %bitcast.side_ref, bf16[960,2048]{1,0:T(8,128)(2,1)} %bitcast.155, bf16[960,2048]{1,0:T(8,128)(2,1)} %bitcast.156, bf16[960,640]{1,0:T(8,128)(2,1)} %bitcast.159, bf16[4,80,3072]{2,1,0:T(8,128)(2,1)} %get-tuple-element.108.after_ref), custom_call_target="tpu_custom_call" | custom-call | flops 5033164800 | bytes 14000000 | tf_op jit(solution)/shard_map/pallas_call | solution.py:917
  179.5 9.1 %shard_map.481 = (bf16[1,192,512]{2,1,0:T(8,128)(2,1)}, f32[1,320,512]{2,1,0:T(8,128)}, f32[1,320,512]{2,1,0:T(8,128)}, bf16[3,320,1024]{2,1,0:T(8,128)(2,1)}, f32[1,1,256]{2,1,0:T(1,128)}) custom-call(bf16[3,2,640,256]{3,2,1,0:T(8,128)(2,1)} %get-tuple-element.91.refs_0_.q_ref, bf16[3,2,640,256]{3,2,1,0:T(8,128)(2,1)} %get-tuple-element.100.qraw_ref, ...), custom_call_target="tpu_custom_call" | custom-call | flops 5284823040 | bytes 8000000 | tf_op jit(solution)/shard_map/pallas_call | solution.py:956
  190.6 2.4 shard_map.482.refs_2_
  195.0 2.7 shard_map.483.refs_1_
  198.5 9.1 %shard_map.484 = (bf16[1,192,512]{2,1,0:T(8,128)(2,1)}, f32[1,320,512]{2,1,0:T(8,128)}, f32[1,320,512]{2,1,0:T(8,128)}, bf16[3,320,1024]{2,1,0:T(8,128)(2,1)}, f32[1,1,256]{2,1,0:T(1,128)}) custom-call(bf16[3,2,640,256]{3,2,1,0:T(8,128)(2,1)} %get-tuple-element.91.refs_0_.q_ref, ...), custom_call_target="tpu_custom_call", output_to_operand_aliasing={{3}: (12, {})} | custom-call | flops 5284823040 | bytes 8000000 | tf_op jit(solution)/shard_map/pallas_call | solution.py:956
  212.5 9.1 %shard_map.486 = (bf16[1,192,512]{2,1,0:T(8,128)(2,1)}, f32[1,320,512]{2,1,0:T(8,128)}, f32[1,320,512]{2,1,0:T(8,128)}, bf16[3,320,1024]{2,1,0:T(8,128)(2,1)}, f32[1,1,256]{2,1,0:T(1,128)}) custom-call(bf16[3,2,640,256]{3,2,1,0:T(8,128)(2,1)} %get-tuple-element.91.refs_0_.q_ref, ...), custom_call_target="tpu_custom_call", output_to_operand_aliasing={{3}: (12, {})} | custom-call | flops 5284823040 | bytes 8000000 | tf_op jit(solution)/shard_map/pallas_call | solution.py:956
  222.5 2.3 shard_map.487
  230.1 5.2 %shard_map.489.refs_0_ = bf16[1024,640]{1,0:T(8,128)(2,1)} custom-call(bf16[960,1024]{1,0:T(8,128)(2,1)} %bitcast.104, bf16[960,640]{1,0:T(8,128)(2,1)} %bitcast.139, bf16[1,320,512]{2,1,0:T(8,128)(2,1)} %shard_map.488.refs_0_, bf16[80,3072]{1,0:T(8,128)(2,1)} %bitcast.130, bf16[1,320,512]{2,1,0:T(8,128)(2,1)} %copy-done.14), custom_call_target="tpu_custom_call" | custom-call | flops 1258291200 | bytes 5000000 | tf_op jit(solution)/shard_map/pallas_call | solution.py:1057
  238.0 5.8 %collective-permute-done.25.refs_4_.recv_ref = bf16[1,320,512]{2,1,0:T(8,128)(2,1)} collective-permute-done((bf16[1,320,512]{2,1,0:T(8,128)(2,1)}, bf16[1,320,512]{2,1,0:T(8,128)(2,1)}, u32[]{:S(2)}, u32[]{:S(2)}) %collective-permute-start.25) | collective-permute-done | bytes 327712 | tf_op jit(solution)/shard_map/ppermute | solution.py:1055
  244.9 2.6 shard_map.491
  253.3 4.7 %shard_map.492 = (f32[3,320,640]{2,1,0:T(8,128)}, bf16[3,320,512]{2,1,0:T(8,128)(2,1)}, f32[1,1,640]{2,1,0:T(1,128)}, f32[1,1,256]{2,1,0:T(1,128)}) custom-call(f32[1,320,512]{2,1,0:T(8,128)} %get-tuple-element.113.refs_2_.own_ref, bf16[1,320,512]{2,1,0:T(8,128)(2,1)} %copy-done.14, bf16[3,320,256]{2,1,0:T(8,128)(2,1)} %get-tuple-element.124.kraw_ref, ...), custom_call_target="tpu_custom_call" | custom-call | flops 629145600 | bytes 8000000 | tf_op jit(solution)/shard_map/pallas_call | solution.py:956
  258.0 4.7 %shard_map.493 = (f32[3,320,640]{2,1,0:T(8,128)}, bf16[3,320,512]{2,1,0:T(8,128)(2,1)}, f32[1,1,640]{2,1,0:T(1,128)}, f32[1,1,256]{2,1,0:T(1,128)}) custom-call(f32[1,320,512]{2,1,0:T(8,128)} %get-tuple-element.117.refs_0_.own_ref, bf16[1,320,512]{2,1,0:T(8,128)(2,1)} %collective-permute-done.25.refs_4_.recv_ref, ...), custom_call_target="tpu_custom_call", output_to_operand_aliasing={{0}: (13, {}), {1}: (14, {})} | custom-call | flops 629145600 | bytes 8000000 | tf_op jit(solution)/shard_map/pallas_call | solution.py:956
  262.7 5.2 %collective-permute-done.24.refs_5_.recv_ref = bf16[1,320,512]{2,1,0:T(8,128)(2,1)S(1)} collective-permute-done((bf16[1,320,512]{2,1,0:T(8,128)(2,1)S(1)}, bf16[1,320,512]{2,1,0:T(8,128)(2,1)S(1)}, u32[]{:S(2)}, u32[]{:S(2)}) %collective-permute-start.24) | collective-permute-done | bytes 327712 | tf_op jit(solution)/shard_map/ppermute | solution.py:1077
  269.0 2.5 shard_map.494
  271.5 5.3 %collective-permute-start.34 = (bf16[80,3072]{1,0:T(8,128)(2,1)}, bf16[80,3072]{1,0:T(8,128)(2,1)}, u32[]{:S(2)}, u32[]{:S(2)}) collective-permute-start(bf16[80,3072]{1,0:T(8,128)(2,1)} %bitcast.127), channel_id=1, source_target_pairs={{0,1},{1,0},{2,3},{3,2},{4,5},{5,4},{6,7},{7,6},{8,9},{9,8},{10,11... | collective-permute-start | bytes 1474568 | tf_op jit(solution)/shard_map/ppermute | solution.py:578
  276.7 2.8 shard_map.495
  281.4 4.8 %shard_map.496 = (f32[3,320,640]{2,1,0:T(8,128)}, bf16[3,320,512]{2,1,0:T(8,128)(2,1)}, f32[1,1,640]{2,1,0:T(1,128)}, f32[1,1,256]{2,1,0:T(1,128)}) custom-call(f32[1,320,512]{2,1,0:T(8,128)} %get-tuple-element.118.refs_3_.own_ref, bf16[1,320,512]{2,1,0:T(8,128)(2,1)} %copy-done.21, ...), custom_call_target="tpu_custom_call", output_to_operand_aliasing={{0}: (13, {}), {1}: (14, {})} | custom-call | flops 629145600 | bytes 8000000 | tf_op jit(solution)/shard_map/pallas_call | solution.py:956
  288.1 2.0 collective-permute-start.38
  290.2 2.2 fusion
  293.0 6.0 %collective-permute-done.36 = bf16[256,640]{1,0:T(8,128)(2,1)S(1)} collective-permute-done((bf16[256,640]{1,0:T(8,128)(2,1)}, bf16[256,640]{1,0:T(8,128)(2,1)S(1)}, u32[]{:S(2)}, u32[]{:S(2)}) %collective-permute-start.36) | collective-permute-done | bytes 327712 | tf_op jit(solution)/shard_map/ppermute | solution.py:578
  299.0 3.8 collective-permute-done.38
  302.9 4.1 %collective-permute-start.39 = (bf16[256,640]{1,0:T(8,128)(2,1)S(1)}, bf16[256,640]{1,0:T(8,128)(2,1)S(1)}, u32[]{:S(2)}, u32[]{:S(2)}) collective-permute-start(bf16[256,640]{1,0:T(8,128)(2,1)S(1)} %get-tuple-element.170), channel_id=1, source_target_pairs={{0,2},{1,3},{2,0},{3,1},{4,6},{5,7},{6,4},{7,5},{8,10},{9,11},{10,... | collective-permute-start | bytes 983048 | tf_op jit(solution)/shard_map/ppermute | solution.py:578
  308.4 2.8 collective-permute-start.35
  312.2 24.4 %collective-permute-done.39 = bf16[256,640]{1,0:T(8,128)(2,1)S(1)} collective-permute-done((bf16[256,640]{1,0:T(8,128)(2,1)S(1)}, bf16[256,640]{1,0:T(8,128)(2,1)S(1)}, u32[]{:S(2)}, u32[]{:S(2)}) %collective-permute-start.39) | collective-permute-done | bytes 327712 | tf_op jit(solution)/shard_map/ppermute | solution.py:578
  338.2 5.4 %collective-permute-done.37 = bf16[256,640]{1,0:T(8,128)(2,1)S(1)} collective-permute-done((bf16[256,640]{1,0:T(8,128)(2,1)S(1)}, bf16[256,640]{1,0:T(8,128)(2,1)S(1)}, u32[]{:S(2)}, u32[]{:S(2)}) %collective-permute-start.37) | collective-permute-done | bytes 327712 | tf_op jit(solution)/shard_map/ppermute | solution.py:578
  346.3 6.1 %collective-permute-done.35 = bf16[80,3072]{1,0:T(8,128)(2,1)S(1)} collective-permute-done((bf16[80,3072]{1,0:T(8,128)(2,1)S(1)}, bf16[80,3072]{1,0:T(8,128)(2,1)S(1)}, u32[]{:S(2)}, u32[]{:S(2)}) %collective-permute-start.35) | collective-permute-done | bytes 491552 | tf_op jit(solution)/shard_map/ppermute | solution.py:578
  354.5 5.1 %collective-permute-done.32 = bf16[208,640]{1,0:T(8,128)(2,1)S(1)} collective-permute-done((bf16[208,640]{1,0:T(8,128)(2,1)S(1)}, bf16[208,640]{1,0:T(8,128)(2,1)S(1)}, u32[]{:S(2)}, u32[]{:S(2)}) %collective-permute-start.32) | collective-permute-done | bytes 266272 | tf_op jit(solution)/shard_map/ppermute | solution.py:578
  359.7 2.1 collective-permute-start.33
  363.0 9.9 %collective-permute-done.33 = bf16[208,640]{1,0:T(8,128)(2,1)S(1)} collective-permute-done((bf16[208,640]{1,0:T(8,128)(2,1)S(1)}, bf16[208,640]{1,0:T(8,128)(2,1)S(1)}, u32[]{:S(2)}, u32[]{:S(2)}) %collective-permute-start.33) | collective-permute-done | bytes 266272 | tf_op jit(solution)/shard_map/ppermute | solution.py:578
  (278 shorter events, 78.0 us)
Async XLA Ops:
  3.7 9.6 %collective-permute-start = (bf16[208,640]{1,0:T(8,128)(2,1)}, bf16[208,640]{1,0:T(8,128)(2,1)S(1)}, u32[]{:S(2)}, u32[]{:S(2)}) collective-permute-start(bf16[208,640]{1,0:T(8,128)(2,1)} %shard_map.467.refs_0_), channel_id=1, source_target_pairs={{0,16},{4,20},{8,24},{12,28},{16,0},{20,4},{24,8},{28,12},{1,17},{... | collective-permute-start | bytes 798728 | tf_op jit(solution)/shard_map/ppermute | solution.py:635
  15.8 13.5 %collective-permute-start.1 = (bf16[2,208,640]{2,1,0:T(8,128)(2,1)}, bf16[2,208,640]{2,1,0:T(8,128)(2,1)S(1)}, u32[]{:S(2)}, u32[]{:S(2)}) collective-permute-start(bf16[2,208,640]{2,1,0:T(8,128)(2,1)} %shard_map.468.refs_0_), channel_id=1, source_target_pairs={{0,8},{4,12},{8,0},{12,4},{16,24},{20,28},{24,16},{28,20},{1,9},{5... | collective-permute-start | bytes 1597448 | tf_op jit(solution)/shard_map/ppermute | solution.py:665
  32.4 8.8 %collective-permute-start.2 = (bf16[2,2,208,640]{3,2,1,0:T(8,128)(2,1)}, bf16[2,2,208,640]{3,2,1,0:T(8,128)(2,1)S(1)}, u32[]{:S(2)}, u32[]{:S(2)}) collective-permute-start(bf16[2,2,208,640]{3,2,1,0:T(8,128)(2,1)} %shard_map.470.refs_0_), channel_id=1, source_target_pairs={{0,4},{4,0},{8,12},{12,8},{16,20},{20,16},{24,28},{28,24},{1,5},{5... | collective-permute-start | bytes 3194888 | tf_op jit(solution)/shard_map/ppermute | solution.py:665
  37.2 16.5 %collective-permute-start.3 = (bf16[256,640]{1,0:T(8,128)(2,1)S(1)}, bf16[256,640]{1,0:T(8,128)(2,1)S(1)}, u32[]{:S(2)}, u32[]{:S(2)}) collective-permute-start(bf16[256,640]{1,0:T(8,128)(2,1)S(1)} %copy-done.9), channel_id=1, source_target_pairs={{0,8},{4,12},{8,0},{12,4},{16,24},{20,28},{24,16},{28,20},{1,9},{5... | collective-permute-start | bytes 983048 | tf_op jit(solution)/shard_map/ppermute | solution.py:652
  38.6 15.1 %collective-permute-start.4 = (bf16[256,640]{1,0:T(8,128)(2,1)S(1)}, bf16[256,640]{1,0:T(8,128)(2,1)S(1)}, u32[]{:S(2)}, u32[]{:S(2)}) collective-permute-start(bf16[256,640]{1,0:T(8,128)(2,1)S(1)} %copy-done.51), channel_id=1, source_target_pairs={{0,16},{4,20},{8,24},{12,28},{16,0},{20,4},{24,8},{28,12},{1,17},{... | collective-permute-start | bytes 983048 | tf_op jit(solution)/shard_map/ppermute | solution.py:652
  40.1 12.4 %collective-permute-start.5 = (bf16[80,1536]{1,0:T(8,128)(2,1)S(1)}, bf16[80,1536]{1,0:T(8,128)(2,1)S(1)}, u32[]{:S(2)}, u32[]{:S(2)}) collective-permute-start(bf16[80,1536]{1,0:T(8,128)(2,1)S(1)} %copy-done.52), channel_id=1, source_target_pairs={{0,8},{4,12},{8,0},{12,4},{16,24},{20,28},{24,16},{28,20},{1,9},{5... | collective-permute-start | bytes 737288 | tf_op jit(solution)/shard_map/ppermute | solution.py:652
  40.6 13.0 %collective-permute-start.6 = (bf16[80,1536]{1,0:T(8,128)(2,1)S(1)}, bf16[80,1536]{1,0:T(8,128)(2,1)S(1)}, u32[]{:S(2)}, u32[]{:S(2)}) collective-permute-start(bf16[80,1536]{1,0:T(8,128)(2,1)S(1)} %copy-done.53), channel_id=1, source_target_pairs={{0,16},{4,20},{8,24},{12,28},{16,0},{20,4},{24,8},{28,12},{1,17},{... | collective-permute-start | bytes 737288 | tf_op jit(solution)/shard_map/ppermute | solution.py:652
  59.6 24.3 %collective-permute-start.7 = (bf16[3,320,512]{2,1,0:T(8,128)(2,1)}, bf16[3,320,512]{2,1,0:T(8,128)(2,1)S(1)}, u32[]{:S(2)}, u32[]{:S(2)}) collective-permute-start(bf16[3,320,512]{2,1,0:T(8,128)(2,1)} %get-tuple-element.89.refs_8_.own_ref), channel_id=1, source_target_pairs={{0,1},{1,2},{2,3},{4,5},{5,6},{6,7},{8,9},{9,10},{10,11},{12,13},{... | collective-permute-start | bytes 2949128 | tf_op jit(solution)/shard_map/ppermute | solution.py:739
  67.3 33.3 %collective-permute-start.10 = (bf16[2,256,640]{2,1,0:T(8,128)(2,1)}, bf16[2,256,640]{2,1,0:T(8,128)(2,1)S(1)}, u32[]{:S(2)}, u32[]{:S(2)}) collective-permute-start(bf16[2,256,640]{2,1,0:T(8,128)(2,1)} %get-tuple-element.92.refs_2_), channel_id=1, source_target_pairs={{0,8},{4,12},{8,0},{12,4},{16,24},{20,28},{24,16},{28,20},{1,9},{5... | collective-permute-start | bytes 1966088 | tf_op jit(solution)/shard_map/ppermute | solution.py:652
  67.9 32.7 %collective-permute-start.9 = (bf16[2,256,640]{2,1,0:T(8,128)(2,1)}, bf16[2,256,640]{2,1,0:T(8,128)(2,1)S(1)}, u32[]{:S(2)}, u32[]{:S(2)}) collective-permute-start(bf16[2,256,640]{2,1,0:T(8,128)(2,1)} %get-tuple-element.90.refs_0_), channel_id=1, source_target_pairs={{0,16},{4,20},{8,24},{12,28},{16,0},{20,4},{24,8},{28,12},{1,17},{... | collective-permute-start | bytes 1966088 | tf_op jit(solution)/shard_map/ppermute | solution.py:652
  87.0 13.6 %collective-permute-start.8 = (bf16[3,192,512]{2,1,0:T(8,128)(2,1)}, bf16[3,192,512]{2,1,0:T(8,128)(2,1)S(1)}, u32[]{:S(2)}, u32[]{:S(2)}) collective-permute-start(bf16[3,192,512]{2,1,0:T(8,128)(2,1)} %shard_map.475), channel_id=1, source_target_pairs={{1,2},{2,3},{5,6},{6,7},{9,10},{10,11},{13,14},{14,15},{17,18},{18... | collective-permute-start | bytes 1769480 | tf_op jit(solution)/shard_map/ppermute | solution.py:765
  87.7 11.6 %collective-permute-start.11 = (bf16[2,80,1536]{2,1,0:T(8,128)(2,1)S(1)}, bf16[2,80,1536]{2,1,0:T(8,128)(2,1)S(1)}, u32[]{:S(2)}, u32[]{:S(2)}) collective-permute-start(bf16[2,80,1536]{2,1,0:T(8,128)(2,1)S(1)} %copy-done.41), channel_id=1, source_target_pairs={{0,16},{4,20},{8,24},{12,28},{16,0},{20,4},{24,8},{28,12},{1,17},{... | collective-permute-start | bytes 1474568 | tf_op jit(solution)/shard_map/ppermute | solution.py:652
  89.3 11.3 %collective-permute-start.12 = (bf16[2,80,1536]{2,1,0:T(8,128)(2,1)S(1)}, bf16[2,80,1536]{2,1,0:T(8,128)(2,1)S(1)}, u32[]{:S(2)}, u32[]{:S(2)}) collective-permute-start(bf16[2,80,1536]{2,1,0:T(8,128)(2,1)S(1)} %copy-done.42), channel_id=1, source_target_pairs={{0,8},{4,12},{8,0},{12,4},{16,24},{20,28},{24,16},{28,20},{1,9},{5... | collective-permute-start | bytes 1474568 | tf_op jit(solution)/shard_map/ppermute | solution.py:652
  107.2 9.0 %collective-permute-start.13 = (bf16[4,256,640]{2,1,0:T(8,128)(2,1)}, bf16[4,256,640]{2,1,0:T(8,128)(2,1)S(1)}, u32[]{:S(2)}, u32[]{:S(2)}) collective-permute-start(bf16[4,256,640]{2,1,0:T(8,128)(2,1)} %bitcast.147), channel_id=1, source_target_pairs={{0,4},{4,0},{8,12},{12,8},{16,20},{20,16},{24,28},{28,24},{1,5},{5... | collective-permute-start | bytes 3932168 | tf_op jit(solution)/shard_map/ppermute | solution.py:771
  107.2 9.0 %collective-permute-start.14 = (bf16[4,256,640]{2,1,0:T(8,128)(2,1)}, bf16[4,256,640]{2,1,0:T(8,128)(2,1)S(1)}, u32[]{:S(2)}, u32[]{:S(2)}) collective-permute-start(bf16[4,256,640]{2,1,0:T(8,128)(2,1)} %bitcast.149), channel_id=1, source_target_pairs={{0,4},{4,0},{8,12},{12,8},{16,20},{20,16},{24,28},{28,24},{1,5},{5... | collective-permute-start | bytes 3932168 | tf_op jit(solution)/shard_map/ppermute | solution.py:771
  107.7 8.5 %collective-permute-start.15 = (bf16[4,80,1536]{2,1,0:T(8,128)(2,1)}, bf16[4,80,1536]{2,1,0:T(8,128)(2,1)}, u32[]{:S(2)}, u32[]{:S(2)}) collective-permute-start(bf16[4,80,1536]{2,1,0:T(8,128)(2,1)} %bitcast.151), channel_id=1, source_target_pairs={{0,4},{4,0},{8,12},{12,8},{16,20},{20,16},{24,28},{28,24},{1,5},{5... | collective-permute-start | bytes 2949128 | tf_op jit(solution)/shard_map/ppermute | solution.py:771
  107.7 8.5 %collective-permute-start.16 = (bf16[4,80,1536]{2,1,0:T(8,128)(2,1)}, bf16[4,80,1536]{2,1,0:T(8,128)(2,1)}, u32[]{:S(2)}, u32[]{:S(2)}) collective-permute-start(bf16[4,80,1536]{2,1,0:T(8,128)(2,1)} %bitcast.153), channel_id=1, source_target_pairs={{0,4},{4,0},{8,12},{12,8},{16,20},{20,16},{24,28},{28,24},{1,5},{5... | collective-permute-start | bytes 2949128 | tf_op jit(solution)/shard_map/ppermute | solution.py:771
  179.0 14.6 %collective-permute-start.17 = (bf16[4,512,640]{2,1,0:T(8,128)(2,1)}, bf16[4,512,640]{2,1,0:T(8,128)(2,1)S(1)}, u32[]{:S(2)}, u32[]{:S(2)}) collective-permute-start(bf16[4,512,640]{2,1,0:T(8,128)(2,1)} %get-tuple-element.109.refs_0_), channel_id=1, source_target_pairs={{0,4},{4,0},{8,12},{12,8},{16,20},{20,16},{24,28},{28,24},{1,5},{5... | collective-permute-start | bytes 7864328 | tf_op jit(solution)/shard_map/ppermute | solution.py:491
  179.0 10.2 %collective-permute-start.18 = (bf16[4,80,3072]{2,1,0:T(8,128)(2,1)S(1)}, bf16[4,80,3072]{2,1,0:T(8,128)(2,1)S(1)}, u32[]{:S(2)}, u32[]{:S(2)}) collective-permute-start(bf16[4,80,3072]{2,1,0:T(8,128)(2,1)S(1)} %copy-done.74), channel_id=1, source_target_pairs={{0,4},{4,0},{8,12},{12,8},{16,20},{20,16},{24,28},{28,24},{1,5},{5... | collective-permute-start | bytes 5898248 | tf_op jit(solution)/shard_map/ppermute | solution.py:491
  188.6 20.1 %collective-permute-start.19 = (bf16[1,192,512]{2,1,0:T(8,128)(2,1)}, bf16[1,192,512]{2,1,0:T(8,128)(2,1)S(1)}, u32[]{:S(2)}, u32[]{:S(2)}) collective-permute-start(bf16[1,192,512]{2,1,0:T(8,128)(2,1)} %get-tuple-element.116), channel_id=1, source_target_pairs={{2,1},{3,2},{6,5},{7,6},{10,9},{11,10},{14,13},{15,14},{18,17},{19... | collective-permute-start | bytes 589832 | tf_op jit(solution)/shard_map/ppermute | solution.py:1039
  193.0 28.6 %collective-permute-start.22 = (bf16[2,80,3072]{2,1,0:T(8,128)(2,1)}, bf16[2,80,3072]{2,1,0:T(8,128)(2,1)S(1)}, u32[]{:S(2)}, u32[]{:S(2)}) collective-permute-start(bf16[2,80,3072]{2,1,0:T(8,128)(2,1)} %shard_map.482.refs_2_), channel_id=1, source_target_pairs={{0,16},{4,20},{8,24},{12,28},{16,0},{20,4},{24,8},{28,12},{1,17},{... | collective-permute-start | bytes 2949128 | tf_op jit(solution)/shard_map/ppermute | solution.py:549
  197.7 46.1 %collective-permute-start.26 = (bf16[2,512,640]{2,1,0:T(8,128)(2,1)}, bf16[2,512,640]{2,1,0:T(8,128)(2,1)S(1)}, u32[]{:S(2)}, u32[]{:S(2)}) collective-permute-start(bf16[2,512,640]{2,1,0:T(8,128)(2,1)} %shard_map.483.refs_1_), channel_id=1, source_target_pairs={{0,8},{4,12},{8,0},{12,4},{16,24},{20,28},{24,16},{28,20},{1,9},{5... | collective-permute-start | bytes 3932168 | tf_op jit(solution)/shard_map/ppermute | solution.py:549
  207.6 17.2 %collective-permute-start.21 = (bf16[1,192,512]{2,1,0:T(8,128)(2,1)}, bf16[1,192,512]{2,1,0:T(8,128)(2,1)S(1)}, u32[]{:S(2)}, u32[]{:S(2)}) collective-permute-start(bf16[1,192,512]{2,1,0:T(8,128)(2,1)} %get-tuple-element.123), channel_id=1, source_target_pairs={{2,1},{3,2},{6,5},{7,6},{10,9},{11,10},{14,13},{15,14},{18,17},{19... | collective-permute-start | bytes 589832 | tf_op jit(solution)/shard_map/ppermute | solution.py:1039
  211.2 18.1 %collective-permute-start.23 = (bf16[1,320,512]{2,1,0:T(8,128)(2,1)}, bf16[1,320,512]{2,1,0:T(8,128)(2,1)S(1)}, u32[]{:S(2)}, u32[]{:S(2)}) collective-permute-start(bf16[1,320,512]{2,1,0:T(8,128)(2,1)} %shard_map.485.refs_1_), channel_id=1, source_target_pairs={{1,0},{2,1},{3,2},{5,4},{6,5},{7,6},{9,8},{10,9},{11,10},{13,12},{... | collective-permute-start | bytes 983048 | tf_op jit(solution)/shard_map/ppermute | solution.py:1050
  227.4 16.4 %collective-permute-start.25 = (bf16[1,320,512]{2,1,0:T(8,128)(2,1)}, bf16[1,320,512]{2,1,0:T(8,128)(2,1)}, u32[]{:S(2)}, u32[]{:S(2)}) collective-permute-start(bf16[1,320,512]{2,1,0:T(8,128)(2,1)} %shard_map.488.refs_0_), channel_id=1, source_target_pairs={{1,0},{2,1},{3,2},{5,4},{6,5},{7,6},{9,8},{10,9},{11,10},{13,12},{... | collective-permute-start | bytes 983048 | tf_op jit(solution)/shard_map/ppermute | solution.py:1055
  228.7 6.7 %collective-permute-start.20 = (bf16[1,192,512]{2,1,0:T(8,128)(2,1)S(1)}, bf16[1,192,512]{2,1,0:T(8,128)(2,1)S(1)}, u32[]{:S(2)}, u32[]{:S(2)}) collective-permute-start(bf16[1,192,512]{2,1,0:T(8,128)(2,1)S(1)} %copy-done.77), channel_id=1, source_target_pairs={{2,1},{3,2},{6,5},{7,6},{10,9},{11,10},{14,13},{15,14},{18,17},{19... | collective-permute-start | bytes 589832 | tf_op jit(solution)/shard_map/ppermute | solution.py:1039
  247.4 20.4 %collective-permute-start.27 = (bf16[512,640]{1,0:T(8,128)(2,1)}, bf16[512,640]{1,0:T(8,128)(2,1)S(1)}, u32[]{:S(2)}, u32[]{:S(2)}) collective-permute-start(bf16[512,640]{1,0:T(8,128)(2,1)} %bitcast.124), channel_id=1, source_target_pairs={{0,16},{4,20},{8,24},{12,28},{16,0},{20,4},{24,8},{28,12},{1,17},{... | collective-permute-start | bytes 1966088 | tf_op jit(solution)/shard_map/ppermute | solution.py:549
  249.0 18.9 %collective-permute-start.28 = (bf16[80,3072]{1,0:T(8,128)(2,1)S(1)}, bf16[80,3072]{1,0:T(8,128)(2,1)S(1)}, u32[]{:S(2)}, u32[]{:S(2)}) collective-permute-start(bf16[80,3072]{1,0:T(8,128)(2,1)S(1)} %bitcast.131), channel_id=1, source_target_pairs={{0,8},{4,12},{8,0},{12,4},{16,24},{20,28},{24,16},{28,20},{1,9},{5... | collective-permute-start | bytes 1474568 | tf_op jit(solution)/shard_map/ppermute | solution.py:549
  250.3 17.6 %collective-permute-start.24 = (bf16[1,320,512]{2,1,0:T(8,128)(2,1)S(1)}, bf16[1,320,512]{2,1,0:T(8,128)(2,1)S(1)}, u32[]{:S(2)}, u32[]{:S(2)}) collective-permute-start(bf16[1,320,512]{2,1,0:T(8,128)(2,1)S(1)} %copy-done.15), channel_id=1, source_target_pairs={{1,0},{2,1},{3,2},{5,4},{6,5},{7,6},{9,8},{10,9},{11,10},{13,12},{... | collective-permute-start | bytes 983048 | tf_op jit(solution)/shard_map/ppermute | solution.py:1077
  271.5 35.7 %collective-permute-start.34 = (bf16[80,3072]{1,0:T(8,128)(2,1)}, bf16[80,3072]{1,0:T(8,128)(2,1)}, u32[]{:S(2)}, u32[]{:S(2)}) collective-permute-start(bf16[80,3072]{1,0:T(8,128)(2,1)} %bitcast.127), channel_id=1, source_target_pairs={{0,1},{1,0},{2,3},{3,2},{4,5},{5,4},{6,7},{7,6},{8,9},{9,8},{10,11... | collective-permute-start | bytes 1474568 | tf_op jit(solution)/shard_map/ppermute | solution.py:578
  288.1 10.9 %collective-permute-start.36 = (bf16[256,640]{1,0:T(8,128)(2,1)}, bf16[256,640]{1,0:T(8,128)(2,1)S(1)}, u32[]{:S(2)}, u32[]{:S(2)}) collective-permute-start(bf16[256,640]{1,0:T(8,128)(2,1)} %get-tuple-element.173), channel_id=1, source_target_pairs={{0,1},{1,0},{2,3},{3,2},{4,5},{5,4},{6,7},{7,6},{8,9},{9,8},{10,11... | collective-permute-start | bytes 983048 | tf_op jit(solution)/shard_map/ppermute | solution.py:578
  288.1 14.6 %collective-permute-start.38 = (bf16[256,640]{1,0:T(8,128)(2,1)S(1)}, bf16[256,640]{1,0:T(8,128)(2,1)S(1)}, u32[]{:S(2)}, u32[]{:S(2)}) collective-permute-start(bf16[256,640]{1,0:T(8,128)(2,1)S(1)} %get-tuple-element.172), channel_id=1, source_target_pairs={{0,1},{1,0},{2,3},{3,2},{4,5},{5,4},{6,7},{7,6},{8,9},{9,8},{10,11... | collective-permute-start | bytes 983048 | tf_op jit(solution)/shard_map/ppermute | solution.py:578
  292.6 18.6 %collective-permute-start.29 = (bf16[2,2,208,640]{3,2,1,0:T(8,128)(2,1)S(1)}, bf16[2,2,208,640]{3,2,1,0:T(8,128)(2,1)S(1)}, u32[]{:S(2)}, u32[]{:S(2)}) collective-permute-start(bf16[2,2,208,640]{3,2,1,0:T(8,128)(2,1)S(1)} %pad_maximum_fusion), channel_id=1, source_target_pairs={{0,4},{4,0},{8,12},{12,8},{16,20},{20,16},{24,28},{28,24},{1,5},{5... | collective-permute-start | bytes 3194888 | tf_op jit(solution)/shard_map/ppermute | solution.py:549
  292.9 14.3 %copy-start.6 = (bf16[1,80,3072]{2,1,0:T(8,128)(2,1)S(1)}, bf16[1,80,3072]{2,1,0:T(8,128)(2,1)}, u32[]{:S(2)}) copy-start(bf16[1,80,3072]{2,1,0:T(8,128)(2,1)} %shard_map.494) | copy-start | bytes 1474564
  292.9 18.3 %copy-start.20 = (bf16[2,128,640]{2,1,0:T(8,128)(2,1)S(1)}, bf16[2,128,640]{2,1,0:T(8,128)(2,1)}, u32[]{:S(2)}) copy-start(bf16[2,128,640]{2,1,0:T(8,128)(2,1)} %dynamic-slice_bitcast_fusion.1) | copy-start | bytes 983044
  302.9 33.7 %collective-permute-start.39 = (bf16[256,640]{1,0:T(8,128)(2,1)S(1)}, bf16[256,640]{1,0:T(8,128)(2,1)S(1)}, u32[]{:S(2)}, u32[]{:S(2)}) collective-permute-start(bf16[256,640]{1,0:T(8,128)(2,1)S(1)} %get-tuple-element.170), channel_id=1, source_target_pairs={{0,2},{1,3},{2,0},{3,1},{4,6},{5,7},{6,4},{7,5},{8,10},{9,11},{10,... | collective-permute-start | bytes 983048 | tf_op jit(solution)/shard_map/ppermute | solution.py:578
  307.0 29.5 %copy-start.11 = (f32[256,640]{1,0:T(8,128)S(1)}, f32[256,640]{1,0:T(8,128)}, u32[]{:S(2)}) copy-start(f32[256,640]{1,0:T(8,128)} %wu_ref.1) | copy-start | bytes 1966084
  307.0 29.5 %copy-start.28 = (f32[256,640]{1,0:T(8,128)S(1)}, f32[256,640]{1,0:T(8,128)}, u32[]{:S(2)}) copy-start(f32[256,640]{1,0:T(8,128)} %param.53) | copy-start | bytes 1966084
  307.0 29.5 %copy-start.29 = (f32[256,640]{1,0:T(8,128)S(1)}, f32[256,640]{1,0:T(8,128)}, u32[]{:S(2)}) copy-start(f32[256,640]{1,0:T(8,128)} %param.45) | copy-start | bytes 1966084
  307.0 36.5 %collective-permute-start.37 = (bf16[256,640]{1,0:T(8,128)(2,1)S(1)}, bf16[256,640]{1,0:T(8,128)(2,1)S(1)}, u32[]{:S(2)}, u32[]{:S(2)}) collective-permute-start(bf16[256,640]{1,0:T(8,128)(2,1)S(1)} %get-tuple-element.171), channel_id=1, source_target_pairs={{0,2},{1,3},{2,0},{3,1},{4,6},{5,7},{6,4},{7,5},{8,10},{9,11},{10,... | collective-permute-start | bytes 983048 | tf_op jit(solution)/shard_map/ppermute | solution.py:578
  308.4 44.0 %collective-permute-start.35 = (bf16[80,3072]{1,0:T(8,128)(2,1)S(1)}, bf16[80,3072]{1,0:T(8,128)(2,1)S(1)}, u32[]{:S(2)}, u32[]{:S(2)}) collective-permute-start(bf16[80,3072]{1,0:T(8,128)(2,1)S(1)} %add_convert_fusion), channel_id=1, source_target_pairs={{0,2},{1,3},{2,0},{3,1},{4,6},{5,7},{6,4},{7,5},{8,10},{9,11},{10,... | collective-permute-start | bytes 1474568 | tf_op jit(solution)/shard_map/ppermute | solution.py:578
  311.3 32.3 %copy-start.12 = (f32[256,640]{1,0:T(8,128)S(1)}, f32[256,640]{1,0:T(8,128)}, u32[]{:S(2)}) copy-start(f32[256,640]{1,0:T(8,128)} %wg_ref.1) | copy-start | bytes 1966084
  311.4 32.2 %copy-start.30 = (f32[256,640]{1,0:T(8,128)S(1)}, f32[256,640]{1,0:T(8,128)}, u32[]{:S(2)}) copy-start(f32[256,640]{1,0:T(8,128)} %param.52) | copy-start | bytes 1966084
  311.4 32.2 %copy-start.31 = (f32[256,640]{1,0:T(8,128)S(1)}, f32[256,640]{1,0:T(8,128)}, u32[]{:S(2)}) copy-start(f32[256,640]{1,0:T(8,128)} %param.44) | copy-start | bytes 1966084
  311.4 33.9 %collective-permute-start.30 = (bf16[2,208,640]{2,1,0:T(8,128)(2,1)S(1)}, bf16[2,208,640]{2,1,0:T(8,128)(2,1)S(1)}, u32[]{:S(2)}, u32[]{:S(2)}) collective-permute-start(bf16[2,208,640]{2,1,0:T(8,128)(2,1)S(1)} %fusion.1), channel_id=1, source_target_pairs={{0,16},{4,20},{8,24},{12,28},{16,0},{20,4},{24,8},{28,12},{1,17},{... | collective-permute-start | bytes 1597448 | tf_op jit(solution)/shard_map/ppermute | solution.py:549
  345.4 7.2 %collective-permute-start.31 = (bf16[208,640]{1,0:T(8,128)(2,1)S(1)}, bf16[208,640]{1,0:T(8,128)(2,1)S(1)}, u32[]{:S(2)}, u32[]{:S(2)}) collective-permute-start(bf16[208,640]{1,0:T(8,128)(2,1)S(1)} %fusion.5), channel_id=1, source_target_pairs={{0,8},{4,12},{8,0},{12,4},{16,24},{20,28},{24,16},{28,20},{1,9},{5... | collective-permute-start | bytes 798728 | tf_op jit(solution)/shard_map/ppermute | solution.py:549
  352.8 6.8 %collective-permute-start.32 = (bf16[208,640]{1,0:T(8,128)(2,1)S(1)}, bf16[208,640]{1,0:T(8,128)(2,1)S(1)}, u32[]{:S(2)}, u32[]{:S(2)}) collective-permute-start(bf16[208,640]{1,0:T(8,128)(2,1)S(1)} %fusion.7), channel_id=1, source_target_pairs={{0,1},{1,0},{2,3},{3,2},{4,5},{5,4},{6,7},{7,6},{8,9},{9,8},{10,11... | collective-permute-start | bytes 798728 | tf_op jit(solution)/shard_map/ppermute | solution.py:578
  359.7 13.1 %collective-permute-start.33 = (bf16[208,640]{1,0:T(8,128)(2,1)S(1)}, bf16[208,640]{1,0:T(8,128)(2,1)S(1)}, u32[]{:S(2)}, u32[]{:S(2)}) collective-permute-start(bf16[208,640]{1,0:T(8,128)(2,1)S(1)} %add_convert_fusion.3), channel_id=1, source_target_pairs={{0,2},{1,3},{2,0},{3,1},{4,6},{5,7},{6,4},{7,5},{8,10},{9,11},{10,... | collective-permute-start | bytes 798728 | tf_op jit(solution)/shard_map/ppermute | solution.py:578
  (70 other events, 344.7 us)

commit v5 on v3

--- a/solution.py
+++ b/solution.py
@@ -261,14 +261,14 @@
         bias = mask_bias(qid_ref, kid_ref, t, part, span)
         keys = win_ref[t * part : t * part + span, :size]
         values = win_ref[t * part : t * part + span, size:]
+        scores = dot_nt(q_ref[0, t], keys).reshape(heads, part, span)
+        weights = jnp.exp(scores + bias[None]).reshape(heads * part, span)
+        total = jnp.sum(weights, axis=-1, keepdims=True)
+        mixed = (dot_nn(weights.astype(jnp.bfloat16), values) / total).astype(jnp.bfloat16)
         for head in range(heads):
-            scores = dot_nt(q_ref[0, t, head * part : (head + 1) * part, :], keys)
-            weights = jnp.exp(scores + bias)
-            total = jnp.sum(weights, axis=-1, keepdims=True)
-            mixed = dot_nn(weights.astype(jnp.bfloat16), values) / total
-            mixed_ref[0, t * part : (t + 1) * part, head * size : (head + 1) * size] = (
-                mixed.astype(jnp.bfloat16)
-            )
+            mixed_ref[0, t * part : (t + 1) * part, head * size : (head + 1) * size] = mixed[
+                head * part : (head + 1) * part
+            ]
 
 
 def middle_kernel(
@@ -390,30 +390,33 @@
         keys = win_ref[window, :size]
         values = win_ref[window, size:]
         cosine, sine = cos_ref[0, rows, :], sin_ref[0, rows, :]
+        query = q_ref[0, t]
+        d_out = dmix_ref[0, t]
+        scores = dot_nt(query, keys).reshape(heads, part, span)
+        weights = jnp.exp(scores + bias[None]).reshape(heads * part, span)
+        weights = weights * (1.0 / jnp.sum(weights, axis=-1, keepdims=True))
+        mixed = jnp.concatenate(
+            [mixed_ref[0, rows, head * size : (head + 1) * size] for head in range(heads)], axis=0
+        )
+        delta = jnp.sum(
+            d_out.astype(jnp.float32) * mixed.astype(jnp.float32), axis=-1, keepdims=True
+        )
+        d_scores = (weights * (dot_nt(d_out, values) - delta)).astype(jnp.bfloat16)
+        weights = weights.astype(jnp.bfloat16)
+        grad_ref[window, :size] += dot_tn(d_scores, query)
+        grad_ref[window, size:] += dot_tn(weights, d_out)
+        d_query = dot_nn(d_scores, keys) * size ** (-0.5)
+        d_raw, part_g = rms_back(
+            qraw_ref[0, t].astype(jnp.float32),
+            gq_ref[...],
+            turn(d_query, stack_heads(cosine, heads), -stack_heads(sine, heads)),
+        )
+        d_raw = d_raw.astype(jnp.bfloat16)
         for head in range(heads):
-            line = slice(head * part, (head + 1) * part)
-            lanes = slice(head * size, (head + 1) * size)
-            query = q_ref[0, t, line, :]
-            d_out = dmix_ref[0, t, line, :]
-            weights = jnp.exp(dot_nt(query, keys) + bias)
-            weights = weights * (1.0 / jnp.sum(weights, axis=-1, keepdims=True))
-            delta = jnp.sum(
-                d_out.astype(jnp.float32) * mixed_ref[0, rows, lanes].astype(jnp.float32),
-                axis=-1,
-                keepdims=True,
-            )
-            d_scores = (weights * (dot_nt(d_out, values) - delta)).astype(jnp.bfloat16)
-            weights = weights.astype(jnp.bfloat16)
-            grad_ref[window, :size] += dot_tn(d_scores, query)
-            grad_ref[window, size:] += dot_tn(weights, d_out)
-            d_query = dot_nn(d_scores, keys) * size ** (-0.5)
-            d_raw, part_g = rms_back(
-                qraw_ref[0, t, line, :].astype(jnp.float32),
-                gq_ref[...],
-                turn(d_query, cosine, -sine),
-            )
-            dqraw_ref[0, rows, lanes] = d_raw.astype(jnp.bfloat16)
-            dg += part_g
+            dqraw_ref[0, rows, head * size : (head + 1) * size] = d_raw[
+                head * part : (head + 1) * part
+            ]
+        dg += part_g
     dg_ref[0] = dg
     dfar_ref[0] = grad_ref[:far, :].astype(jnp.bfloat16)
     dnear_ref[0] = grad_ref[far : far + near, :]

time: 356 us -> 348 us (0.978)
  Pallas kernels: 169 us -> 161 us
    pallas_call x6, Pallas kernels: 41.4 us -> 34.8 us  [seq_call(): pl.pallas_call(kernel, grid=(1,), out_shape=outs, in_specs=in_specs, out_...]
  transfers between devices with their start and end apart: 44 -> 44, of which waited for: 15 -> 16; matrix products, arithmetic and copies ran while one was open for 7% -> 7% of each run, Pallas kernels for 26% -> 25%
where the time goes in v5:
time: 348 us; the launch traced here: 342 us
  Pallas kernels  161 us (46%)
  waiting for transfers between devices  68.2 us (20%)
  starting transfers between devices  66.5 us (19%)
  local copies, waits for them, and re-layouts  27.2 us (8%)
  other arithmetic  14.1 us (4%)
    pallas_call x1, Pallas kernels, body(): call(functools.partial(middle_kernel, heads, 512), [array((seqs, rows, wi...  38.1 us
    pallas_call x6, Pallas kernels, seq_call(): pl.pallas_call(kernel, grid=(1,), out_shape=outs, in_specs=in_specs, out_...  34.8 us
    ppermute x4, starting transfers between devices, seq_sum(): terms.append(lax.ppermute(total().astype(jnp.bfloat16), 'seq', pairs))  27.2 us
    ppermute x4, waiting for transfers between devices, seq_sum(): received = lax.ppermute(result.astype(jnp.bfloat16), 'seq', pairs)  20.4 us
    pallas_call x6, Pallas kernels, ordered_total(): pl.pallas_call(functools.partial(sum_kernel, len(terms)), out_shape=jax.S...  15.3 us
    ppermute x8, waiting for transfers between devices, rest_step(): lax.ppermute(own, 'dp', flips(order[i]))  15 us
    pallas_call x5, Pallas kernels, stack_step(): pl.pallas_call(functools.partial(stack_kernel, bits, axes, len(arrived)),...  15 us
    unnamed x143, local copies, waits for them, and re-layouts  14.9 us
  transfers between devices with their start and end apart: 44, of which 16 were waited for; matrix products, arithmetic and copies ran while one was open for 7% of the time, Pallas kernels for 25%

profile of v5, /device:TPU:0, one launch (start us, length us, event | category | flops | bytes accessed | tf_op | source)
XLA Modules:
  0.0 342.1 jit_solution(649177288031798446)
XLA Ops:
  3.7 3.0 collective-permute-start
  6.6 6.6 %collective-permute-done.refs_1_.refs_0_ = bf16[208,640]{1,0:T(8,128)(2,1)S(1)} collective-permute-done((bf16[208,640]{1,0:T(8,128)(2,1)}, bf16[208,640]{1,0:T(8,128)(2,1)S(1)}, u32[]{:S(2)}, u32[]{:S(2)}) %collective-permute-start) | collective-permute-done | bytes 266272 | tf_op jit(solution)/shard_map/ppermute | solution.py:649
  13.9 1.9 shard_map.468.refs_0_
  17.5 2.6 shard_map.469
  20.1 9.2 %collective-permute-done.1.refs_1_ = bf16[2,208,640]{2,1,0:T(8,128)(2,1)S(1)} collective-permute-done((bf16[2,208,640]{2,1,0:T(8,128)(2,1)}, bf16[2,208,640]{2,1,0:T(8,128)(2,1)S(1)}, u32[]{:S(2)}, u32[]{:S(2)}) %collective-permute-start.1) | collective-permute-done | bytes 532512 | tf_op jit(solution)/shard_map/ppermute | solution.py:679
  30.1 2.3 shard_map.470.refs_0_
  34.4 2.8 multiply_sine_fusion
  42.2 3.0 shard_map.471
  47.3 2.0 fusion.31
  49.2 3.3 collective-permute-done.5.refs_4_.refs_5_
  54.5 5.0 %shard_map.472 = (bf16[3,320,640]{2,1,0:T(8,128)(2,1)}, bf16[3,320,512]{2,1,0:T(8,128)(2,1)}, bf16[3,320,256]{2,1,0:T(8,128)(2,1)}) custom-call(bf16[3,320,640]{2,1,0:T(8,128)(2,1)} %x_ref.9, f32[3,320,128]{2,1,0:T(8,128)} %get-tuple-element.193.cos_ref, f32[3,320,128]{2,1,0:T(8,128)} %get-tuple-element.192.sin_ref, bf16[256,640]{1,0:T(8,128)(2,1)} %bitcast.136, ...), custom_call_target="tpu_custom_call" | custom-call | flops 629145600 | bytes 6000000 | tf_op jit(solution)/shard_map/pallas_call | solution.py:728
  59.6 3.5 %collective-permute-start.7 = (bf16[3,320,512]{2,1,0:T(8,128)(2,1)}, bf16[3,320,512]{2,1,0:T(8,128)(2,1)S(1)}, u32[]{:S(2)}, u32[]{:S(2)}) collective-permute-start(bf16[3,320,512]{2,1,0:T(8,128)(2,1)} %get-tuple-element.89.refs_8_.own_ref), channel_id=1, source_target_pairs={{0,1},{1,2},{2,3},{4,5},{5,6},{6,7},{8,9},{9,10},{10,11},{12,13},{... | collective-permute-start | bytes 2949128 | tf_op jit(solution)/shard_map/ppermute | solution.py:753
  64.3 3.0 shard_map.473
  69.4 5.7 %shard_map.474 = (bf16[3,2,640,256]{3,2,1,0:T(8,128)(2,1)}, bf16[3,2,640,256]{3,2,1,0:T(8,128)(2,1)}) custom-call(bf16[3,320,640]{2,1,0:T(8,128)(2,1)} %get-tuple-element.88.normed_ref, f32[3,320,128]{2,1,0:T(8,128)} %get-tuple-element.193.cos_ref, f32[3,320,128]{2,1,0:T(8,128)} %get-tuple-element.192.sin_ref, bf16[1024,640]{1,0:T(8,128)(2,1)} %bitcast.123, ...), custom_call_target="tpu_custom_call" | custom-call | flops 1258291200 | bytes 8000000 | tf_op jit(solution)/shard_map/pallas_call | solution.py:755
  75.1 8.8 %collective-permute-done.7.near_ref = bf16[3,320,512]{2,1,0:T(8,128)(2,1)S(1)} collective-permute-done((bf16[3,320,512]{2,1,0:T(8,128)(2,1)}, bf16[3,320,512]{2,1,0:T(8,128)(2,1)S(1)}, u32[]{:S(2)}, u32[]{:S(2)}) %collective-permute-start.7) | collective-permute-done | bytes 983072 | tf_op jit(solution)/shard_map/ppermute | solution.py:753
  84.8 2.1 shard_map.475
  90.0 9.4 %collective-permute-done.11.refs_5_ = bf16[2,80,1536]{2,1,0:T(8,128)(2,1)S(1)} collective-permute-done((bf16[2,80,1536]{2,1,0:T(8,128)(2,1)S(1)}, bf16[2,80,1536]{2,1,0:T(8,128)(2,1)S(1)}, u32[]{:S(2)}, u32[]{:S(2)}) %collective-permute-start.11) | collective-permute-done | bytes 491552 | tf_op jit(solution)/shard_map/ppermute | solution.py:666
  102.6 4.7 %shard_map.477 = (bf16[2,2,256,640]{3,2,1,0:T(8,128)(2,1)}, bf16[2,2,256,640]{3,2,1,0:T(8,128)(2,1)}, bf16[2,2,80,1536]{3,2,1,0:T(8,128)(2,1)}, bf16[2,2,80,1536]{3,2,1,0:T(8,128)(2,1)}) custom-call(s32[1]{0:T(128)} %bitcast.1.index_ref, bf16[2,256,640]{2,1,0:T(8,128)(2,1)} %get-tuple-element.90.refs_0_, bf16[2,256,640]{2,1,0:T(8,128)(2,1)} %copy-done.31, ...), custom_call_target="tpu_custom_call" | custom-call | tf_op jit(solution)/shard_map/pallas_call | solution.py:467
  108.3 6.8 %shard_map.476.mixed_ref = bf16[3,320,1024]{2,1,0:T(8,128)(2,1)} custom-call(bf16[3,2,640,256]{3,2,1,0:T(8,128)(2,1)} %get-tuple-element.91.refs_0_.q_ref, bf16[3,192,512]{2,1,0:T(8,128)(2,1)} %copy-done.32, bf16[3,320,512]{2,1,0:T(8,128)(2,1)} %copy-done.19, bf16[3,320,512]{2,1,0:T(8,128)(2,1)} %get-tuple-element.89.refs_8_.own_ref, ...), custom_call_target="tpu_custom_call" | custom-call | flops 5284823040 | bytes 16000000 | tf_op jit(solution)/shard_map/pallas_call | solution.py:796
  116.9 38.1 %shard_map.478 = (bf16[3,320,640]{2,1,0:T(8,128)(2,1)}, bf16[3,320,640]{2,1,0:T(8,128)(2,1)}, bf16[3,320,2048]{2,1,0:T(8,128)(2,1)}, bf16[3,320,640]{2,1,0:T(8,1...) custom-call(s32[1]{0:T(128)} %bitcast.side_ref, ...), custom_call_target="tpu_custom_call" | custom-call | flops 17616076800 | bytes 40000000 | tf_op jit(solution)/shard_map/pallas_call | solution.py:817
  155.0 10.3 %shard_map.479 = (bf16[4,80,3072]{2,1,0:T(8,128)(2,1)}, bf16[4,80,3072]{2,1,0:T(8,128)(2,1)}) custom-call(s32[1]{0:T(128)} %bitcast.side_ref, bf16[960,2048]{1,0:T(8,128)(2,1)} %bitcast.172, bf16[960,1024]{1,0:T(8,128)(2,1)} %bitcast.173, bf16[960,640]{1,0:T(8,128)(2,1)} %bitcast.175, bf16[960,640]{1,0:T(8,128)(2,1)} %bitcast.176), custom_call_target="tpu_custom_call" | custom-call | flops 3774873600 | bytes 13000000 | tf_op jit(solution)/shard_map/pallas_call | solution.py:895
  165.3 12.8 %shard_map.480 = (bf16[4,512,640]{2,1,0:T(8,128)(2,1)}, bf16[4,512,640]{2,1,0:T(8,128)(2,1)}) custom-call(s32[1]{0:T(128)} %bitcast.side_ref, bf16[960,2048]{1,0:T(8,128)(2,1)} %bitcast.170, bf16[960,2048]{1,0:T(8,128)(2,1)} %bitcast.171, bf16[960,640]{1,0:T(8,128)(2,1)} %bitcast.174, bf16[4,80,3072]{2,1,0:T(8,128)(2,1)} %get-tuple-element.108.after_ref), custom_call_target="tpu_custom_call" | custom-call | flops 5033164800 | bytes 14000000 | tf_op jit(solution)/shard_map/pallas_call | solution.py:931
  178.6 6.9 %shard_map.481 = (bf16[1,192,512]{2,1,0:T(8,128)(2,1)}, f32[1,320,512]{2,1,0:T(8,128)}, f32[1,320,512]{2,1,0:T(8,128)}, bf16[3,320,1024]{2,1,0:T(8,128)(2,1)}, f32[1,1,256]{2,1,0:T(1,128)}) custom-call(bf16[3,2,640,256]{3,2,1,0:T(8,128)(2,1)} %get-tuple-element.91.refs_0_.q_ref, bf16[3,2,640,256]{3,2,1,0:T(8,128)(2,1)} %get-tuple-element.100.qraw_ref, ...), custom_call_target="tpu_custom_call" | custom-call | flops 5284823040 | bytes 8000000 | tf_op jit(solution)/shard_map/pallas_call | solution.py:970
  186.3 2.4 shard_map.482.refs_2_
  190.7 2.7 shard_map.483.refs_1_
  194.2 6.9 %shard_map.484 = (bf16[1,192,512]{2,1,0:T(8,128)(2,1)}, f32[1,320,512]{2,1,0:T(8,128)}, f32[1,320,512]{2,1,0:T(8,128)}, bf16[3,320,1024]{2,1,0:T(8,128)(2,1)}, f32[1,1,256]{2,1,0:T(1,128)}) custom-call(bf16[3,2,640,256]{3,2,1,0:T(8,128)(2,1)} %get-tuple-element.91.refs_0_.q_ref, ...), custom_call_target="tpu_custom_call", output_to_operand_aliasing={{3}: (12, {})} | custom-call | flops 5284823040 | bytes 8000000 | tf_op jit(solution)/shard_map/pallas_call | solution.py:970
  202.4 1.9 shard_map.485.refs_1_
  206.1 6.9 %shard_map.486 = (bf16[1,192,512]{2,1,0:T(8,128)(2,1)}, f32[1,320,512]{2,1,0:T(8,128)}, f32[1,320,512]{2,1,0:T(8,128)}, bf16[3,320,1024]{2,1,0:T(8,128)(2,1)}, f32[1,1,256]{2,1,0:T(1,128)}) custom-call(bf16[3,2,640,256]{3,2,1,0:T(8,128)(2,1)} %get-tuple-element.91.refs_0_.q_ref, ...), custom_call_target="tpu_custom_call", output_to_operand_aliasing={{3}: (12, {})} | custom-call | flops 5284823040 | bytes 8000000 | tf_op jit(solution)/shard_map/pallas_call | solution.py:970
  214.3 2.3 shard_map.487
  218.5 1.9 shard_map.488.refs_0_
  221.7 5.2 %shard_map.489.refs_0_ = bf16[1024,640]{1,0:T(8,128)(2,1)} custom-call(bf16[960,1024]{1,0:T(8,128)(2,1)} %bitcast.122, bf16[960,640]{1,0:T(8,128)(2,1)} %bitcast.155, bf16[1,320,512]{2,1,0:T(8,128)(2,1)} %shard_map.488.refs_0_, bf16[80,3072]{1,0:T(8,128)(2,1)} %bitcast.148), custom_call_target="tpu_custom_call" | custom-call | flops 1258291200 | bytes 5000000 | tf_op jit(solution)/shard_map/pallas_call | solution.py:1069
  227.6 1.9 shard_map.490.refs_3_
  233.4 2.6 shard_map.491
  237.5 4.7 %shard_map.492 = (f32[3,320,640]{2,1,0:T(8,128)}, bf16[3,320,512]{2,1,0:T(8,128)(2,1)}, f32[1,1,640]{2,1,0:T(1,128)}, f32[1,1,256]{2,1,0:T(1,128)}) custom-call(f32[1,320,512]{2,1,0:T(8,128)} %get-tuple-element.113.refs_2_.own_ref, bf16[1,320,512]{2,1,0:T(8,128)(2,1)} %collective-permute-done.25.recv_ref, bf16[3,320,256]{2,1,0:T(8,128)(2,1)} %get-tuple-element.124.kraw_ref, ...), custom_call_target="tpu_custom_call" | custom-call | flops 629145600 | bytes 8000000 | tf_op jit(solution)/shard_map/pallas_call | solution.py:970
  242.2 4.7 %shard_map.493 = (f32[3,320,640]{2,1,0:T(8,128)}, bf16[3,320,512]{2,1,0:T(8,128)(2,1)}, f32[1,1,640]{2,1,0:T(1,128)}, f32[1,1,256]{2,1,0:T(1,128)}) custom-call(f32[1,320,512]{2,1,0:T(8,128)} %get-tuple-element.117.refs_0_.own_ref, bf16[1,320,512]{2,1,0:T(8,128)(2,1)} %collective-permute-done.24.recv_ref, ...), custom_call_target="tpu_custom_call", output_to_operand_aliasing={{0}: (13, {}), {1}: (14, {})} | custom-call | flops 629145600 | bytes 8000000 | tf_op jit(solution)/shard_map/pallas_call | solution.py:970
  246.9 2.5 shard_map.494
  249.4 10.6 %collective-permute-start.34 = (bf16[80,3072]{1,0:T(8,128)(2,1)}, bf16[80,3072]{1,0:T(8,128)(2,1)S(1)}, u32[]{:S(2)}, u32[]{:S(2)}) collective-permute-start(bf16[80,3072]{1,0:T(8,128)(2,1)} %bitcast.127), channel_id=1, source_target_pairs={{0,1},{3,2},{4,5},{7,6},{8,9},{11,10},{12,13},{15,14},{16,17},{19,... | collective-permute-start | bytes 1474568 | tf_op jit(solution)/shard_map/ppermute | solution.py:586
  260.7 4.8 %shard_map.495 = (f32[3,320,640]{2,1,0:T(8,128)}, bf16[3,320,512]{2,1,0:T(8,128)(2,1)}, f32[1,1,640]{2,1,0:T(1,128)}, f32[1,1,256]{2,1,0:T(1,128)}) custom-call(f32[1,320,512]{2,1,0:T(8,128)} %get-tuple-element.118.refs_3_.own_ref, bf16[1,320,512]{2,1,0:T(8,128)(2,1)} %copy-done.38, ...), custom_call_target="tpu_custom_call", output_to_operand_aliasing={{0}: (13, {}), {1}: (14, {})} | custom-call | flops 629145600 | bytes 8000000 | tf_op jit(solution)/shard_map/pallas_call | solution.py:970
  265.6 3.1 fusion
  272.6 2.8 shard_map.496
  276.7 8.1 %collective-permute-start.41 = (bf16[256,640]{1,0:T(8,128)(2,1)S(1)}, bf16[256,640]{1,0:T(8,128)(2,1)S(1)}, u32[]{:S(2)}, u32[]{:S(2)}) collective-permute-start(bf16[256,640]{1,0:T(8,128)(2,1)S(1)} %get-tuple-element.171), channel_id=1, source_target_pairs={{0,1},{3,2},{4,5},{7,6},{8,9},{11,10},{12,13},{15,14},{16,17},{19,... | collective-permute-start | bytes 983048 | tf_op jit(solution)/shard_map/ppermute | solution.py:586
  284.9 4.8 %collective-permute-done.41 = bf16[256,640]{1,0:T(8,128)(2,1)S(1)} collective-permute-done((bf16[256,640]{1,0:T(8,128)(2,1)S(1)}, bf16[256,640]{1,0:T(8,128)(2,1)S(1)}, u32[]{:S(2)}, u32[]{:S(2)}) %collective-permute-start.41) | collective-permute-done | bytes 327712 | tf_op jit(solution)/shard_map/ppermute | solution.py:586
  292.1 6.0 %collective-permute-start.38 = (bf16[256,640]{1,0:T(8,128)(2,1)S(1)}, bf16[256,640]{1,0:T(8,128)(2,1)S(1)}, u32[]{:S(2)}, u32[]{:S(2)}) collective-permute-start(bf16[256,640]{1,0:T(8,128)(2,1)S(1)} %get-tuple-element.172), channel_id=1, source_target_pairs={{0,1},{3,2},{4,5},{7,6},{8,9},{11,10},{12,13},{15,14},{16,17},{19,... | collective-permute-start | bytes 983048 | tf_op jit(solution)/shard_map/ppermute | solution.py:586
  300.4 7.4 %collective-permute-done.36 = bf16[80,3072]{1,0:T(8,128)(2,1)S(1)} collective-permute-done((bf16[80,3072]{1,0:T(8,128)(2,1)S(1)}, bf16[80,3072]{1,0:T(8,128)(2,1)S(1)}, u32[]{:S(2)}, u32[]{:S(2)}) %collective-permute-start.36) | collective-permute-done | bytes 491552 | tf_op jit(solution)/shard_map/ppermute | solution.py:592
  311.4 1.8 multiply_subtract_fusion.1
  315.7 2.6 collective-permute-start.31
  325.7 3.5 %collective-permute-done.40 = bf16[256,640]{1,0:T(8,128)(2,1)S(1)} collective-permute-done((bf16[256,640]{1,0:T(8,128)(2,1)S(1)}, bf16[256,640]{1,0:T(8,128)(2,1)S(1)}, u32[]{:S(2)}, u32[]{:S(2)}) %collective-permute-start.40) | collective-permute-done | bytes 327712 | tf_op jit(solution)/shard_map/ppermute | solution.py:592
  330.9 8.1 %collective-permute-done.33 = bf16[208,640]{1,0:T(8,128)(2,1)S(1)} collective-permute-done((bf16[208,640]{1,0:T(8,128)(2,1)S(1)}, bf16[208,640]{1,0:T(8,128)(2,1)S(1)}, u32[]{:S(2)}, u32[]{:S(2)}) %collective-permute-start.33) | collective-permute-done | bytes 266272 | tf_op jit(solution)/shard_map/ppermute | solution.py:592
  (271 shorter events, 76.5 us)
Async XLA Ops:
  3.7 9.6 %collective-permute-start = (bf16[208,640]{1,0:T(8,128)(2,1)}, bf16[208,640]{1,0:T(8,128)(2,1)S(1)}, u32[]{:S(2)}, u32[]{:S(2)}) collective-permute-start(bf16[208,640]{1,0:T(8,128)(2,1)} %shard_map.467.refs_0_), channel_id=1, source_target_pairs={{0,16},{4,20},{8,24},{12,28},{16,0},{20,4},{24,8},{28,12},{1,17},{... | collective-permute-start | bytes 798728 | tf_op jit(solution)/shard_map/ppermute | solution.py:649
  15.8 13.5 %collective-permute-start.1 = (bf16[2,208,640]{2,1,0:T(8,128)(2,1)}, bf16[2,208,640]{2,1,0:T(8,128)(2,1)S(1)}, u32[]{:S(2)}, u32[]{:S(2)}) collective-permute-start(bf16[2,208,640]{2,1,0:T(8,128)(2,1)} %shard_map.468.refs_0_), channel_id=1, source_target_pairs={{0,8},{4,12},{8,0},{12,4},{16,24},{20,28},{24,16},{28,20},{1,9},{5... | collective-permute-start | bytes 1597448 | tf_op jit(solution)/shard_map/ppermute | solution.py:679
  32.4 8.8 %collective-permute-start.2 = (bf16[2,2,208,640]{3,2,1,0:T(8,128)(2,1)}, bf16[2,2,208,640]{3,2,1,0:T(8,128)(2,1)S(1)}, u32[]{:S(2)}, u32[]{:S(2)}) collective-permute-start(bf16[2,2,208,640]{3,2,1,0:T(8,128)(2,1)} %shard_map.470.refs_0_), channel_id=1, source_target_pairs={{0,4},{4,0},{8,12},{12,8},{16,20},{20,16},{24,28},{28,24},{1,5},{5... | collective-permute-start | bytes 3194888 | tf_op jit(solution)/shard_map/ppermute | solution.py:679
  37.2 16.5 %collective-permute-start.3 = (bf16[256,640]{1,0:T(8,128)(2,1)S(1)}, bf16[256,640]{1,0:T(8,128)(2,1)S(1)}, u32[]{:S(2)}, u32[]{:S(2)}) collective-permute-start(bf16[256,640]{1,0:T(8,128)(2,1)S(1)} %copy-done.7), channel_id=1, source_target_pairs={{0,8},{4,12},{8,0},{12,4},{16,24},{20,28},{24,16},{28,20},{1,9},{5... | collective-permute-start | bytes 983048 | tf_op jit(solution)/shard_map/ppermute | solution.py:666
  38.6 15.1 %collective-permute-start.4 = (bf16[256,640]{1,0:T(8,128)(2,1)S(1)}, bf16[256,640]{1,0:T(8,128)(2,1)S(1)}, u32[]{:S(2)}, u32[]{:S(2)}) collective-permute-start(bf16[256,640]{1,0:T(8,128)(2,1)S(1)} %copy-done.45), channel_id=1, source_target_pairs={{0,16},{4,20},{8,24},{12,28},{16,0},{20,4},{24,8},{28,12},{1,17},{... | collective-permute-start | bytes 983048 | tf_op jit(solution)/shard_map/ppermute | solution.py:666
  40.1 12.4 %collective-permute-start.5 = (bf16[80,1536]{1,0:T(8,128)(2,1)S(1)}, bf16[80,1536]{1,0:T(8,128)(2,1)S(1)}, u32[]{:S(2)}, u32[]{:S(2)}) collective-permute-start(bf16[80,1536]{1,0:T(8,128)(2,1)S(1)} %copy-done.46), channel_id=1, source_target_pairs={{0,8},{4,12},{8,0},{12,4},{16,24},{20,28},{24,16},{28,20},{1,9},{5... | collective-permute-start | bytes 737288 | tf_op jit(solution)/shard_map/ppermute | solution.py:666
  40.6 13.0 %collective-permute-start.6 = (bf16[80,1536]{1,0:T(8,128)(2,1)S(1)}, bf16[80,1536]{1,0:T(8,128)(2,1)S(1)}, u32[]{:S(2)}, u32[]{:S(2)}) collective-permute-start(bf16[80,1536]{1,0:T(8,128)(2,1)S(1)} %copy-done.47), channel_id=1, source_target_pairs={{0,16},{4,20},{8,24},{12,28},{16,0},{20,4},{24,8},{28,12},{1,17},{... | collective-permute-start | bytes 737288 | tf_op jit(solution)/shard_map/ppermute | solution.py:666
  59.6 24.3 %collective-permute-start.7 = (bf16[3,320,512]{2,1,0:T(8,128)(2,1)}, bf16[3,320,512]{2,1,0:T(8,128)(2,1)S(1)}, u32[]{:S(2)}, u32[]{:S(2)}) collective-permute-start(bf16[3,320,512]{2,1,0:T(8,128)(2,1)} %get-tuple-element.89.refs_8_.own_ref), channel_id=1, source_target_pairs={{0,1},{1,2},{2,3},{4,5},{5,6},{6,7},{8,9},{9,10},{10,11},{12,13},{... | collective-permute-start | bytes 2949128 | tf_op jit(solution)/shard_map/ppermute | solution.py:753
  67.4 33.2 %collective-permute-start.10 = (bf16[2,256,640]{2,1,0:T(8,128)(2,1)}, bf16[2,256,640]{2,1,0:T(8,128)(2,1)S(1)}, u32[]{:S(2)}, u32[]{:S(2)}) collective-permute-start(bf16[2,256,640]{2,1,0:T(8,128)(2,1)} %get-tuple-element.92.refs_2_), channel_id=1, source_target_pairs={{0,8},{4,12},{8,0},{12,4},{16,24},{20,28},{24,16},{28,20},{1,9},{5... | collective-permute-start | bytes 1966088 | tf_op jit(solution)/shard_map/ppermute | solution.py:666
  67.9 32.7 %collective-permute-start.9 = (bf16[2,256,640]{2,1,0:T(8,128)(2,1)}, bf16[2,256,640]{2,1,0:T(8,128)(2,1)S(1)}, u32[]{:S(2)}, u32[]{:S(2)}) collective-permute-start(bf16[2,256,640]{2,1,0:T(8,128)(2,1)} %get-tuple-element.90.refs_0_), channel_id=1, source_target_pairs={{0,16},{4,20},{8,24},{12,28},{16,0},{20,4},{24,8},{28,12},{1,17},{... | collective-permute-start | bytes 1966088 | tf_op jit(solution)/shard_map/ppermute | solution.py:666
  87.0 13.6 %collective-permute-start.8 = (bf16[3,192,512]{2,1,0:T(8,128)(2,1)}, bf16[3,192,512]{2,1,0:T(8,128)(2,1)S(1)}, u32[]{:S(2)}, u32[]{:S(2)}) collective-permute-start(bf16[3,192,512]{2,1,0:T(8,128)(2,1)} %shard_map.475), channel_id=1, source_target_pairs={{1,2},{2,3},{5,6},{6,7},{9,10},{10,11},{13,14},{14,15},{17,18},{18... | collective-permute-start | bytes 1769480 | tf_op jit(solution)/shard_map/ppermute | solution.py:779
  87.7 11.6 %collective-permute-start.11 = (bf16[2,80,1536]{2,1,0:T(8,128)(2,1)S(1)}, bf16[2,80,1536]{2,1,0:T(8,128)(2,1)S(1)}, u32[]{:S(2)}, u32[]{:S(2)}) collective-permute-start(bf16[2,80,1536]{2,1,0:T(8,128)(2,1)S(1)} %copy-done.34), channel_id=1, source_target_pairs={{0,16},{4,20},{8,24},{12,28},{16,0},{20,4},{24,8},{28,12},{1,17},{... | collective-permute-start | bytes 1474568 | tf_op jit(solution)/shard_map/ppermute | solution.py:666
  89.3 11.3 %collective-permute-start.12 = (bf16[2,80,1536]{2,1,0:T(8,128)(2,1)S(1)}, bf16[2,80,1536]{2,1,0:T(8,128)(2,1)S(1)}, u32[]{:S(2)}, u32[]{:S(2)}) collective-permute-start(bf16[2,80,1536]{2,1,0:T(8,128)(2,1)S(1)} %copy-done.35), channel_id=1, source_target_pairs={{0,8},{4,12},{8,0},{12,4},{16,24},{20,28},{24,16},{28,20},{1,9},{5... | collective-permute-start | bytes 1474568 | tf_op jit(solution)/shard_map/ppermute | solution.py:666
  107.3 8.1 %collective-permute-start.13 = (bf16[4,256,640]{2,1,0:T(8,128)(2,1)}, bf16[4,256,640]{2,1,0:T(8,128)(2,1)S(1)}, u32[]{:S(2)}, u32[]{:S(2)}) collective-permute-start(bf16[4,256,640]{2,1,0:T(8,128)(2,1)} %bitcast.162), channel_id=1, source_target_pairs={{0,4},{4,0},{8,12},{12,8},{16,20},{20,16},{24,28},{28,24},{1,5},{5... | collective-permute-start | bytes 3932168 | tf_op jit(solution)/shard_map/ppermute | solution.py:785
  107.3 8.1 %collective-permute-start.14 = (bf16[4,256,640]{2,1,0:T(8,128)(2,1)}, bf16[4,256,640]{2,1,0:T(8,128)(2,1)S(1)}, u32[]{:S(2)}, u32[]{:S(2)}) collective-permute-start(bf16[4,256,640]{2,1,0:T(8,128)(2,1)} %bitcast.164), channel_id=1, source_target_pairs={{0,4},{4,0},{8,12},{12,8},{16,20},{20,16},{24,28},{28,24},{1,5},{5... | collective-permute-start | bytes 3932168 | tf_op jit(solution)/shard_map/ppermute | solution.py:785
  107.8 7.3 %collective-permute-start.15 = (bf16[4,80,1536]{2,1,0:T(8,128)(2,1)}, bf16[4,80,1536]{2,1,0:T(8,128)(2,1)}, u32[]{:S(2)}, u32[]{:S(2)}) collective-permute-start(bf16[4,80,1536]{2,1,0:T(8,128)(2,1)} %bitcast.166), channel_id=1, source_target_pairs={{0,4},{4,0},{8,12},{12,8},{16,20},{20,16},{24,28},{28,24},{1,5},{5... | collective-permute-start | bytes 2949128 | tf_op jit(solution)/shard_map/ppermute | solution.py:785
  107.8 7.5 %collective-permute-start.16 = (bf16[4,80,1536]{2,1,0:T(8,128)(2,1)}, bf16[4,80,1536]{2,1,0:T(8,128)(2,1)}, u32[]{:S(2)}, u32[]{:S(2)}) collective-permute-start(bf16[4,80,1536]{2,1,0:T(8,128)(2,1)} %bitcast.168), channel_id=1, source_target_pairs={{0,4},{4,0},{8,12},{12,8},{16,20},{20,16},{24,28},{28,24},{1,5},{5... | collective-permute-start | bytes 2949128 | tf_op jit(solution)/shard_map/ppermute | solution.py:785
  178.1 11.1 %collective-permute-start.17 = (bf16[4,512,640]{2,1,0:T(8,128)(2,1)}, bf16[4,512,640]{2,1,0:T(8,128)(2,1)S(1)}, u32[]{:S(2)}, u32[]{:S(2)}) collective-permute-start(bf16[4,512,640]{2,1,0:T(8,128)(2,1)} %get-tuple-element.109.refs_0_), channel_id=1, source_target_pairs={{0,4},{4,0},{8,12},{12,8},{16,20},{20,16},{24,28},{28,24},{1,5},{5... | collective-permute-start | bytes 7864328 | tf_op jit(solution)/shard_map/ppermute | solution.py:494
  178.2 8.0 %collective-permute-start.18 = (bf16[4,80,3072]{2,1,0:T(8,128)(2,1)}, bf16[4,80,3072]{2,1,0:T(8,128)(2,1)}, u32[]{:S(2)}, u32[]{:S(2)}) collective-permute-start(bf16[4,80,3072]{2,1,0:T(8,128)(2,1)} %get-tuple-element.108.after_ref), channel_id=1, source_target_pairs={{0,4},{4,0},{8,12},{12,8},{16,20},{20,16},{24,28},{28,24},{1,5},{5... | collective-permute-start | bytes 5898248 | tf_op jit(solution)/shard_map/ppermute | solution.py:494
  185.5 16.2 %collective-permute-start.19 = (bf16[1,192,512]{2,1,0:T(8,128)(2,1)}, bf16[1,192,512]{2,1,0:T(8,128)(2,1)S(1)}, u32[]{:S(2)}, u32[]{:S(2)}) collective-permute-start(bf16[1,192,512]{2,1,0:T(8,128)(2,1)} %get-tuple-element.116), channel_id=1, source_target_pairs={{2,1},{3,2},{6,5},{7,6},{10,9},{11,10},{14,13},{15,14},{18,17},{19... | collective-permute-start | bytes 589832 | tf_op jit(solution)/shard_map/ppermute | solution.py:1053
  188.7 25.6 %collective-permute-start.22 = (bf16[2,80,3072]{2,1,0:T(8,128)(2,1)}, bf16[2,80,3072]{2,1,0:T(8,128)(2,1)}, u32[]{:S(2)}, u32[]{:S(2)}) collective-permute-start(bf16[2,80,3072]{2,1,0:T(8,128)(2,1)} %shard_map.482.refs_2_), channel_id=1, source_target_pairs={{0,16},{4,20},{8,24},{12,28},{16,0},{20,4},{24,8},{28,12},{1,17},{... | collective-permute-start | bytes 2949128 | tf_op jit(solution)/shard_map/ppermute | solution.py:552
  193.4 38.9 %collective-permute-start.26 = (bf16[2,512,640]{2,1,0:T(8,128)(2,1)}, bf16[2,512,640]{2,1,0:T(8,128)(2,1)S(1)}, u32[]{:S(2)}, u32[]{:S(2)}) collective-permute-start(bf16[2,512,640]{2,1,0:T(8,128)(2,1)} %shard_map.483.refs_1_), channel_id=1, source_target_pairs={{0,8},{4,12},{8,0},{12,4},{16,24},{20,28},{24,16},{28,20},{1,9},{5... | collective-permute-start | bytes 3932168 | tf_op jit(solution)/shard_map/ppermute | solution.py:552
  201.1 16.7 %collective-permute-start.21 = (bf16[1,192,512]{2,1,0:T(8,128)(2,1)}, bf16[1,192,512]{2,1,0:T(8,128)(2,1)S(1)}, u32[]{:S(2)}, u32[]{:S(2)}) collective-permute-start(bf16[1,192,512]{2,1,0:T(8,128)(2,1)} %get-tuple-element.123), channel_id=1, source_target_pairs={{2,1},{3,2},{6,5},{7,6},{10,9},{11,10},{14,13},{15,14},{18,17},{19... | collective-permute-start | bytes 589832 | tf_op jit(solution)/shard_map/ppermute | solution.py:1053
  204.3 33.1 %collective-permute-start.25 = (bf16[1,320,512]{2,1,0:T(8,128)(2,1)}, bf16[1,320,512]{2,1,0:T(8,128)(2,1)}, u32[]{:S(2)}, u32[]{:S(2)}) collective-permute-start(bf16[1,320,512]{2,1,0:T(8,128)(2,1)} %shard_map.485.refs_1_), channel_id=1, source_target_pairs={{1,0},{2,1},{3,2},{5,4},{6,5},{7,6},{9,8},{10,9},{11,10},{13,12},{... | collective-permute-start | bytes 983048 | tf_op jit(solution)/shard_map/ppermute | solution.py:1086
  212.9 14.0 %collective-permute-start.20 = (bf16[1,192,512]{2,1,0:T(8,128)(2,1)}, bf16[1,192,512]{2,1,0:T(8,128)(2,1)S(1)}, u32[]{:S(2)}, u32[]{:S(2)}) collective-permute-start(bf16[1,192,512]{2,1,0:T(8,128)(2,1)} %get-tuple-element.120), channel_id=1, source_target_pairs={{2,1},{3,2},{6,5},{7,6},{10,9},{11,10},{14,13},{15,14},{18,17},{19... | collective-permute-start | bytes 589832 | tf_op jit(solution)/shard_map/ppermute | solution.py:1053
  216.6 30.3 %collective-permute-start.27 = (bf16[80,3072]{1,0:T(8,128)(2,1)}, bf16[80,3072]{1,0:T(8,128)(2,1)}, u32[]{:S(2)}, u32[]{:S(2)}) collective-permute-start(bf16[80,3072]{1,0:T(8,128)(2,1)} %bitcast.146), channel_id=1, source_target_pairs={{0,8},{4,12},{8,0},{12,4},{16,24},{20,28},{24,16},{28,20},{1,9},{5... | collective-permute-start | bytes 1474568 | tf_op jit(solution)/shard_map/ppermute | solution.py:552
  220.4 21.8 %collective-permute-start.24 = (bf16[1,320,512]{2,1,0:T(8,128)(2,1)}, bf16[1,320,512]{2,1,0:T(8,128)(2,1)}, u32[]{:S(2)}, u32[]{:S(2)}) collective-permute-start(bf16[1,320,512]{2,1,0:T(8,128)(2,1)} %shard_map.488.refs_0_), channel_id=1, source_target_pairs={{1,0},{2,1},{3,2},{5,4},{6,5},{7,6},{9,8},{10,9},{11,10},{13,12},{... | collective-permute-start | bytes 983048 | tf_op jit(solution)/shard_map/ppermute | solution.py:1086
  229.5 30.5 %collective-permute-start.23 = (bf16[1,320,512]{2,1,0:T(8,128)(2,1)}, bf16[1,320,512]{2,1,0:T(8,128)(2,1)S(1)}, u32[]{:S(2)}, u32[]{:S(2)}) collective-permute-start(bf16[1,320,512]{2,1,0:T(8,128)(2,1)} %shard_map.490.refs_3_), channel_id=1, source_target_pairs={{1,0},{2,1},{3,2},{5,4},{6,5},{7,6},{9,8},{10,9},{11,10},{13,12},{... | collective-permute-start | bytes 983048 | tf_op jit(solution)/shard_map/ppermute | solution.py:1086
  236.0 35.8 %collective-permute-start.37 = (bf16[512,640]{1,0:T(8,128)(2,1)}, bf16[512,640]{1,0:T(8,128)(2,1)S(1)}, u32[]{:S(2)}, u32[]{:S(2)}) collective-permute-start(bf16[512,640]{1,0:T(8,128)(2,1)} %bitcast.143), channel_id=1, source_target_pairs={{0,16},{4,20},{8,24},{12,28},{16,0},{20,4},{24,8},{28,12},{1,17},{... | collective-permute-start | bytes 1966088 | tf_op jit(solution)/shard_map/ppermute | solution.py:552
  249.4 20.8 %collective-permute-start.34 = (bf16[80,3072]{1,0:T(8,128)(2,1)}, bf16[80,3072]{1,0:T(8,128)(2,1)S(1)}, u32[]{:S(2)}, u32[]{:S(2)}) collective-permute-start(bf16[80,3072]{1,0:T(8,128)(2,1)} %bitcast.127), channel_id=1, source_target_pairs={{0,1},{3,2},{4,5},{7,6},{8,9},{11,10},{12,13},{15,14},{16,17},{19,... | collective-permute-start | bytes 1474568 | tf_op jit(solution)/shard_map/ppermute | solution.py:586
  270.1 28.0 %collective-permute-start.28 = (bf16[2,2,208,640]{3,2,1,0:T(8,128)(2,1)S(1)}, bf16[2,2,208,640]{3,2,1,0:T(8,128)(2,1)S(1)}, u32[]{:S(2)}, u32[]{:S(2)}) collective-permute-start(bf16[2,2,208,640]{3,2,1,0:T(8,128)(2,1)S(1)} %pad_maximum_fusion.refs_4_), channel_id=1, source_target_pairs={{0,4},{4,0},{8,12},{12,8},{16,20},{20,16},{24,28},{28,24},{1,5},{5... | collective-permute-start | bytes 3194888 | tf_op jit(solution)/shard_map/ppermute | solution.py:552
  271.1 19.5 %collective-permute-start.35 = (bf16[80,3072]{1,0:T(8,128)(2,1)S(1)}, bf16[80,3072]{1,0:T(8,128)(2,1)S(1)}, u32[]{:S(2)}, u32[]{:S(2)}) collective-permute-start(bf16[80,3072]{1,0:T(8,128)(2,1)S(1)} %fusion.2), channel_id=1, source_target_pairs={{1,2},{2,1},{5,6},{6,5},{9,10},{10,9},{13,14},{14,13},{17,18},{18,... | collective-permute-start | bytes 1474568 | tf_op jit(solution)/shard_map/ppermute | solution.py:588
  275.5 14.2 %copy-start.1 = (bf16[1,512,640]{2,1,0:T(8,128)(2,1)S(1)}, bf16[1,512,640]{2,1,0:T(8,128)(2,1)}, u32[]{:S(2)}) copy-start(bf16[1,512,640]{2,1,0:T(8,128)(2,1)} %shard_map.496) | copy-start | bytes 1966084
  276.7 13.0 %collective-permute-start.41 = (bf16[256,640]{1,0:T(8,128)(2,1)S(1)}, bf16[256,640]{1,0:T(8,128)(2,1)S(1)}, u32[]{:S(2)}, u32[]{:S(2)}) collective-permute-start(bf16[256,640]{1,0:T(8,128)(2,1)S(1)} %get-tuple-element.171), channel_id=1, source_target_pairs={{0,1},{3,2},{4,5},{7,6},{8,9},{11,10},{12,13},{15,14},{16,17},{19,... | collective-permute-start | bytes 983048 | tf_op jit(solution)/shard_map/ppermute | solution.py:586
  284.8 13.2 %copy-start.15 = (bf16[2,128,640]{2,1,0:T(8,128)(2,1)S(1)}, bf16[2,128,640]{2,1,0:T(8,128)(2,1)}, u32[]{:S(2)}) copy-start(bf16[2,128,640]{2,1,0:T(8,128)(2,1)} %dynamic-slice_bitcast_fusion.1) | copy-start | bytes 983044
  289.7 9.1 %collective-permute-start.42 = (bf16[256,640]{1,0:T(8,128)(2,1)S(1)}, bf16[256,640]{1,0:T(8,128)(2,1)S(1)}, u32[]{:S(2)}, u32[]{:S(2)}) collective-permute-start(bf16[256,640]{1,0:T(8,128)(2,1)S(1)} %fusion.8), channel_id=1, source_target_pairs={{1,2},{2,1},{5,6},{6,5},{9,10},{10,9},{13,14},{14,13},{17,18},{18,... | collective-permute-start | bytes 983048 | tf_op jit(solution)/shard_map/ppermute | solution.py:588
  290.8 17.0 %collective-permute-start.36 = (bf16[80,3072]{1,0:T(8,128)(2,1)S(1)}, bf16[80,3072]{1,0:T(8,128)(2,1)S(1)}, u32[]{:S(2)}, u32[]{:S(2)}) collective-permute-start(bf16[80,3072]{1,0:T(8,128)(2,1)S(1)} %fusion.6), channel_id=1, source_target_pairs={{1,0},{2,3},{5,4},{6,7},{9,8},{10,11},{13,12},{14,15},{17,16},{18,... | collective-permute-start | bytes 1474568 | tf_op jit(solution)/shard_map/ppermute | solution.py:592
  292.1 17.8 %collective-permute-start.38 = (bf16[256,640]{1,0:T(8,128)(2,1)S(1)}, bf16[256,640]{1,0:T(8,128)(2,1)S(1)}, u32[]{:S(2)}, u32[]{:S(2)}) collective-permute-start(bf16[256,640]{1,0:T(8,128)(2,1)S(1)} %get-tuple-element.172), channel_id=1, source_target_pairs={{0,1},{3,2},{4,5},{7,6},{8,9},{11,10},{12,13},{15,14},{16,17},{19,... | collective-permute-start | bytes 983048 | tf_op jit(solution)/shard_map/ppermute | solution.py:586
  298.2 10.7 %collective-permute-start.29 = (bf16[2,208,640]{2,1,0:T(8,128)(2,1)S(1)}, bf16[2,208,640]{2,1,0:T(8,128)(2,1)S(1)}, u32[]{:S(2)}, u32[]{:S(2)}) collective-permute-start(bf16[2,208,640]{2,1,0:T(8,128)(2,1)S(1)} %fusion.1), channel_id=1, source_target_pairs={{0,16},{4,20},{8,24},{12,28},{16,0},{20,4},{24,8},{28,12},{1,17},{... | collective-permute-start | bytes 1597448 | tf_op jit(solution)/shard_map/ppermute | solution.py:552
  298.9 12.4 %copy-start.8 = (f32[256,640]{1,0:T(8,128)S(1)}, f32[256,640]{1,0:T(8,128)}, u32[]{:S(2)}) copy-start(f32[256,640]{1,0:T(8,128)} %wu_ref.1) | copy-start | bytes 1966084
  299.0 12.4 %copy-start.23 = (f32[256,640]{1,0:T(8,128)S(1)}, f32[256,640]{1,0:T(8,128)}, u32[]{:S(2)}) copy-start(f32[256,640]{1,0:T(8,128)} %param.53) | copy-start | bytes 1966084
  299.0 12.4 %collective-permute-start.43 = (bf16[256,640]{1,0:T(8,128)(2,1)S(1)}, bf16[256,640]{1,0:T(8,128)(2,1)S(1)}, u32[]{:S(2)}, u32[]{:S(2)}) collective-permute-start(bf16[256,640]{1,0:T(8,128)(2,1)S(1)} %fusion.17), channel_id=1, source_target_pairs={{1,0},{2,3},{5,4},{6,7},{9,8},{10,11},{13,12},{14,15},{17,16},{18,... | collective-permute-start | bytes 983048 | tf_op jit(solution)/shard_map/ppermute | solution.py:592
  309.0 6.5 %collective-permute-start.30 = (bf16[208,640]{1,0:T(8,128)(2,1)S(1)}, bf16[208,640]{1,0:T(8,128)(2,1)S(1)}, u32[]{:S(2)}, u32[]{:S(2)}) collective-permute-start(bf16[208,640]{1,0:T(8,128)(2,1)S(1)} %fusion.9), channel_id=1, source_target_pairs={{0,8},{4,12},{8,0},{12,4},{16,24},{20,28},{24,16},{28,20},{1,9},{5... | collective-permute-start | bytes 798728 | tf_op jit(solution)/shard_map/ppermute | solution.py:552
  313.2 6.8 %collective-permute-start.39 = (bf16[256,640]{1,0:T(8,128)(2,1)S(1)}, bf16[256,640]{1,0:T(8,128)(2,1)S(1)}, u32[]{:S(2)}, u32[]{:S(2)}) collective-permute-start(bf16[256,640]{1,0:T(8,128)(2,1)S(1)} %get-tuple-element.170), channel_id=1, source_target_pairs={{1,2},{2,1},{5,6},{6,5},{9,10},{10,9},{13,14},{14,13},{17,18},{18,... | collective-permute-start | bytes 983048 | tf_op jit(solution)/shard_map/ppermute | solution.py:588
  315.7 6.5 %collective-permute-start.31 = (bf16[208,640]{1,0:T(8,128)(2,1)S(1)}, bf16[208,640]{1,0:T(8,128)(2,1)S(1)}, u32[]{:S(2)}, u32[]{:S(2)}) collective-permute-start(bf16[208,640]{1,0:T(8,128)(2,1)S(1)} %fusion.11), channel_id=1, source_target_pairs={{0,1},{3,2},{4,5},{7,6},{8,9},{11,10},{12,13},{15,14},{16,17},{19,... | collective-permute-start | bytes 798728 | tf_op jit(solution)/shard_map/ppermute | solution.py:586
  320.1 9.1 %collective-permute-start.40 = (bf16[256,640]{1,0:T(8,128)(2,1)S(1)}, bf16[256,640]{1,0:T(8,128)(2,1)S(1)}, u32[]{:S(2)}, u32[]{:S(2)}) collective-permute-start(bf16[256,640]{1,0:T(8,128)(2,1)S(1)} %fusion.16), channel_id=1, source_target_pairs={{1,0},{2,3},{5,4},{6,7},{9,8},{10,11},{13,12},{14,15},{17,16},{18,... | collective-permute-start | bytes 983048 | tf_op jit(solution)/shard_map/ppermute | solution.py:592
  322.3 1.9 collective-permute-start.32
  324.4 14.6 %collective-permute-start.33 = (bf16[208,640]{1,0:T(8,128)(2,1)S(1)}, bf16[208,640]{1,0:T(8,128)(2,1)S(1)}, u32[]{:S(2)}, u32[]{:S(2)}) collective-permute-start(bf16[208,640]{1,0:T(8,128)(2,1)S(1)} %fusion.13), channel_id=1, source_target_pairs={{1,0},{2,3},{5,4},{6,7},{9,8},{10,11},{13,12},{14,15},{17,16},{18,... | collective-permute-start | bytes 798728 | tf_op jit(solution)/shard_map/ppermute | solution.py:592
  (67 other events, 239.4 us)
